TPU v7x, 32 devices: a whole 2x2x4 slice. The times are simulated.
32 devices in a mesh: section: 4 (over z), dp: 8 (over y, x, core).
Axes of the slice: x: 2, y: 2, z: 4, core: 2. Of those that a mesh axis runs over, the one named last changes fastest.
Arguments:
- inputs: bfloat16 [2, 1024, 2048], P(None, 'dp', 'section'), may hold values from -6 to 6
- cotangent: bfloat16 [2, 1024, 2048], P(None, 'dp', 'section'), may hold values from -6 to 6
- resets: int32 [2, 1024], replicated, may hold values from 0 to 1, as said below
- branch_in: bfloat16 [2, 2048, 2560], P(None, 'dp'), may hold values from -0.125 to 0.125
- gate_in: bfloat16 [2, 2048, 2560], P(None, 'dp'), may hold values from -0.125 to 0.125
- rec_out: bfloat16 [2, 2560, 2048], P(None, 'dp'), may hold values from -0.5 to 0.5
- rate_gate: bfloat16 [2, 10, 256, 256], P(None, None, 'dp'), may hold values from -0.375 to 0.375
- input_gate: bfloat16 [2, 10, 256, 256], P(None, None, 'dp'), may hold values from -0.375 to 0.375
- conv_taps: bfloat16 [2, 4, 2560], P(None, None, 'dp'), may hold values from -3 to 3
- conv_bias: bfloat16 [2, 2560], P(None, 'dp'), may hold values from -3 to 3
- rate_bias: bfloat16 [2, 2560], P(None, 'dp'), may hold values from -4 to 4
- input_bias: bfloat16 [2, 2560], P(None, 'dp'), may hold values from -4 to 4
- decay_param: bfloat16 [2, 2560], P(None, 'dp'), may hold values from 4 to 12
- norm_rec: bfloat16 [2, 2048], P(None, 'dp'), may hold values from 0.5 to 1.5
- norm_mlp: bfloat16 [2, 2048], P(None, 'dp'), may hold values from 0.5 to 1.5
- mlp_gate: bfloat16 [2, 2048, 6144], P(None, 'dp'), may hold values from -0.125 to 0.125
- mlp_up: bfloat16 [2, 2048, 6144], P(None, 'dp'), may hold values from -0.125 to 0.125
- mlp_down: bfloat16 [2, 6144, 2048], P(None, 'dp'), may hold values from -0.15625 to 0.15625
Outputs:
- output: bfloat16 [2, 1024, 2048], P(None, 'dp', 'section')
- input_grad: bfloat16 [2, 1024, 2048], P(None, 'dp', 'section')
- grad_branch_in: float32 [2, 2048, 2560], P(None, 'dp')
- grad_gate_in: float32 [2, 2048, 2560], P(None, 'dp')
- grad_rec_out: float32 [2, 2560, 2048], P(None, 'dp')
- grad_rate_gate: float32 [2, 10, 256, 256], P(None, None, 'dp')
- grad_input_gate: float32 [2, 10, 256, 256], P(None, None, 'dp')
- grad_conv_taps: float32 [2, 4, 2560], P(None, None, 'dp')
- grad_conv_bias: float32 [2, 2560], P(None, 'dp')
- grad_rate_bias: float32 [2, 2560], P(None, 'dp')
- grad_input_bias: float32 [2, 2560], P(None, 'dp')
- grad_decay_param: float32 [2, 2560], P(None, 'dp')
- grad_norm_rec: float32 [2, 2048], P(None, 'dp')
- grad_norm_mlp: float32 [2, 2048], P(None, 'dp')
- grad_mlp_gate: float32 [2, 2048, 6144], P(None, 'dp')
- grad_mlp_up: float32 [2, 2048, 6144], P(None, 'dp')
- grad_mlp_down: float32 [2, 6144, 2048], P(None, 'dp')
Inputs may be any that keep to these rules, and one draw needn't show every extreme that they name: `resets`: every micro-batch has a 1 at position 0. In one micro-batch, chosen by the seed, a row starts within the first half of 128 positions and the next row starts within the last half of 128 positions, with no other row start between; the other starts fall at random positions.
All inputs are finite; a program needn't handle non-finite values.
Results may differ from a plain program's by a relative error of at most 0.018.
Values may be sent and summed in bfloat16 or wider, within the bound.
No kernel may reach another device: no remote copies, remote signals or barrier semaphores. Data moves between devices by JAX's collectives and lax.ppermute only.
A program may use at most 640 MiB of HBM per device.

v0:
```python
import jax
import jax.numpy as jnp
from jax import lax
from jax.sharding import PartitionSpec as P

D = 2048
H = 10
BW = 256
F = 6144
R = 2560
CONV = 4
MICRO = 2


EPS = 1e-06
LRU_EPS = 0.04
RATE_SCALE = 8.0


def passed_along(value, axis, steps):
    count = lax.axis_size(axis)
    leading, last = (max(0, -steps), min(count, count - steps))
    return lax.ppermute(value, axis, [(source, source + steps) for source in range(leading, last)])


def prefix(value, axis, combine, identity, reverse):
    devices, index = (lax.axis_size(axis), lax.axis_index(axis))
    everything = jax.tree.map(lambda part: lax.all_gather(part, axis), value)
    start = jax.tree.map(
        lambda part, zero: jnp.broadcast_to(jnp.asarray(zero, part.dtype), part.shape),
        value,
        identity,
    )

    def turn(k, before):
        at = devices - 1 - k if reverse else k
        reached = at > index if reverse else at < index
        new = combine(before, jax.tree.map(lambda part: part[at], everything))
        return jax.tree.map(lambda a, b: jnp.where(reached, a, b), new, before)

    return lax.fori_loop(0, devices, turn, start)


def shortened(value):

    def short(part):
        return part.astype(jnp.bfloat16) if part.dtype == jnp.float32 else part

    return jax.tree.map(short, value)


def from_root(block, axis, source):
    block = jnp.where(lax.axis_index(axis) == source, block, jnp.zeros_like(block))
    return lax.psum(block, axis)


def rms_scale(values, scales):
    return values * lax.rsqrt(jnp.mean(values * values, axis=-1, keepdims=True) + EPS) * scales


def times_weight(left, right):
    return jnp.dot(left, right, preferred_element_type=jnp.float32)


def times_transposed(left, right):
    return lax.dot_general(
        left, right, (((1,), (1,)), ((), ())), preferred_element_type=jnp.float32
    )


def rows_outer(left, right):
    return lax.dot_general(
        left, right, (((0,), (0,)), ((), ())), preferred_element_type=jnp.float32
    )


def spread_term(left, right):
    share = left.shape[1] // lax.axis_size("dp")
    return lax.psum_scatter(
        rows_outer(lax.slice_in_dim(left, 0, share * lax.axis_size("dp"), axis=1), right).astype(
            jnp.bfloat16
        ),
        "dp",
        scatter_dimension=0,
        tiled=True,
    ).astype(jnp.float32)


def block_forward(values, blocks):
    split = values.reshape(values.shape[0], H, BW)
    return jnp.einsum("tha,hab->thb", split, blocks, preferred_element_type=jnp.float32).reshape(
        values.shape[0], H * BW
    )


def block_backward(grads, blocks):
    split = grads.reshape(grads.shape[0], H, BW)
    return jnp.einsum("thb,hab->tha", split, blocks, preferred_element_type=jnp.float32).reshape(
        grads.shape[0], H * BW
    )


def block_outer(values, grads):
    left_split = values.reshape(values.shape[0], H, BW)
    right_split = grads.reshape(grads.shape[0], H, BW)
    return jnp.einsum("tha,thb->hab", left_split, right_split, preferred_element_type=jnp.float32)


def combine_pair(earlier, later):
    return (earlier[0] * later[0], later[0] * earlier[1] + later[1])


def local_scan(decays, drives):
    return lax.associative_scan(combine_pair, (decays, drives), axis=0)


def conv_apply(extended, taps_values, shift_values, usable):
    margin = CONV - 1
    block_rows = extended.shape[0] - margin
    summed = shift_values + taps_values[0] * extended[margin:]
    for lag_steps in range(1, CONV):
        start_row = margin - lag_steps
        summed = (
            summed
            + taps_values[lag_steps]
            * usable[lag_steps]
            * extended[start_row : start_row + block_rows]
        )
    return summed


def lru_apply(conved, rate_raw, input_raw, rate_shift, input_shift, decay_values, carry_mask):
    decays = (
        jnp.exp(
            -RATE_SCALE * jax.nn.softplus(-decay_values) * jax.nn.sigmoid(rate_raw + rate_shift)
        )
        * carry_mask
    )
    drives = (
        jnp.sqrt(1.0 + LRU_EPS - decays * decays) * jax.nn.sigmoid(input_raw + input_shift) * conved
    )
    return (decays, drives)


def gated_gelu(gate_val, up_val):
    return jax.nn.gelu(gate_val) * up_val


def gelu_product(states, side):
    return states * jax.nn.gelu(side)


def when(active, function, *operands):
    return lax.cond(
        active, function, lambda *inner: jax.tree.map(jnp.zeros_like, function(*inner)), *operands
    )


def store(buffer, slot_index, values, active):
    return jnp.where(active, lax.dynamic_update_index_in_dim(buffer, values, slot_index, 0), buffer)


def forward_step(section_in, weights, carry_mask, usable, mode, rec_active):
    (
        branch_in,
        gate_in,
        rec_out,
        rate_gate,
        input_gate,
        conv_taps,
        conv_bias,
        rate_bias,
        input_bias,
        decay_param,
        norm_rec,
        norm_mlp,
        mlp_gate,
        mlp_up,
        mlp_down,
    ) = weights
    margin = CONV - 1
    block_rows = section_in.shape[0]

    def rec_branch(section_in):
        normed = rms_scale(section_in.astype(jnp.float32), norm_rec.astype(jnp.float32)).astype(
            jnp.bfloat16
        )
        return (
            normed,
            times_weight(normed, branch_in),
            times_weight(normed, gate_in),
            jnp.zeros((block_rows, D), jnp.bfloat16),
            jnp.zeros((block_rows, F), jnp.float32),
            jnp.zeros((block_rows, F), jnp.float32),
            jnp.zeros((block_rows, F), jnp.bfloat16),
            jnp.zeros((block_rows, D), jnp.float32),
        )

    def mlp_branch(section_in):
        middle = section_in.astype(jnp.float32)
        normed_mlp = rms_scale(middle, norm_mlp.astype(jnp.float32)).astype(jnp.bfloat16)
        gate_val = times_weight(normed_mlp, mlp_gate)
        up_val = times_weight(normed_mlp, mlp_up)
        hidden = gated_gelu(gate_val, up_val).astype(jnp.bfloat16)
        return (
            jnp.zeros((block_rows, D), jnp.bfloat16),
            jnp.zeros((block_rows, R), jnp.float32),
            jnp.zeros((block_rows, R), jnp.float32),
            normed_mlp,
            gate_val,
            up_val,
            hidden,
            middle + times_weight(hidden, mlp_down),
        )

    def spare_branch(section_in):
        return jax.tree.map(jnp.zeros_like, rec_branch(section_in))

    normed, branch, side, normed_mlp, gate_val, up_val, hidden, mlp_result = lax.switch(
        mode, (spare_branch, rec_branch, mlp_branch), section_in
    )
    rim_rows = passed_along(branch[block_rows - margin :], "dp", 1)
    extended = jnp.concatenate([rim_rows, branch], axis=0)

    def middle_part(extended):
        conved = conv_apply(
            extended, conv_taps.astype(jnp.float32), conv_bias.astype(jnp.float32), usable
        )
        conv_low = conved.astype(jnp.bfloat16)
        rate_raw = block_forward(conv_low, rate_gate)
        input_raw = block_forward(conv_low, input_gate)
        decays, drives = lru_apply(
            conved,
            rate_raw,
            input_raw,
            rate_bias.astype(jnp.float32),
            input_bias.astype(jnp.float32),
            decay_param.astype(jnp.float32),
            carry_mask,
        )
        cumulative, partial_states = local_scan(decays, drives)
        return (conved, conv_low, rate_raw, input_raw, decays, cumulative, partial_states)

    conved, conv_low, rate_raw, input_raw, decays, cumulative, partial_states = when(
        rec_active, middle_part, extended
    )
    carried = prefix(
        (cumulative[-1], partial_states[-1]),
        "dp",
        combine_pair,
        (jnp.ones((R,), jnp.float32), jnp.zeros((R,), jnp.float32)),
        False,
    )
    carried_in = carried[1]

    def tail_part(section_in, side, cumulative, partial_states, carried_in):
        states = partial_states + cumulative * carried_in[None]
        mixture = gelu_product(states, side).astype(jnp.bfloat16)
        return (states, mixture, section_in.astype(jnp.float32) + times_weight(mixture, rec_out))

    states, mixture, rec_result = when(
        rec_active, tail_part, section_in, side, cumulative, partial_states, carried_in
    )
    kept = {
        "normed": normed,
        "side": side,
        "extended": extended,
        "conved": conved,
        "conv_low": conv_low,
        "rate_raw": rate_raw,
        "input_raw": input_raw,
        "decays": decays,
        "carried_in": carried_in,
        "states": states,
        "mixture": mixture,
        "normed_mlp": normed_mlp,
        "gate_val": gate_val,
        "up_val": up_val,
        "hidden": hidden,
    }
    return (kept, rec_result, mlp_result)


def backward_step(section_in, weights, kept, grad_in, carry_mask, usable, mode, rec_active):
    (
        branch_in,
        gate_in,
        rec_out,
        rate_gate,
        input_gate,
        conv_taps,
        conv_bias,
        rate_bias,
        input_bias,
        decay_param,
        norm_rec,
        norm_mlp,
        mlp_gate,
        mlp_up,
        mlp_down,
    ) = weights
    margin = CONV - 1
    block_rows = section_in.shape[0]

    def rec_upper(grad_in):
        grad_mixture = times_transposed(grad_in, rec_out)
        _, mix_pull = jax.vjp(gelu_product, kept["states"], kept["side"])
        grad_states, side_grad = mix_pull(grad_mixture)
        decays = kept["decays"]
        following = jnp.concatenate([decays[1:], jnp.ones_like(decays[:1])], axis=0)
        reach_flip, local_flip = local_scan(following[::-1], grad_states[::-1])
        return (
            side_grad,
            reach_flip[::-1],
            local_flip[::-1],
            jnp.zeros((block_rows, D), jnp.float32),
            jnp.zeros((block_rows, F), jnp.bfloat16),
            jnp.zeros((block_rows, F), jnp.bfloat16),
            jnp.zeros((D,), jnp.float32),
        )

    def mlp_whole(grad_in):
        grad_hidden = times_transposed(grad_in, mlp_down)
        _, act_pull = jax.vjp(gated_gelu, kept["gate_val"], kept["up_val"])
        gate_grad, up_grad = act_pull(grad_hidden)
        gate_grad = gate_grad.astype(jnp.bfloat16)
        up_grad = up_grad.astype(jnp.bfloat16)
        grad_normed = times_transposed(gate_grad, mlp_gate) + times_transposed(up_grad, mlp_up)
        _, norm_pull = jax.vjp(
            rms_scale, section_in.astype(jnp.float32), norm_mlp.astype(jnp.float32)
        )
        grad_middle, norm_grad = norm_pull(grad_normed)
        zero_rows = jnp.zeros((block_rows, R), jnp.float32)
        return (
            zero_rows,
            zero_rows,
            zero_rows,
            grad_middle + grad_in.astype(jnp.float32),
            gate_grad,
            up_grad,
            norm_grad,
        )

    def spare_whole(grad_in):
        return jax.tree.map(jnp.zeros_like, rec_upper(grad_in))

    side_grad, reach, local_grad, mlp_section_grad, gate_grad, up_grad, norm_mlp_grad = lax.switch(
        mode, (spare_whole, rec_upper, mlp_whole), grad_in
    )
    decays = kept["decays"]
    leaving = prefix(
        (decays[0] * reach[0], decays[0] * local_grad[0]),
        "dp",
        combine_pair,
        (jnp.ones((R,), jnp.float32), jnp.zeros((R,), jnp.float32)),
        True,
    )
    incoming = leaving[1]

    def lower(local_grad, reach, incoming):
        grad_states = local_grad + reach * incoming[None]
        previous = jnp.concatenate([kept["carried_in"][None], kept["states"][:-1]], axis=0)
        grad_decays = grad_states * previous

        def lru_local(conved, rate_raw, input_raw, rate_shift, input_shift, decay_values):
            return lru_apply(
                conved, rate_raw, input_raw, rate_shift, input_shift, decay_values, carry_mask
            )

        _, lru_pull = jax.vjp(
            lru_local,
            kept["conved"],
            kept["rate_raw"],
            kept["input_raw"],
            rate_bias.astype(jnp.float32),
            input_bias.astype(jnp.float32),
            decay_param.astype(jnp.float32),
        )
        conv_grad, rate_raw_grad, input_raw_grad, rate_bias_grad, input_bias_grad, decay_grad = (
            lru_pull((grad_decays, grad_states))
        )
        rate_grad = rate_raw_grad.astype(jnp.bfloat16)
        input_low_grad = input_raw_grad.astype(jnp.bfloat16)
        conv_grad = (
            conv_grad
            + block_backward(rate_grad, rate_gate)
            + block_backward(input_low_grad, input_gate)
        )

        def conv_local(extended, taps_values, shift_values):
            return conv_apply(extended, taps_values, shift_values, usable)

        _, conv_pull = jax.vjp(
            conv_local,
            kept["extended"],
            conv_taps.astype(jnp.float32),
            conv_bias.astype(jnp.float32),
        )
        extended_grad, taps_grad, conv_bias_grad = conv_pull(conv_grad)
        return (
            rate_grad,
            input_low_grad,
            rate_bias_grad,
            input_bias_grad,
            decay_grad,
            extended_grad,
            taps_grad,
            conv_bias_grad,
        )

    (
        rate_grad,
        input_low_grad,
        rate_bias_grad,
        input_bias_grad,
        decay_grad,
        extended_grad,
        taps_grad,
        conv_bias_grad,
    ) = when(rec_active, lower, local_grad, reach, incoming)
    rim_grad = passed_along(extended_grad[:margin], "dp", -1)

    def bottom(extended_grad, rim_grad, side_grad, grad_in):
        branch_grad = extended_grad[margin:] + jnp.concatenate(
            [jnp.zeros((block_rows - margin, R), jnp.float32), rim_grad], axis=0
        )
        branch_grad = branch_grad.astype(jnp.bfloat16)
        side_low = side_grad.astype(jnp.bfloat16)
        grad_normed = times_transposed(branch_grad, branch_in) + times_transposed(side_low, gate_in)
        _, norm_pull = jax.vjp(
            rms_scale, section_in.astype(jnp.float32), norm_rec.astype(jnp.float32)
        )
        grad_section, norm_rec_grad = norm_pull(grad_normed)
        return (grad_section + grad_in.astype(jnp.float32), branch_grad, side_low, norm_rec_grad)

    rec_section_grad, branch_grad, side_low, norm_rec_grad = when(
        rec_active, bottom, extended_grad, rim_grad, side_grad, grad_in
    )
    return {
        "rec_section_grad": rec_section_grad,
        "mlp_section_grad": mlp_section_grad,
        "branch_grad": branch_grad,
        "side_grad": side_low,
        "rate_grad": rate_grad,
        "input_low_grad": input_low_grad,
        "gate_grad": gate_grad,
        "up_grad": up_grad,
        "norm_rec": norm_rec_grad,
        "norm_mlp": norm_mlp_grad,
        "conv_taps": taps_grad,
        "conv_bias": conv_bias_grad,
        "rate_bias": rate_bias_grad,
        "input_bias": input_bias_grad,
        "decay_param": decay_grad,
    }


def local(
    inputs,
    cotangent,
    resets,
    branch_in,
    gate_in,
    rec_out,
    rate_gate,
    input_gate,
    conv_taps,
    conv_bias,
    rate_bias,
    input_bias,
    decay_param,
    norm_rec,
    norm_mlp,
    mlp_gate,
    mlp_up,
    mlp_down,
):
    section_rank = lax.axis_index("section")
    section_count = lax.axis_size("section")
    data_rank = lax.axis_index("dp")
    kind_mlp = section_rank % 2 == 1
    layer_index = section_rank // 2
    layer_count = section_count // 2
    block_rows = inputs.shape[1]
    margin = CONV - 1
    all_weights = (
        branch_in,
        gate_in,
        rec_out,
        rate_gate,
        input_gate,
        conv_taps,
        conv_bias,
        rate_bias,
        input_bias,
        decay_param,
        norm_rec,
        norm_mlp,
        mlp_gate,
        mlp_up,
        mlp_down,
    )
    own_shards = tuple(
        (lax.dynamic_index_in_dim(weight, layer_index, 0, keepdims=False) for weight in all_weights)
    )
    weights = (
        lax.all_gather(own_shards[0], "dp", axis=0, tiled=True),
        lax.all_gather(own_shards[1], "dp", axis=0, tiled=True),
        lax.all_gather(own_shards[2], "dp", axis=0, tiled=True),
        lax.all_gather(own_shards[3], "dp", axis=1, tiled=True),
        lax.all_gather(own_shards[4], "dp", axis=1, tiled=True),
        lax.all_gather(own_shards[5], "dp", axis=1, tiled=True),
        lax.all_gather(own_shards[6], "dp", axis=0, tiled=True),
        lax.all_gather(own_shards[7], "dp", axis=0, tiled=True),
        lax.all_gather(own_shards[8], "dp", axis=0, tiled=True),
        lax.all_gather(own_shards[9], "dp", axis=0, tiled=True),
        lax.all_gather(own_shards[10], "dp", axis=0, tiled=True),
        lax.all_gather(own_shards[11], "dp", axis=0, tiled=True),
        lax.all_gather(own_shards[12], "dp", axis=0, tiled=True),
        lax.all_gather(own_shards[13], "dp", axis=0, tiled=True),
        lax.all_gather(own_shards[14], "dp", axis=0, tiled=True),
    )
    whole_inputs, whole_cotangent = (
        lax.all_gather(inputs, "section", axis=2, tiled=True),
        lax.all_gather(cotangent, "section", axis=2, tiled=True),
    )
    keep_all = jnp.concatenate(
        [jnp.ones((MICRO, margin), jnp.float32), (1 - resets).astype(jnp.float32)], axis=1
    )
    keep_block = lax.dynamic_slice_in_dim(keep_all, data_rank * block_rows, block_rows + margin, 1)

    def geometry(slot_index):
        row_flags = lax.dynamic_index_in_dim(keep_block, slot_index, 0, keepdims=False)
        carry_mask = row_flags[margin:][:, None]
        usable = [jnp.ones((block_rows, 1), jnp.float32)]
        for lag_steps in range(1, CONV):
            start_row = margin - lag_steps + 1
            usable.append(usable[-1] * row_flags[start_row : start_row + block_rows][:, None])
        return (carry_mask, jnp.stack(usable))

    steps_count = MICRO + section_count - 1
    received = jnp.zeros((block_rows, D), jnp.bfloat16)
    saved_inputs = jnp.zeros((MICRO, block_rows, D), jnp.bfloat16)
    finished = jnp.zeros((MICRO, block_rows, D), jnp.bfloat16)
    stored = None
    for moment in range(steps_count):
        micro_index = moment - section_rank
        active = (micro_index >= 0) & (micro_index < MICRO)
        rec_active = active & jnp.logical_not(kind_mlp)
        mode = jnp.where(active, 1 + kind_mlp.astype(jnp.int32), 0)
        slot_index = jnp.clip(micro_index, 0, MICRO - 1)
        first_in = lax.dynamic_index_in_dim(whole_inputs, slot_index, 0, keepdims=False)
        section_in = jnp.where(section_rank == 0, first_in, received)
        carry_mask, usable = geometry(slot_index)
        kept, rec_result, mlp_result = forward_step(
            section_in, weights, carry_mask, usable, mode, rec_active
        )
        if stored is None:
            stored = {
                entry_name: jnp.zeros((MICRO,) + entry.shape, entry.dtype)
                for entry_name, entry in kept.items()
            }
        for entry_name in kept:
            stored[entry_name] = store(stored[entry_name], slot_index, kept[entry_name], active)
        section_out = jnp.where(kind_mlp, mlp_result, rec_result).astype(jnp.bfloat16)
        saved_inputs = store(saved_inputs, slot_index, section_in, active)
        finished = store(finished, slot_index, section_out, active)
        received = passed_along(section_out, "section", 1)
    back_weights = (
        lax.all_gather(own_shards[0], "dp", axis=0, tiled=True),
        lax.all_gather(own_shards[1], "dp", axis=0, tiled=True),
        lax.all_gather(own_shards[2], "dp", axis=0, tiled=True),
        lax.all_gather(own_shards[3], "dp", axis=1, tiled=True),
        lax.all_gather(own_shards[4], "dp", axis=1, tiled=True),
        lax.all_gather(own_shards[5], "dp", axis=1, tiled=True),
        lax.all_gather(own_shards[6], "dp", axis=0, tiled=True),
        lax.all_gather(own_shards[7], "dp", axis=0, tiled=True),
        lax.all_gather(own_shards[8], "dp", axis=0, tiled=True),
        lax.all_gather(own_shards[9], "dp", axis=0, tiled=True),
        lax.all_gather(own_shards[10], "dp", axis=0, tiled=True),
        lax.all_gather(own_shards[11], "dp", axis=0, tiled=True),
        lax.all_gather(own_shards[12], "dp", axis=0, tiled=True),
        lax.all_gather(own_shards[13], "dp", axis=0, tiled=True),
        lax.all_gather(own_shards[14], "dp", axis=0, tiled=True),
    )
    term_widths = {
        "branch_grad": R,
        "side_grad": R,
        "rate_grad": R,
        "input_low_grad": R,
        "gate_grad": F,
        "up_grad": F,
        "grad_in": D,
    }
    buffers = {
        entry_name: jnp.zeros((MICRO, block_rows, entry_width), jnp.bfloat16)
        for entry_name, entry_width in term_widths.items()
    }
    small_shapes = {
        "norm_rec": (D,),
        "norm_mlp": (D,),
        "conv_taps": (CONV, R),
        "conv_bias": (R,),
        "rate_bias": (R,),
        "input_bias": (R,),
        "decay_param": (R,),
    }
    small_sums = {
        entry_name: jnp.zeros(entry_shape, jnp.float32)
        for entry_name, entry_shape in small_shapes.items()
    }
    grad_received = jnp.zeros((block_rows, D), jnp.bfloat16)
    input_grads = jnp.zeros((MICRO, block_rows, D), jnp.bfloat16)
    for moment in range(steps_count):
        micro_index = moment - (section_count - 1 - section_rank)
        active = (micro_index >= 0) & (micro_index < MICRO)
        rec_active = active & jnp.logical_not(kind_mlp)
        mode = jnp.where(active, 1 + kind_mlp.astype(jnp.int32), 0)
        slot_index = jnp.clip(micro_index, 0, MICRO - 1)
        top_grad = lax.dynamic_index_in_dim(whole_cotangent, slot_index, 0, keepdims=False)
        grad_in = jnp.where(section_rank == section_count - 1, top_grad, grad_received)
        section_in = lax.dynamic_index_in_dim(saved_inputs, slot_index, 0, keepdims=False)
        carry_mask, usable = geometry(slot_index)
        kept = {
            entry_name: lax.dynamic_index_in_dim(stored[entry_name], slot_index, 0, keepdims=False)
            for entry_name in stored
        }
        backward = backward_step(
            section_in, back_weights, kept, grad_in, carry_mask, usable, mode, rec_active
        )
        for entry_name in term_widths:
            if entry_name == "grad_in":
                buffers[entry_name] = store(buffers[entry_name], slot_index, grad_in, active)
            else:
                buffers[entry_name] = store(
                    buffers[entry_name], slot_index, backward[entry_name], active
                )
        for entry_name in small_shapes:
            small_sums[entry_name] = small_sums[entry_name] + backward[entry_name]
        section_grad = jnp.where(
            kind_mlp, backward["mlp_section_grad"], backward["rec_section_grad"]
        )
        grad_low = section_grad.astype(jnp.bfloat16)
        input_grads = store(input_grads, slot_index, grad_low, active)
        grad_received = passed_along(grad_low, "section", -1)

    def merged(source, entry_name):
        entry = source[entry_name]
        return entry.reshape(MICRO * block_rows, entry.shape[-1])

    share_branch = spread_term(merged(stored, "normed"), merged(buffers, "branch_grad"))
    share_gate_in = spread_term(merged(stored, "normed"), merged(buffers, "side_grad"))
    share_rec_out = spread_term(merged(stored, "mixture"), merged(buffers, "grad_in"))
    share_mlp_gate = spread_term(merged(stored, "normed_mlp"), merged(buffers, "gate_grad"))
    share_mlp_up = spread_term(merged(stored, "normed_mlp"), merged(buffers, "up_grad"))
    share_mlp_down = spread_term(merged(stored, "hidden"), merged(buffers, "grad_in"))
    term_rate_gate = block_outer(merged(stored, "conv_low"), merged(buffers, "rate_grad"))
    term_input_gate = block_outer(merged(stored, "conv_low"), merged(buffers, "input_low_grad"))
    summed = (
        lax.psum_scatter(
            term_rate_gate.astype(jnp.bfloat16), "dp", scatter_dimension=1, tiled=True
        ).astype(jnp.float32),
        lax.psum_scatter(
            term_input_gate.astype(jnp.bfloat16), "dp", scatter_dimension=1, tiled=True
        ).astype(jnp.float32),
        lax.psum_scatter(
            small_sums["conv_taps"].astype(jnp.bfloat16), "dp", scatter_dimension=1, tiled=True
        ).astype(jnp.float32),
        lax.psum_scatter(
            small_sums["conv_bias"].astype(jnp.bfloat16), "dp", scatter_dimension=0, tiled=True
        ).astype(jnp.float32),
        lax.psum_scatter(
            small_sums["rate_bias"].astype(jnp.bfloat16), "dp", scatter_dimension=0, tiled=True
        ).astype(jnp.float32),
        lax.psum_scatter(
            small_sums["input_bias"].astype(jnp.bfloat16), "dp", scatter_dimension=0, tiled=True
        ).astype(jnp.float32),
        lax.psum_scatter(
            small_sums["decay_param"].astype(jnp.bfloat16), "dp", scatter_dimension=0, tiled=True
        ).astype(jnp.float32),
        lax.psum_scatter(
            small_sums["norm_rec"].astype(jnp.bfloat16), "dp", scatter_dimension=0, tiled=True
        ).astype(jnp.float32),
        lax.psum_scatter(
            small_sums["norm_mlp"].astype(jnp.bfloat16), "dp", scatter_dimension=0, tiled=True
        ).astype(jnp.float32),
    )
    owned = (
        share_branch,
        share_gate_in,
        share_rec_out,
        summed[0],
        summed[1],
        summed[2],
        summed[3],
        summed[4],
        summed[5],
        summed[6],
        summed[7],
        summed[8],
        share_mlp_gate,
        share_mlp_up,
        share_mlp_down,
    )
    layer_pick = jnp.arange(layer_count) == layer_index
    stacked = tuple(
        (
            jnp.where(
                layer_pick.reshape((layer_count,) + (1,) * piece.ndim),
                piece[None],
                jnp.zeros((), jnp.float32),
            )
            for piece in owned
        )
    )
    totals = jax.tree.map(
        lambda part: part.astype(jnp.float32), lax.psum(shortened(stacked), "section")
    )
    feature_share = D // section_count
    output_all = from_root(finished, "section", section_count - 1)
    grads_all = from_root(input_grads, "section", 0)
    output = lax.dynamic_slice_in_dim(output_all, section_rank * feature_share, feature_share, 2)
    input_grad = lax.dynamic_slice_in_dim(grads_all, section_rank * feature_share, feature_share, 2)
    return (
        output,
        input_grad,
        totals[0],
        totals[1],
        totals[2],
        totals[3],
        totals[4],
        totals[5],
        totals[6],
        totals[7],
        totals[8],
        totals[9],
        totals[10],
        totals[11],
        totals[12],
        totals[13],
        totals[14],
    )


def solution(mesh):
    return jax.shard_map(
        local,
        mesh=mesh,
        in_specs=(
            P(None, "dp", "section"),
            P(None, "dp", "section"),
            P(),
            P(None, "dp", None),
            P(None, "dp", None),
            P(None, "dp", None),
            P(None, None, "dp", None),
            P(None, None, "dp", None),
            P(None, None, "dp"),
            P(None, "dp"),
            P(None, "dp"),
            P(None, "dp"),
            P(None, "dp"),
            P(None, "dp"),
            P(None, "dp"),
            P(None, "dp", None),
            P(None, "dp", None),
            P(None, "dp", None),
        ),
        out_specs=(
            P(None, "dp", "section"),
            P(None, "dp", "section"),
            P(None, "dp", None),
            P(None, "dp", None),
            P(None, "dp", None),
            P(None, None, "dp", None),
            P(None, None, "dp", None),
            P(None, None, "dp"),
            P(None, "dp"),
            P(None, "dp"),
            P(None, "dp"),
            P(None, "dp"),
            P(None, "dp"),
            P(None, "dp"),
            P(None, "dp", None),
            P(None, "dp", None),
            P(None, "dp", None),
        ),
        check_vma=False,
    )
```

profile of v0, /device:TPU:0, one launch (start us, length us, event | category | flops | bytes accessed | tf_op | source)
XLA Modules:
  0.0 7015.9 jit_solution(5096238380942299903)
XLA Ops:
  64.0 24.2 all-reduce.347
  92.4 42.2 all-gather.50.cloned.1.call-done
  134.6 65.6 all-gather.52.cloned.1.call-done
  200.2 127.7 %all-gather.54.cloned.1.call-done = bf16[1,2048,6144]{2,1,0:T(8,128)(2,1)} async-done(((bf16[1,256,6144]{2,1,0:T(8,128)(2,1)}), bf16[1,2048,6144]{2,1,0:T(8,128)(2,1)}) %all-gather.54.cloned.1.call-update) | async-done | bytes 25165840 | tf_op jit(solution)/shard_map/all_gather | solution.py:519
  327.9 127.7 %all-gather.56.cloned.1.call-done = bf16[1,2048,6144]{2,1,0:T(8,128)(2,1)} async-done(((bf16[1,256,6144]{2,1,0:T(8,128)(2,1)}), bf16[1,2048,6144]{2,1,0:T(8,128)(2,1)}) %all-gather.56.cloned.1.call-update) | async-done | bytes 25165840 | tf_op jit(solution)/shard_map/all_gather | solution.py:520
  455.5 127.8 %all-gather.58.cloned.1.call-done = bf16[1,6144,2048]{2,1,0:T(8,128)(2,1)} async-done(((bf16[1,768,2048]{2,1,0:T(8,128)(2,1)}), bf16[1,6144,2048]{2,1,0:T(8,128)(2,1)}) %all-gather.58.cloned.1.call-update) | async-done | bytes 25165840 | tf_op jit(solution)/shard_map/all_gather | solution.py:521
  617.8 19.8 all-gather.62.cloned.1.call-done
  637.6 872.7 %conditional.31 = (f32[128,2560]{0,1:T(8,128)S(1)}, f32[128,2560]{0,1:T(8,128)S(1)}, f32[128,2560]{1,0:T(8,128)}, f32[128,2560]{1,0:T(8,128)}, f32[128,2560]{1,0...) conditional(s32[]{:T(128)} %convert_element_type.931, () %tuple.807, ...), branch_computations={%region_5.6_spmd, %region_6.7_spmd} | conditional | flops 348562176 | bytes 161818528 | solution.py:154
  667.9 26.0 slice.2938
  693.8 26.3 slice.2909
  720.1 24.3 slice.2908
  745.8 25.9 slice.2906
  771.7 26.3 slice.2877
  798.0 24.5 slice.2876
  1393.4 27.1 pad.1153
  1420.5 26.9 pad.1139
  1450.2 26.8 pad.1152
  1481.5 26.5 pad.1138
  1610.8 880.8 %conditional.34 = (f32[128,2560]{0,1:T(8,128)S(1)}, f32[128,2560]{0,1:T(8,128)S(1)}, f32[1,128,2560]{2,1,0:T(8,128)}, f32[1,128,2560]{2,1,0:T(8,128)}, f32[1,128...) conditional(s32[]{:T(128)} %convert_element_type.934, () %tuple.815, ...), branch_computations={%region_16.17_spmd, %region_17.18_spmd} | conditional | flops 350528256 | bytes 167082432 | solution.py:154
  1643.7 25.9 slice.3012
  1669.6 26.3 slice.2983
  1695.9 24.3 slice.2982
  1720.2 25.9 slice.2980
  1746.1 26.5 slice.2951
  1772.6 24.3 slice.2950
  2374.6 26.9 pad.1181
  2401.4 27.1 pad.1167
  2431.4 26.6 pad.1180
  2462.5 26.6 pad.1166
  2623.6 30.0 collective-permute-start.5
  2905.3 897.7 %collective-permute-done.10 = bf16[128,2048]{1,0:T(8,128)(2,1)S(1)} collective-permute-done((bf16[128,2048]{1,0:T(8,128)(2,1)S(1)}, bf16[128,2048]{1,0:T(8,128)(2,1)S(1)}, u32[]{:S(2)}, u32[]{:S(2)}) %collective-permute-start.10) | collective-permute-done | bytes 524320 | tf_op jit(solution)/shard_map/ppermute | solution.py:23
  3898.5 16.8 conditional.51
  3962.9 440.1 %collective-permute-done.14 = bf16[128,2048]{1,0:T(8,128)(2,1)S(1)} collective-permute-done((bf16[128,2048]{1,0:T(8,128)(2,1)S(1)}, bf16[128,2048]{1,0:T(8,128)(2,1)S(1)}, u32[]{:S(2)}, u32[]{:S(2)}) %collective-permute-start.14) | collective-permute-done | bytes 524320 | tf_op jit(solution)/shard_map/ppermute | solution.py:23
  4405.6 235.8 %conditional.54 = (f32[128,2560]{1,0:T(8,128)}, f32[128,2560]{1,0:T(8,128)}, f32[128,2560]{1,0:T(8,128)}, bf16[128,2048]{1,0:T(8,128)(2,1)}, f32[2048]{0:T(1024)...) conditional(s32[]{:T(128)} %clamp.93, () %tuple.867, ...), branch_computations={%region_125.127_spmd, %region_126.128_spmd, %region_127.132_spmd} | conditional | flops 9687794688 | bytes 135275200 | solution.py:347
  4673.4 68.2 conditional.55
  4748.9 21.5 conditional.56
  4790.8 234.6 %conditional.57 = (f32[128,2560]{1,0:T(8,128)}, f32[128,2560]{1,0:T(8,128)}, f32[128,2560]{1,0:T(8,128)}, bf16[128,2048]{1,0:T(8,128)(2,1)}, f32[2048]{0:T(1024)...) conditional(s32[]{:T(128)} %clamp.94, () %tuple.875, ...), branch_computations={%region_148.150_spmd, %region_149.151_spmd, %region_150.155_spmd} | conditional | flops 9687794688 | bytes 135275168 | solution.py:347
  5056.9 61.8 conditional.58
  5163.2 21.4 conditional.59
  5311.5 64.5 reduce-scatter.12.cloned.1.call-done
  5376.1 85.5 %reduce-scatter.14.cloned.1.call-done = bf16[256,2560]{1,0:T(8,128)(2,1)} async-done(((bf16[2048,2560]{1,0:T(8,128)(2,1)}), bf16[256,2560]{1,0:T(8,128)(2,1)}) %reduce-scatter.14.cloned.1.call-update) | async-done | bytes 1310736 | tf_op jit(solution)/shard_map/reduce_scatter | solution.py:79
  5466.7 155.2 %reduce-scatter.22.cloned.1.call-done = bf16[256,6144]{1,0:T(8,128)(2,1)} async-done(((bf16[2048,6144]{1,0:T(8,128)(2,1)}), bf16[256,6144]{1,0:T(8,128)(2,1)}) %reduce-scatter.22.cloned.1.call-update) | async-done | bytes 3145744 | tf_op jit(solution)/shard_map/reduce_scatter | solution.py:79
  5622.0 160.4 %reduce-scatter.24.cloned.1.call-done = bf16[256,6144]{1,0:T(8,128)(2,1)} async-done(((bf16[2048,6144]{1,0:T(8,128)(2,1)}), bf16[256,6144]{1,0:T(8,128)(2,1)}) %reduce-scatter.24.cloned.1.call-update) | async-done | bytes 3145744 | tf_op jit(solution)/shard_map/reduce_scatter | solution.py:79
  5791.4 151.3 %reduce-scatter.26.cloned.1.call-done = bf16[768,2048]{1,0:T(8,128)(2,1)} async-done(((bf16[6144,2048]{1,0:T(8,128)(2,1)}), bf16[768,2048]{1,0:T(8,128)(2,1)}) %reduce-scatter.26.cloned.1.call-update) | async-done | bytes 3145744 | tf_op jit(solution)/shard_map/reduce_scatter | solution.py:79
  5951.0 30.0 reduce-scatter.28.cloned.1.call-done
  5982.0 23.5 all-reduce.346
  6006.2 22.7 all-reduce.348
  6033.0 938.4 %all-reduce.352.cloned.1.call-done = (bf16[2,128,2048]{2,1,0:T(8,128)(2,1)}, bf16[2,128,2048]{2,1,0:T(8,128)(2,1)}, bf16[2,256,2560]{2,1,0:T(8,128)(2,1)}, bf16[...) async-done(((bf16[2,128,2048]{2,1,0:T(8,128)(2,1)}, ...) | async-done | bytes 29491216 | tf_op jit(solution)/shard_map/psum | solution.py:54
  (2068 shorter events, 3074.2 us)
Async XLA Ops:
  7.2 81.0 %all-gather.48.cloned.1.call-start = ((), (), s32[]{:S(2)}) async-start(), calls=%async_computation.10 | async-start | bytes 1310720 | tf_op jit(solution)/shard_map/all_gather | solution.py:525
  7.9 83.1 %all-gather.46.cloned.1.call-start = ((), (), s32[]{:S(2)}) async-start(), calls=%async_computation.9 | async-start | bytes 1310720 | tf_op jit(solution)/shard_map/all_gather | solution.py:524
  8.7 125.9 %all-gather.50.cloned.1.call-start = ((), (), s32[]{:S(2)}) async-start(), calls=%async_computation.19 | async-start | bytes 11796480 | tf_op jit(solution)/shard_map/all_gather | solution.py:507
  10.1 190.1 %all-gather.52.cloned.1.call-start = ((), (), s32[]{:S(2)}) async-start(), calls=%async_computation.20 | async-start | bytes 11796480 | tf_op jit(solution)/shard_map/all_gather | solution.py:508
  12.6 315.2 %all-gather.54.cloned.1.call-start = ((), (), s32[]{:S(2)}) async-start(), calls=%async_computation.21 | async-start | bytes 28311552 | tf_op jit(solution)/shard_map/all_gather | solution.py:519
  16.6 438.9 %all-gather.56.cloned.1.call-start = ((), (), s32[]{:S(2)}) async-start(), calls=%async_computation.22 | async-start | bytes 28311552 | tf_op jit(solution)/shard_map/all_gather | solution.py:520
  20.6 562.8 %all-gather.58.cloned.1.call-start = ((), (), s32[]{:S(2)}) async-start(), calls=%async_computation.23 | async-start | bytes 28311552 | tf_op jit(solution)/shard_map/all_gather | solution.py:521
  24.6 593.2 %all-gather.60.cloned.1.call-start = ((), (), s32[]{:S(2)}) async-start(), calls=%async_computation.24 | async-start | bytes 1474560 | tf_op jit(solution)/shard_map/all_gather | solution.py:510
  26.3 611.3 %all-gather.62.cloned.1.call-start = ((), (), s32[]{:S(2)}) async-start(), calls=%async_computation.25 | async-start | bytes 1474560 | tf_op jit(solution)/shard_map/all_gather | solution.py:511
  27.0 1505.7 %all-gather.64.cloned.1.call-start = ((), (), s32[]{:S(2)}) async-start(), calls=%async_computation.26 | async-start | bytes 11796480 | tf_op jit(solution)/shard_map/all_gather | solution.py:509
  28.4 5277.0 %reduce-scatter.20.cloned.1.call-start = ((), (), s32[]{:S(2)}) async-start(), calls=%async_computation.15 | async-start | bytes 1474560 | tf_op jit(solution)/shard_map/reduce_scatter | solution.py:663
  39.5 543.9 %copy-start.424 = (bf16[2048]{0:T(1024)(128)(2,1)}, bf16[2048]{0:T(1024)(128)(2,1)S(1)}, u32[]{:S(2)}) copy-start(bf16[2048]{0:T(1024)(128)(2,1)S(1)} %reduce.61) | copy-start | bytes 12292
  48.4 534.9 %copy-start.418 = (bf16[2048]{0:T(1024)(128)(2,1)}, bf16[2048]{0:T(1024)(128)(2,1)S(1)}, u32[]{:S(2)}) copy-start(bf16[2048]{0:T(1024)(128)(2,1)S(1)} %reduce.60) | copy-start | bytes 12292
  92.4 491.0 %copy-start.54 = (bf16[2,128,2048]{2,1,0:T(8,128)(2,1)}, bf16[2,128,2048]{2,1,0:T(8,128)(2,1)S(1)}, u32[]{:S(2)}) copy-start(bf16[2,128,2048]{2,1,0:T(8,128)(2,1)S(1)} %get-tuple-element.6404) | copy-start | bytes 3145732
  598.8 13.6 collective-permute-start
  1549.9 26.5 collective-permute-start.1
  1590.9 14.3 collective-permute-start.2
  2532.2 24.5 collective-permute-start.3
  2563.3 14.3 collective-permute-start.4
  2621.1 34.6 copy-start.16
  2623.6 48.7 collective-permute-start.5
  2679.0 14.0 collective-permute-start.6
  2739.0 21.2 collective-permute-start.7
  2768.9 15.5 collective-permute-start.8
  2844.0 38.9 copy-start.20
  2895.8 3.4 collective-permute-start.9
  2903.6 901.9 %copy-start.98 = (bf16[2,128,2048]{2,1,0:T(8,128)(2,1)}, bf16[2,128,2048]{2,1,0:T(8,128)(2,1)S(1)}, u32[]{:S(2)}) copy-start(bf16[2,128,2048]{2,1,0:T(8,128)(2,1)S(1)} %get-tuple-element.5906) | copy-start | bytes 3145732
  2903.6 899.4 %copy-start.267 = (bf16[2,128,2048]{2,1,0:T(8,128)(2,1)S(1)}, bf16[2,128,2048]{2,1,0:T(8,128)(2,1)}, u32[]{:S(2)}) copy-start(bf16[2,128,2048]{2,1,0:T(8,128)(2,1)} %all-gather.48.cloned.1.call-done) | copy-start | bytes 3145732
  2903.6 899.4 %collective-permute-start.10 = (bf16[128,2048]{1,0:T(8,128)(2,1)S(1)}, bf16[128,2048]{1,0:T(8,128)(2,1)S(1)}, u32[]{:S(2)}, u32[]{:S(2)}) collective-permute-start(bf16[128,2048]{1,0:T(8,128)(2,1)S(1)} %get-tuple-element.5907), channel_id=1, source_target_pairs={{8,0},{16,8},{24,16},{9,1},{17,9},{25,17},{10,2},{18,10},{26,18},{... | collective-permute-start | bytes 1572872 | tf_op jit(solution)/shard_map/ppermute | solution.py:23
  2905.3 900.2 %copy-start.86 = (bf16[2,128,2560]{2,1,0:T(8,128)(2,1)}, bf16[2,128,2560]{2,1,0:T(8,128)(2,1)S(1)}, u32[]{:S(2)}) copy-start(bf16[2,128,2560]{2,1,0:T(8,128)(2,1)S(1)} %select_dynamic-update-slice_fusion.54) | copy-start | bytes 3932164
  3860.6 12.1 collective-permute-start.11
  3877.7 18.4 collective-permute-start.12
  3952.5 3.4 collective-permute-start.13
  3961.3 441.8 %copy-start.269 = (bf16[2,128,2048]{2,1,0:T(8,128)(2,1)S(1)}, bf16[2,128,2048]{2,1,0:T(8,128)(2,1)}, u32[]{:S(2)}) copy-start(bf16[2,128,2048]{2,1,0:T(8,128)(2,1)} %all-gather.48.cloned.1.call-done) | copy-start | bytes 3145732
  3961.3 441.8 %collective-permute-start.14 = (bf16[128,2048]{1,0:T(8,128)(2,1)S(1)}, bf16[128,2048]{1,0:T(8,128)(2,1)S(1)}, u32[]{:S(2)}, u32[]{:S(2)}) collective-permute-start(bf16[128,2048]{1,0:T(8,128)(2,1)S(1)} %get-tuple-element.5903), channel_id=1, source_target_pairs={{8,0},{16,8},{24,16},{9,1},{17,9},{25,17},{10,2},{18,10},{26,18},{... | collective-permute-start | bytes 1572872 | tf_op jit(solution)/shard_map/ppermute | solution.py:23
  3962.9 442.6 %copy-start.89 = (bf16[2,128,2560]{2,1,0:T(8,128)(2,1)}, bf16[2,128,2560]{2,1,0:T(8,128)(2,1)S(1)}, u32[]{:S(2)}) copy-start(bf16[2,128,2560]{2,1,0:T(8,128)(2,1)S(1)} %select_dynamic-update-slice_fusion.47) | copy-start | bytes 3932164
  4745.6 3.4 collective-permute-start.15
  4772.8 15.4 collective-permute-start.16
  5129.5 175.9 %reduce-scatter.18.cloned.1.call-start = ((), (), s32[]{:S(2)}) async-start(), calls=%async_computation.14 | async-start | bytes 1474560 | tf_op jit(solution)/shard_map/reduce_scatter | solution.py:660
  5143.5 164.2 %reduce-scatter.16.cloned.1.call-start = ((), (), s32[]{:S(2)}) async-start(), calls=%async_computation.13 | async-start | bytes 11796480 | tf_op jit(solution)/shard_map/reduce_scatter | solution.py:79
  5152.2 223.9 %reduce-scatter.12.cloned.1.call-start = ((), (), s32[]{:S(2)}) async-start(), calls=%async_computation.11 | async-start | bytes 11796480 | tf_op jit(solution)/shard_map/reduce_scatter | solution.py:79
  5160.1 3.1 collective-permute-start.17
  5191.5 270.0 %reduce-scatter.14.cloned.1.call-start = ((), (), s32[]{:S(2)}) async-start(), calls=%async_computation.12 | async-start | bytes 11796480 | tf_op jit(solution)/shard_map/reduce_scatter | solution.py:79
  5200.6 421.4 %reduce-scatter.22.cloned.1.call-start = ((), (), s32[]{:S(2)}) async-start(), calls=%async_computation.16 | async-start | bytes 28311552 | tf_op jit(solution)/shard_map/reduce_scatter | solution.py:79
  5236.5 545.9 %reduce-scatter.24.cloned.1.call-start = ((), (), s32[]{:S(2)}) async-start(), calls=%async_computation.17 | async-start | bytes 28311552 | tf_op jit(solution)/shard_map/reduce_scatter | solution.py:79
  5267.3 675.4 %reduce-scatter.26.cloned.1.call-start = ((), (), s32[]{:S(2)}) async-start(), calls=%async_computation.18 | async-start | bytes 28311552 | tf_op jit(solution)/shard_map/reduce_scatter | solution.py:79
  5298.4 682.5 %reduce-scatter.28.cloned.1.call-start = ((), (), s32[]{:S(2)}) async-start(), calls=%async_computation.27 | async-start | bytes 737280
  5302.6 1668.7 %all-reduce.352.cloned.1.call-start = ((), (), s32[]{:S(2)}) async-start(), calls=%async_computation.28 | async-start | bytes 58982400 | tf_op jit(solution)/shard_map/psum | solution.py:54
  (355 other events, 1740.3 us)
Sparse Core Ops, SparseCore 0:
  9.6 30.6 all-gather.47
  41.8 27.4 all-gather.45
  71.8 62.7 all-gather.49
  136.9 63.2 all-gather.51
  202.5 125.3 all-gather.53
  330.2 125.3 all-gather.55
  458.0 125.3 all-gather.57
  585.8 24.5 all-gather.59
  613.0 24.5 all-gather.61
  639.3 63.5 all-gather.63
  5129.6 34.8 reduce-scatter.19
  5167.6 37.3 reduce-scatter.17
  5209.0 81.5 reduce-scatter.15
  5294.5 81.5 reduce-scatter.11
  5380.0 81.5 reduce-scatter.13
  5465.1 156.8 reduce-scatter.21
  5625.4 156.8 reduce-scatter.23
  5785.8 156.8 reduce-scatter.25
  5946.4 34.5 reduce-scatter.27
  5986.5 984.7 all-reduce.351
where the time goes:
time: 7070 us; the launch traced here: 7020 us
  waiting for transfers between devices  3470 us (49%)
  local copies, waits for them, and re-layouts  2200 us (31%)
  other arithmetic  743 us (11%)
  blocking collectives  286 us (4%)
  matrix products  159 us (2%)
  loops' own time  82.1 us (1%)
    ppermute x18, waiting for transfers between devices, passed_along(): lax.ppermute(value, axis, [(source, source + steps) for source in range(l...  1370 us
    slice x166, local copies, waits for them, and re-layouts, local_scan(): return lax.associative_scan(combine_pair, (decays, drives), axis=0)  1060 us
    psum x1, waiting for transfers between devices, from_root(): return lax.psum(block, axis)  938 us
    pad x96, local copies, waits for them, and re-layouts, local_scan(): return lax.associative_scan(combine_pair, (decays, drives), axis=0)  669 us
    reduce_scatter x6, waiting for transfers between devices, spread_term(): lax.psum_scatter(rows_outer(lax.slice_in_dim(left, 0, share * lax.axis_si...  617 us
    select_n x125, other arithmetic, store(): jnp.where(active, lax.dynamic_update_index_in_dim(buffer, values, slot_in...  227 us
    all_gather x20, blocking collectives, prefix(): everything = jax.tree.map(lambda part: lax.all_gather(part, axis), value)  185 us
  transfers between devices with their start and end apart: 38, of which 18 were waited for; matrix products, arithmetic and copies ran while one was open for 18% of the time, Pallas kernels for 0%

commit v1 on v0

v1 whole, which is shorter than its diff:
```python
import jax
import jax.numpy as jnp
from jax import lax
from jax.experimental import pallas as pl
from jax.experimental.pallas import tpu as pltpu
from jax.sharding import PartitionSpec as P

D = 2048
H = 10
BW = 256
F = 6144
R = 2560
CONV = 4
MICRO = 2
LAYERS = 2
MARGIN = CONV - 1
WIN = 2 * BW

EPS = 1e-06
LRU_EPS = 0.04
RATE_SCALE = 8.0


def low(value):
    return value.astype(jnp.bfloat16)


def high(value):
    return value.astype(jnp.float32)


def dot(left, right):
    return jnp.dot(left, right, preferred_element_type=jnp.float32)


def dot_nt(left, right):
    return lax.dot_general(
        left, right, (((1,), (1,)), ((), ())), preferred_element_type=jnp.float32
    )


def dot_tn(left, right):
    return lax.dot_general(
        left, right, (((0,), (0,)), ((), ())), preferred_element_type=jnp.float32
    )


def rms_scale(values, scales):
    return values * lax.rsqrt(jnp.mean(values * values, axis=-1, keepdims=True) + EPS) * scales


def meeting_order(count):
    return list(range(0, count, 2)) + list(range(1, count, 2))


def swapped(value, offset):
    count = lax.axis_size("dp")
    return lax.ppermute(value, "dp", [(at, at ^ offset) for at in range(count)])


def gather_rows(block):
    count = lax.axis_size("dp")
    same_core = jnp.concatenate([block] + [swapped(block, k) for k in range(2, count, 2)], axis=0)
    other_core = swapped(same_core, 1)
    return jnp.concatenate([same_core, other_core], axis=0)


def scatter_product(product, left):
    count = lax.axis_size("dp")
    half = left.shape[0] // 2
    rows = left.shape[0] // count
    away = swapped(low(product(left[half:])), 1)
    here = product(left[:half]) + high(away)
    total = here[:rows]
    for k in range(2, count, 2):
        piece = here[(k // 2) * rows : (k // 2 + 1) * rows]
        total = total + high(swapped(low(piece), k))
    return total


def spread(pack):
    return lax.all_to_all(pack, "dp", 0, 0, tiled=False)


def section_sum(chunks):
    rank = lax.axis_index("section")
    pick = lambda value, at: lax.dynamic_index_in_dim(value, at, 0, keepdims=False)
    part = lambda value, at, size: lax.dynamic_slice_in_dim(value, at, size, 0)
    first = lax.ppermute(
        part(chunks, jnp.where(rank == 0, 1, 0), 3), "section", [(0, 1), (3, 2)]
    )
    second_own = part(chunks, jnp.where(rank == 1, 2, 0), 2)
    second_came = part(first, jnp.where(rank == 1, 1, 0), 2)
    second = lax.ppermute(
        low(high(second_own) + high(second_came)), "section", [(1, 2), (2, 1)]
    )
    lower_half = rank == 1
    third = lax.ppermute(
        low(
            high(pick(chunks, jnp.where(lower_half, 0, 3)))
            + high(pick(second, jnp.where(lower_half, 0, 1)))
        ),
        "section",
        [(1, 0), (2, 3)],
    )
    return (
        high(pick(chunks, rank))
        + high(pick(first, jnp.where(lower_half, 0, 2)))
        + high(pick(second, jnp.where(lower_half, 1, 0)))
        + high(third)
    )


def window_of(device, count):
    own = R // count
    first_block = min(own * device // BW, H - 2)
    return own * device, own * (device + 1), BW * first_block, BW * first_block + WIN


def own_first(matrix, device, count):
    begin, end, left, right = window_of(device, count)
    return [matrix[:, begin:end], matrix[:, end:right], matrix[:, left:begin]]


def turned(value, axis, shift):
    size = value.shape[axis]
    twice = jnp.concatenate([value, value], axis=axis)
    return lax.dynamic_slice_in_dim(twice, jnp.mod(shift, size), size, axis)


def forward_scan_kernel(decay_ref, drive_ref, reach_ref, state_ref):
    rows = decay_ref.shape[1]
    reach = decay_ref[:, 0, :]
    state = drive_ref[:, 0, :]
    reach_ref[:, 0, :] = reach
    state_ref[:, 0, :] = state
    for row in range(1, rows):
        decay = decay_ref[:, row, :]
        state = decay * state + drive_ref[:, row, :]
        reach = decay * reach
        reach_ref[:, row, :] = reach
        state_ref[:, row, :] = state


def backward_scan_kernel(decay_ref, grad_ref, reach_ref, local_ref, top_ref):
    rows = decay_ref.shape[1]
    reach = jnp.ones_like(decay_ref[:, 0, :])
    local = grad_ref[:, rows - 1, :]
    reach_ref[:, rows - 1, :] = reach
    local_ref[:, rows - 1, :] = local
    for row in range(rows - 2, -1, -1):
        decay = decay_ref[:, row + 1, :]
        local = decay * local + grad_ref[:, row, :]
        reach = decay * reach
        reach_ref[:, row, :] = reach
        local_ref[:, row, :] = local
    top_ref[0] = decay_ref[:, 0, :] * reach
    top_ref[1] = decay_ref[:, 0, :] * local


def carry_kernel(reverse, where_ref, totals_ref, carry_ref):
    planes, count = totals_ref.shape[0], totals_ref.shape[2]
    me, rank = where_ref[0], where_ref[1]
    state = jnp.zeros(carry_ref.shape[1:], jnp.float32)
    for step in range(count):
        device = count - 1 - step if reverse else step
        offset = jnp.bitwise_xor(me, device)
        at = offset // 2 + (offset % 2) * (count // 2)
        for plane in range(planes - 1, -1, -1) if reverse else range(planes):

            @pl.when(rank == plane)
            def _(state=state, at=at):
                carry_ref[at] = state

            state = totals_ref[plane, 0, at] * state + totals_ref[plane, 1, at]


VMEM_SPEC = pl.BlockSpec(memory_space=pltpu.VMEM)


def in_vmem(kernel, shapes, *operands, scalars=0):
    specs = [pl.BlockSpec(memory_space=pltpu.SMEM)] * scalars
    return pl.pallas_call(
        kernel,
        out_shape=tuple(jax.ShapeDtypeStruct(shape, jnp.float32) for shape in shapes),
        in_specs=specs + [VMEM_SPEC] * (len(operands) - scalars),
        out_specs=tuple(VMEM_SPEC for _ in shapes),
        compiler_params=pltpu.CompilerParams(vmem_limit_bytes=40 * 1024 * 1024),
    )(*operands)


def carried(totals, reverse):
    count = lax.axis_size("dp")
    channels = totals.shape[-1]
    everything = lax.all_gather(
        totals.reshape(2, count, MICRO, channels), "section", axis=0, tiled=False
    )
    where = jnp.stack([lax.axis_index("dp"), lax.axis_index("section")]).astype(jnp.int32)

    def kernel(where_ref, totals_ref, carry_ref):
        carry_kernel(reverse, where_ref, totals_ref, carry_ref)

    (carry,) = in_vmem(kernel, [(count, MICRO, channels)], where, everything, scalars=1)
    return carry.reshape(count * MICRO, channels)


def gelu_product(states, side):
    return states * jax.nn.gelu(side)


def gated_gelu(gate_val, up_val):
    return jax.nn.gelu(gate_val) * up_val


def local(
    inputs,
    cotangent,
    resets,
    branch_in,
    gate_in,
    rec_out,
    rate_gate,
    input_gate,
    conv_taps,
    conv_bias,
    rate_bias,
    input_bias,
    decay_param,
    norm_rec,
    norm_mlp,
    mlp_gate,
    mlp_up,
    mlp_down,
):
    planes = lax.axis_size("section")
    count = lax.axis_size("dp")
    rank = lax.axis_index("section")
    me = lax.axis_index("dp")
    block_rows = inputs.shape[1]
    length = block_rows // planes
    seq = resets.shape[1]
    rows = MICRO * length
    segments = MICRO * count
    tokens = segments * length
    own = R // count
    wide = F // count
    strip = D // count
    thin = strip // planes
    order = jnp.array(meeting_order(count), jnp.int32)
    devices = jnp.bitwise_xor(me, order)

    small = jnp.concatenate(
        [
            norm_rec,
            norm_mlp,
            conv_taps.reshape(LAYERS, CONV * own),
            conv_bias,
        ],
        axis=1,
    )
    small_all = lax.all_gather(small, "dp", axis=0, tiled=False)
    own_begin = own * me
    first_block = jnp.minimum(own_begin // BW, H - 2)
    shift = own_begin - BW * first_block

    def small_whole(layer, begin, each):
        return small_all[:, layer, begin : begin + each].reshape(count * each)

    weights = []
    for layer in range(LAYERS):
        in_pack = jnp.stack(
            [
                jnp.concatenate(
                    own_first(branch_in[layer], device, count)
                    + [gate_in[layer][:, own * device : own * (device + 1)]],
                    axis=1,
                )
                for device in range(count)
            ]
        )
        gates = jnp.stack([rate_gate[layer], input_gate[layer]])
        gate_pack = jnp.stack(
            [
                gates[:, window_of(device, count)[2] // BW : window_of(device, count)[3] // BW]
                for device in range(count)
            ]
        )
        mlp_pack = jnp.concatenate(
            [
                mlp_gate[layer].reshape(strip, count, wide),
                mlp_up[layer].reshape(strip, count, wide),
            ],
            axis=2,
        ).transpose(1, 0, 2)
        in_weight = spread(in_pack).reshape(D, WIN + own)
        gate_rows = spread(gate_pack)
        blocks = gate_rows.transpose(1, 2, 0, 3, 4).reshape(2, 2, BW, BW)
        empty = jnp.zeros((BW, BW), jnp.bfloat16)
        gate_weights = []
        for which in range(2):
            whole = jnp.concatenate(
                [
                    jnp.concatenate([blocks[which, 0], empty], axis=1),
                    jnp.concatenate([empty, blocks[which, 1]], axis=1),
                ],
                axis=0,
            )
            gate_weights.append(turned(turned(whole, 0, shift), 1, shift)[:, :own])
        taps = jnp.concatenate(
            [
                small_all[:, layer, 2 * strip :].reshape(count, CONV + 1, own),
            ],
            axis=0,
        )
        taps = taps.transpose(1, 0, 2).reshape(CONV + 1, R)
        taps = lax.dynamic_slice_in_dim(taps, BW * first_block, WIN, 1)
        taps = high(turned(taps, 1, shift))
        weights.append(
            {
                "in": in_weight,
                "gates": jnp.concatenate(gate_weights, axis=1),
                "out": rec_out[layer],
                "taps": taps[:CONV],
                "bias": taps[CONV],
                "rate_bias": high(rate_bias[layer]),
                "input_bias": high(input_bias[layer]),
                "decay": high(decay_param[layer]),
                "norm_rec": high(small_whole(layer, 0, strip)),
                "norm_mlp": high(small_whole(layer, strip, strip)),
                "mlp": spread(mlp_pack).reshape(D, 2 * wide),
                "down": mlp_down[layer],
            }
        )

    keep = (1 - resets).astype(jnp.float32)
    padded = jnp.concatenate(
        [
            jnp.ones((MICRO, MARGIN), jnp.float32),
            keep,
            jnp.zeros((MICRO, length), jnp.float32),
        ],
        axis=1,
    )
    reach = 2 * MARGIN
    window = jnp.concatenate(
        [
            padded[:, :seq].reshape(MICRO, count, planes, length),
            padded[:, length : length + seq].reshape(MICRO, count, planes, length)[..., :reach],
        ],
        axis=3,
    )
    window = lax.dynamic_index_in_dim(window, rank, 2, keepdims=False)
    same = (devices[:, None] == jnp.arange(count)[None, :]).astype(jnp.float32)
    window = jnp.einsum("pj,mjr->pmr", same, window, precision=lax.Precision.HIGHEST)
    window = window.reshape(segments, length + reach)
    usable = [jnp.ones((segments, length + MARGIN, 1), jnp.float32)]
    for lag in range(1, CONV):
        begin = MARGIN - lag + 1
        usable.append(usable[-1] * window[:, begin : begin + length + MARGIN, None])
    carry_mask = window[:, MARGIN : MARGIN + length, None]

    edge_from = {}
    for step, plane in ((1, 0), (-1, planes - 1)):
        wanted = devices - jnp.where(rank == plane, step, 0)
        edge_from[step] = (wanted[:, None] == devices[None, :]).astype(jnp.float32)

    def edge(rows_out, step):
        came = lax.ppermute(
            rows_out, "section", [(at, (at + step) % planes) for at in range(planes)]
        )
        flat = came.reshape(count, -1)
        chosen = edge_from[step]
        moved = sum(chosen[:, q : q + 1] * flat[q][None] for q in range(count))
        return moved.reshape(rows_out.shape)

    def lru_parts(weight):
        rate = RATE_SCALE * jax.nn.softplus(-weight["decay"])
        return rate

    def rec_forward(section_in, weight):
        normed = low(rms_scale(high(section_in), weight["norm_rec"]))
        normed = gather_rows(normed)
        both = dot(normed, weight["in"])
        branch = both[:, :WIN].reshape(segments, length, WIN)
        side = both[:, WIN:].reshape(segments, length, own)
        extended = jnp.concatenate([edge(branch[:, length - MARGIN :], 1), branch], axis=1)
        conved = weight["bias"] + weight["taps"][0] * branch
        for lag in range(1, CONV):
            conved = (
                conved
                + weight["taps"][lag]
                * usable[lag][:, :length]
                * extended[:, MARGIN - lag : MARGIN - lag + length]
            )
        conv_low = low(conved).reshape(tokens, WIN)
        raw = dot(conv_low, weight["gates"])
        rate_sig = jax.nn.sigmoid(raw[:, :own] + weight["rate_bias"])
        input_sig = jax.nn.sigmoid(raw[:, own:] + weight["input_bias"])
        rate_sig = rate_sig.reshape(segments, length, own)
        input_sig = input_sig.reshape(segments, length, own)
        conved = conved[:, :, :own]
        decays = jnp.exp(-lru_parts(weight) * rate_sig) * carry_mask
        root = jnp.sqrt(1.0 + LRU_EPS - decays * decays)
        drives = root * input_sig * conved
        shape = (segments, length, own)
        cumulative, partial = in_vmem(forward_scan_kernel, [shape, shape], decays, drives)
        carry = carried(jnp.stack([cumulative[:, -1], partial[:, -1]]), False)
        states = partial + cumulative * carry[:, None]
        mixture = low(gelu_product(states, side)).reshape(tokens, own)
        result = high(section_in) + scatter_product(
            lambda left: dot(left, weight["out"]), mixture
        )
        kept = {
            "section_in": section_in,
            "normed": normed,
            "extended": extended,
            "side": side,
            "conved": conved,
            "conv_low": conv_low,
            "rate_sig": rate_sig,
            "input_sig": input_sig,
            "decays": decays,
            "root": root,
            "carry": carry,
            "states": states,
            "mixture": mixture,
        }
        return low(result), kept

    def mlp_forward(section_in, weight):
        normed = low(rms_scale(high(section_in), weight["norm_mlp"]))
        normed = gather_rows(normed)
        both = dot(normed, weight["mlp"])
        gate_val, up_val = both[:, :wide], both[:, wide:]
        hidden = low(gated_gelu(gate_val, up_val))
        result = high(section_in) + scatter_product(
            lambda left: dot(left, weight["down"]), hidden
        )
        kept = {
            "section_in": section_in,
            "normed": normed,
            "gate_val": gate_val,
            "up_val": up_val,
            "hidden": hidden,
        }
        return low(result), kept

    def mlp_backward(grad, weight, kept):
        grad_all = gather_rows(grad)
        grad_hidden = dot_nt(grad_all, weight["down"])
        _, pull = jax.vjp(gated_gelu, kept["gate_val"], kept["up_val"])
        gate_grad, up_grad = pull(grad_hidden)
        both = low(jnp.concatenate([gate_grad, up_grad], axis=1))
        grad_normed = scatter_product(lambda left: dot_nt(left, weight["mlp"]), both)
        _, pull = jax.vjp(rms_scale, high(kept["section_in"]), weight["norm_mlp"])
        grad_in, norm_grad = pull(grad_normed)
        terms = {
            "mlp": dot_tn(kept["normed"], both),
            "down": dot_tn(kept["hidden"], grad_all),
            "norm_mlp": norm_grad,
        }
        return low(grad_in + high(grad)), terms

    def rec_backward(grad, weight, kept):
        grad_all = gather_rows(grad)
        shape = (segments, length, own)
        grad_mixture = dot_nt(grad_all, weight["out"]).reshape(shape)
        _, pull = jax.vjp(gelu_product, kept["states"], kept["side"])
        grad_states0, grad_side = pull(grad_mixture)
        decays, root = kept["decays"], kept["root"]
        reached, partial, top = in_vmem(
            backward_scan_kernel,
            [shape, shape, (2, segments, own)],
            decays,
            grad_states0,
        )
        carry = carried(top, True)
        grad_states = partial + reached * carry[:, None]
        previous = jnp.concatenate([kept["carry"][:, None], kept["states"][:, :-1]], axis=1)
        conved, rate_sig, input_sig = kept["conved"], kept["rate_sig"], kept["input_sig"]
        grad_decays = grad_states * (previous - input_sig * conved * decays / root)
        slope = grad_decays * decays * rate_sig
        rate_grad = slope * (-lru_parts(weight)) * (1.0 - rate_sig)
        input_grad = grad_states * root * conved * input_sig * (1.0 - input_sig)
        raw_grad = low(
            jnp.concatenate([rate_grad, input_grad], axis=2).reshape(tokens, 2 * own)
        )
        spare = jnp.zeros((segments, length, WIN - own), jnp.float32)
        conv_grad = jnp.concatenate([grad_states * root * input_sig, spare], axis=2)
        conv_grad = conv_grad + dot_nt(raw_grad, weight["gates"]).reshape(segments, length, WIN)
        longer = jnp.concatenate([conv_grad, edge(conv_grad[:, :MARGIN], -1)], axis=1)
        branch_grad = weight["taps"][0] * conv_grad
        taps_grad = [jnp.sum(kept["extended"][:, MARGIN:] * conv_grad, axis=(0, 1))]
        for lag in range(1, CONV):
            branch_grad = (
                branch_grad
                + weight["taps"][lag]
                * usable[lag][:, lag : lag + length]
                * longer[:, lag : lag + length]
            )
            taps_grad.append(
                jnp.sum(
                    usable[lag][:, :length]
                    * kept["extended"][:, MARGIN - lag : MARGIN - lag + length]
                    * conv_grad,
                    axis=(0, 1),
                )
            )
        both = low(
            jnp.concatenate([branch_grad, grad_side], axis=2).reshape(tokens, WIN + own)
        )
        grad_normed = scatter_product(lambda left: dot_nt(left, weight["in"]), both)
        _, pull = jax.vjp(rms_scale, high(kept["section_in"]), weight["norm_rec"])
        grad_in, norm_grad = pull(grad_normed)
        terms = {
            "in": dot_tn(kept["normed"], both),
            "out": dot_tn(kept["mixture"], grad_all),
            "gates": dot_tn(kept["conv_low"], raw_grad),
            "taps": jnp.stack(taps_grad + [jnp.sum(conv_grad, axis=(0, 1))]),
            "rate_bias": jnp.sum(rate_grad, axis=(0, 1)),
            "input_bias": jnp.sum(input_grad, axis=(0, 1)),
            "decay": jnp.sum(slope, axis=(0, 1)) * RATE_SCALE * jax.nn.sigmoid(-weight["decay"]),
            "norm_rec": norm_grad,
        }
        return low(grad_in + high(grad)), terms

    def planes_first(term):
        split = low(term).reshape(count, planes, thin, term.shape[1])
        return split.transpose(1, 0, 2, 3)

    def gathered(piece, axis=0):
        return lax.all_gather(piece, "section", axis=axis, tiled=True)

    def mlp_gradients(terms):
        mine = spread(low(section_sum(planes_first(terms["mlp"]))))
        mine = mine.transpose(1, 0, 2)
        gate = mine[:, :, :wide].reshape(thin, F)
        up = mine[:, :, wide:].reshape(thin, F)
        down = low(section_sum(low(terms["down"]).reshape(planes, wide // planes, D)))
        return high(gathered(gate)), high(gathered(up)), high(gathered(down))

    def rec_gradients(terms):
        mine = high(spread(low(section_sum(planes_first(terms["in"])))))
        gate = low(mine[:, :, WIN:]).transpose(1, 0, 2).reshape(thin, R)
        branch = mine[:, :, :own].transpose(1, 0, 2).reshape(thin, R)
        for device in range(count):
            begin, end, left, right = window_of(device, count)
            if right > end:
                piece = mine[device, :, own : own + right - end]
                branch = branch + jnp.pad(piece, ((0, 0), (end, R - right)))
            if begin > left:
                piece = mine[device, :, own + right - end : WIN]
                branch = branch + jnp.pad(piece, ((0, 0), (left, R - begin)))
        out = low(section_sum(low(terms["out"]).reshape(planes, own // planes, D)))
        rows_each = BW // count
        blocks = []
        for which in range(2):
            square = jnp.concatenate(
                [
                    terms["gates"][:, which * own : (which + 1) * own],
                    jnp.zeros((WIN, WIN - own), jnp.float32),
                ],
                axis=1,
            )
            square = turned(turned(square, 0, -shift), 1, -shift)
            blocks.append(jnp.stack([square[:BW, :BW], square[BW:, BW:]]))
        blocks = low(jnp.stack(blocks)).reshape(
            2, 2, count, planes, rows_each // planes, BW
        )
        blocks = spread(low(section_sum(blocks.transpose(3, 2, 0, 1, 4, 5))))
        totals = [0.0] * H
        for device in range(count):
            first = window_of(device, count)[2] // BW
            for at in range(2):
                totals[first + at] = totals[first + at] + high(blocks[device, :, at])
        gates = gathered(low(jnp.stack(totals, axis=1)), 2)
        return (
            high(gathered(low(branch))),
            high(gathered(gate)),
            high(gathered(out)),
            high(gates[0]),
            high(gates[1]),
        )

    def small_gradients(terms):
        taps = turned(terms["taps"], 1, -shift)
        taps = lax.dynamic_update_slice(
            jnp.zeros((CONV + 1, R), jnp.float32), taps, (0, BW * first_block)
        )
        owned = jnp.stack([terms["rate_bias"], terms["input_bias"], terms["decay"]])
        owned = lax.dynamic_update_slice(
            jnp.zeros((3, R), jnp.float32), owned, (0, own_begin)
        )
        channels = jnp.concatenate([taps, owned], axis=0)
        norms = jnp.stack([terms["norm_rec"], terms["norm_mlp"]])
        flat = jnp.concatenate([channels.reshape(-1), norms.reshape(-1)])
        flat = lax.psum(flat.reshape(-1, 128), ("section", "dp")).reshape(-1)
        channels = flat[: (CONV + 4) * R].reshape(CONV + 4, R)
        norms = flat[(CONV + 4) * R :].reshape(2, D)
        channels = lax.dynamic_slice_in_dim(channels, own_begin, own, 1)
        norms = lax.dynamic_slice_in_dim(norms, strip * me, strip, 1)
        return channels, norms

    def by_tokens(value):
        moved = lax.all_to_all(value, "section", split_axis=1, concat_axis=2, tiled=True)
        return moved.reshape(rows, D)

    def by_features(value):
        moved = value.reshape(MICRO, length, D)
        return lax.all_to_all(moved, "section", split_axis=2, concat_axis=1, tiled=True)

    stream = by_tokens(inputs)
    kept = []
    for layer in range(LAYERS):
        stream, kept_rec = rec_forward(stream, weights[layer])
        stream, kept_mlp = mlp_forward(stream, weights[layer])
        kept.append((kept_rec, kept_mlp))
    output = by_features(stream)
    grad = by_tokens(cotangent)
    results = [None] * LAYERS
    for layer in reversed(range(LAYERS)):
        grad, mlp_terms = mlp_backward(grad, weights[layer], kept[layer][1])
        mlp_grads = mlp_gradients(mlp_terms)
        grad, rec_terms = rec_backward(grad, weights[layer], kept[layer][0])
        rec_grads = rec_gradients(rec_terms)
        channels, norms = small_gradients({**mlp_terms, **rec_terms})
        results[layer] = rec_grads + (
            channels[:CONV],
            channels[CONV],
            channels[CONV + 1],
            channels[CONV + 2],
            channels[CONV + 3],
            norms[0],
            norms[1],
        ) + mlp_grads
    input_grad = by_features(grad)
    stacked = tuple(jnp.stack(parts) for parts in zip(*results))
    return (output, input_grad) + stacked


def solution(mesh):
    return jax.shard_map(
        local,
        mesh=mesh,
        in_specs=(
            P(None, "dp", "section"),
            P(None, "dp", "section"),
            P(),
            P(None, "dp", None),
            P(None, "dp", None),
            P(None, "dp", None),
            P(None, None, "dp", None),
            P(None, None, "dp", None),
            P(None, None, "dp"),
            P(None, "dp"),
            P(None, "dp"),
            P(None, "dp"),
            P(None, "dp"),
            P(None, "dp"),
            P(None, "dp"),
            P(None, "dp", None),
            P(None, "dp", None),
            P(None, "dp", None),
        ),
        out_specs=(
            P(None, "dp", "section"),
            P(None, "dp", "section"),
            P(None, "dp", None),
            P(None, "dp", None),
            P(None, "dp", None),
            P(None, None, "dp", None),
            P(None, None, "dp", None),
            P(None, None, "dp"),
            P(None, "dp"),
            P(None, "dp"),
            P(None, "dp"),
            P(None, "dp"),
            P(None, "dp"),
            P(None, "dp"),
            P(None, "dp", None),
            P(None, "dp", None),
            P(None, "dp", None),
        ),
        check_vma=False,
    )
```

time: 7070 us -> 2050 us (0.29)
  waiting for transfers between devices: 3470 us -> 1090 us
  local copies, waits for them, and re-layouts: 2200 us -> 210 us
  other arithmetic: 743 us -> 220 us
  starting transfers between devices: 64.6 us -> 240 us
  blocking collectives: 286 us -> 141 us
  loops' own time: 82.1 us -> 0 us
    slice x198 -> x73, local copies, waits for them, and re-layouts: 1080 us -> 34.3 us  [the longest x14 9.16 us: own_first(): return [matrix[:, begin:end], matrix[:, end:right], matrix[:, left:begin]]]
    psum x1, waiting for transfers between devices: 938 us -> 0.02 us  [small_gradients(): flat = lax.psum(flat.reshape(-1, 128), ('section', 'dp')).reshape(-1)]
    pad x96 -> x0, local copies, waits for them, and re-layouts: 669 us -> none  [local_scan(): return lax.associative_scan(combine_pair, (decays, drives), axis=0)]
    reduce_scatter x8 -> x0, waiting for transfers between devices: 617 us -> none  [the longest x6 617 us: spread_term(): lax.psum_scatter(rows_outer(lax.slice_in_dim(left, 0, share * lax.axis_si...]
    all_gather x10 -> x12, waiting for transfers between devices: 511 us -> 49.9 us  [gathered(): return lax.all_gather(piece, 'section', axis=axis, tiled=True)]
    ppermute x18 -> x98, waiting for transfers between devices: 1370 us -> 1020 us  [the longest x10 499 us: section_sum(): lax.ppermute(part(chunks, jnp.where(rank == 0, 1, 0), 3), 'section', [(0,...]
    select_n x207 -> x0, other arithmetic: 278 us -> none  [the longest x125 227 us: store(): jnp.where(active, lax.dynamic_update_index_in_dim(buffer, values, slot_in...]
    add x108 -> x6, other arithmetic: 192 us -> 2.9 us  [the longest x4 2.27 us: edge(): moved = sum((chosen[:, q:q + 1] * flat[q][None] for q in range(count)))]
  transfers between devices with their start and end apart: 38 -> 126, of which waited for: 18 -> 60; matrix products, arithmetic and copies ran while one was open for 18% -> 23% of each run, Pallas kernels for 0% -> 0%
where the time goes in v1:
time: 2050 us; the launch traced here: 2040 us
  waiting for transfers between devices  1090 us (53%)
  starting transfers between devices  240 us (12%)
  other arithmetic  220 us (11%)
  local copies, waits for them, and re-layouts  210 us (10%)
  blocking collectives  141 us (7%)
  matrix products  105 us (5%)
  between operations  21.1 us (1%)
    ppermute x10, waiting for transfers between devices, section_sum(): lax.ppermute(part(chunks, jnp.where(rank == 0, 1, 0), 3), 'section', [(0,...  499 us
    ppermute x64, waiting for transfers between devices, swapped(): return lax.ppermute(value, 'dp', [(at, at ^ offset) for at in range(count)])  263 us
    ppermute x10, waiting for transfers between devices, section_sum(): lax.ppermute(low(high(pick(chunks, jnp.where(lower_half, 0, 3))) + high(p...  247 us
    ppermute x10, starting transfers between devices, section_sum(): lax.ppermute(part(chunks, jnp.where(rank == 0, 1, 0), 3), 'section', [(0,...  80.2 us
    convert_element_type x38, other arithmetic, low(): return value.astype(jnp.bfloat16)  80.2 us
    unnamed x655, local copies, waits for them, and re-layouts  72.3 us
    all_gather x4, blocking collectives, carried(): lax.all_gather(totals.reshape(2, count, MICRO, channels), 'section', axis...  69.6 us
    ppermute x64, starting transfers between devices, swapped(): return lax.ppermute(value, 'dp', [(at, at ^ offset) for at in range(count)])  59.1 us
  transfers between devices with their start and end apart: 126, of which 60 were waited for; matrix products, arithmetic and copies ran while one was open for 23% of the time, Pallas kernels for 0%

profile of v1, /device:TPU:0, one launch (start us, length us, event | category | flops | bytes accessed | tf_op | source)
XLA Modules:
  0.0 2035.6 jit_solution(1110150381114666738)
XLA Ops:
  9.9 6.3 all-to-all-start
  27.5 9.3 all-gather.1
  108.1 25.3 %collective-permute-done.2 = bf16[64,2048]{1,0:T(8,128)(2,1)} collective-permute-done((bf16[64,2048]{1,0:T(8,128)(2,1)}, bf16[64,2048]{1,0:T(8,128)(2,1)}, u32[]{:S(2)}, u32[]{:S(2)}) %collective-permute-start.2) | collective-permute-done | bytes 262176 | tf_op jit(solution)/shard_map/ppermute | solution.py:58
  173.7 13.7 all_gather.62
  201.3 30.0 %collective-permute-done.6 = bf16[64,2048]{1,0:T(8,128)(2,1)S(1)} collective-permute-done((bf16[64,2048]{1,0:T(8,128)(2,1)S(1)}, bf16[64,2048]{1,0:T(8,128)(2,1)S(1)}, u32[]{:S(2)}, u32[]{:S(2)}) %collective-permute-start.6) | collective-permute-done | bytes 262176 | tf_op jit(solution)/shard_map/ppermute | solution.py:58
  231.2 6.1 collective-permute-done.8
  261.0 8.6 copy.605
  271.9 6.2 fusion.470
  311.6 31.0 %collective-permute-done.14 = bf16[64,2048]{1,0:T(8,128)(2,1)S(1)} collective-permute-done((bf16[64,2048]{1,0:T(8,128)(2,1)}, bf16[64,2048]{1,0:T(8,128)(2,1)S(1)}, u32[]{:S(2)}, u32[]{:S(2)}) %collective-permute-start.14) | collective-permute-done | bytes 262176 | tf_op jit(solution)/shard_map/ppermute | solution.py:58
  342.6 6.2 collective-permute-done.16
  354.6 6.0 maximum_bitcast_fusion.1
  401.3 13.6 all_gather.63
  428.1 50.7 %collective-permute-done.36 = bf16[64,2048]{1,0:T(8,128)(2,1)S(1)} collective-permute-done((bf16[64,2048]{1,0:T(8,128)(2,1)S(1)}, bf16[64,2048]{1,0:T(8,128)(2,1)S(1)}, u32[]{:S(2)}, u32[]{:S(2)}) %collective-permute-start.36) | collective-permute-done | bytes 262176 | tf_op jit(solution)/shard_map/ppermute | solution.py:58
  489.2 6.1 collective-permute-done.25
  513.0 8.6 copy.618
  526.3 6.8 fusion.472
  579.0 6.7 collective-permute-done.44
  604.1 13.7 all_gather.64
  658.6 6.4 collective-permute-done.53
  686.2 6.3 fusion.468
  715.5 41.4 %collective-permute-done.77 = bf16[3,80,2048]{2,1,0:T(8,128)(2,1)} collective-permute-done((bf16[3,80,2048]{2,1,0:T(8,128)(2,1)}, bf16[3,80,2048]{2,1,0:T(8,128)(2,1)}, u32[]{:S(2)}, u32[]{:S(2)}) %collective-permute-start.77) | collective-permute-done | bytes 983072 | tf_op jit(solution)/shard_map/ppermute | solution.py:89
  768.0 28.6 %all_gather.65 = f32[4,2,8,2,320]{4,2,3,1,0:T(8,128)S(1)} all-gather(f32[1,2,8,2,320]{4,2,3,1,0:T(8,128)S(1)} %copy.625), channel_id=1, replica_groups=mesh['section'=4,'dp'=8] {'section'}, dimensions={0}, use_global_device_ids=true | all-gather | bytes 204800 | tf_op jit(solution)/shard_map/all_gather | solution.py:195
  855.4 38.6 %collective-permute-done.76 = bf16[80,2048]{1,0:T(8,128)(2,1)S(1)} collective-permute-done((bf16[80,2048]{1,0:T(8,128)(2,1)S(1)}, bf16[80,2048]{1,0:T(8,128)(2,1)S(1)}, u32[]{:S(2)}, u32[]{:S(2)}) %collective-permute-start.76) | collective-permute-done | bytes 327712 | tf_op jit(solution)/shard_map/ppermute | solution.py:98
  904.9 46.9 %collective-permute-start.92 = (bf16[3,192,2048]{2,1,0:T(8,128)(2,1)}, bf16[3,192,2048]{2,1,0:T(8,128)(2,1)S(1)}, u32[]{:S(2)}, u32[]{:S(2)}) collective-permute-start(bf16[3,192,2048]{2,1,0:T(8,128)(2,1)} %constant_dynamic-slice_fusion.19), channel_id=1, source_target_pairs={{0,8},{24,16},{1,9},{25,17},{2,10},{26,18},{3,11},{27,19},{4,12},{... | collective-permute-start | bytes 7077896 | tf_op jit(solution)/shard_map/ppermute | solution.py:89
  952.8 6.7 collective-permute-done.97
  968.2 6.1 copy.634
  985.3 53.2 %collective-permute-done.92 = bf16[3,192,2048]{2,1,0:T(8,128)(2,1)S(1)} collective-permute-done((bf16[3,192,2048]{2,1,0:T(8,128)(2,1)}, bf16[3,192,2048]{2,1,0:T(8,128)(2,1)S(1)}, u32[]{:S(2)}, u32[]{:S(2)}) %collective-permute-start.92) | collective-permute-done | bytes 2359328 | tf_op jit(solution)/shard_map/ppermute | solution.py:89
  1044.7 6.5 collective-permute-start.89
  1056.7 6.0 copy.629
  1070.7 44.5 %collective-permute-done.71 = bf16[3,8,64,832]{3,2,1,0:T(8,128)(2,1)} collective-permute-done((bf16[3,8,64,832]{3,2,1,0:T(8,128)(2,1)}, bf16[3,8,64,832]{3,2,1,0:T(8,128)(2,1)}, u32[]{:S(2)}, u32[]{:S(2)}) %collective-permute-start.71) | collective-permute-done | bytes 2555936 | tf_op jit(solution)/shard_map/ppermute | solution.py:89
  1126.6 195.8 %collective-permute-done.68 = bf16[3,8,64,832]{3,2,1,0:T(8,128)(2,1)} collective-permute-done((bf16[3,8,64,832]{3,2,1,0:T(8,128)(2,1)S(1)}, bf16[3,8,64,832]{3,2,1,0:T(8,128)(2,1)}, u32[]{:S(2)}, u32[]{:S(2)}) %collective-permute-start.68) | collective-permute-done | bytes 2555936 | tf_op jit(solution)/shard_map/ppermute | solution.py:89
  1343.1 7.1 convolution_convert_fusion.1
  1359.5 30.7 %collective-permute-done.70 = bf16[8,64,832]{2,1,0:T(8,128)(2,1)} collective-permute-done((bf16[8,64,832]{2,1,0:T(8,128)(2,1)}, bf16[8,64,832]{2,1,0:T(8,128)(2,1)}, u32[]{:S(2)}, u32[]{:S(2)}) %collective-permute-start.70) | collective-permute-done | bytes 852000 | tf_op jit(solution)/shard_map/ppermute | solution.py:98
  1425.4 144.6 %collective-permute-done.86 = bf16[3,8,64,1536]{3,2,1,0:T(8,128)(2,1)} collective-permute-done((bf16[3,8,64,1536]{3,2,1,0:T(8,128)(2,1)}, bf16[3,8,64,1536]{3,2,1,0:T(8,128)(2,1)}, u32[]{:S(2)}, u32[]{:S(2)}) %collective-permute-start.86) | collective-permute-done | bytes 4718624 | tf_op jit(solution)/shard_map/ppermute | solution.py:89
  1582.8 24.7 %all_to_all.120 = bf16[8,64,1536]{2,1,0:T(8,128)(2,1)S(1)} all-to-all(bf16[8,64,1536]{2,1,0:T(8,128)(2,1)S(1)} %fusion.6), channel_id=1, replica_groups=mesh['section'=4,'dp'=8] {'dp'}, dimensions={0} | all-to-all | bytes 3145728 | tf_op jit(solution)/shard_map/all_to_all | solution.py:82
  1613.1 145.3 %collective-permute-done.88 = bf16[8,64,1536]{2,1,0:T(8,128)(2,1)S(1)} collective-permute-done((bf16[8,64,1536]{2,1,0:T(8,128)(2,1)S(1)}, bf16[8,64,1536]{2,1,0:T(8,128)(2,1)S(1)}, u32[]{:S(2)}, u32[]{:S(2)}) %collective-permute-start.88) | collective-permute-done | bytes 1572896 | tf_op jit(solution)/shard_map/ppermute | solution.py:98
  1774.3 13.4 all-to-all-done.14
  1812.3 7.8 collective-permute-done.80
  1822.0 11.3 collective-permute-done.83
  1837.9 16.9 collective-permute-done.82
  1859.7 9.2 collective-permute-done.85
  1875.2 20.1 all_gather.72
  1895.4 17.1 all_gather.73
  1929.3 7.6 all-to-all-done.9
  1943.6 8.4 maximum_convert_fusion.2
  1960.9 8.8 maximum_convert_fusion
  1969.7 49.9 %all-gather.31.cloned.1.call-done = bf16[256,6144]{1,0:T(8,128)(2,1)} async-done(((bf16[64,6144]{1,0:T(8,128)(2,1)}), bf16[256,6144]{1,0:T(8,128)(2,1)}) %all-gather.31.cloned.1.call-update) | async-done | bytes 3145744 | tf_op jit(solution)/shard_map/all_gather | solution.py:532
  2019.6 8.4 maximum_convert_fusion.1
  (1360 shorter events, 741.6 us)
Async XLA Ops:
  9.9 54.9 %all-to-all-start = ((bf16[2,128,512]{2,0,1:T(2,128)(2,1)}), bf16[2,128,512]{2,0,1:T(2,128)(2,1)}, u32[]{:S(2)}, u32[]{:S(2)}) async-start(bf16[2,128,512]{2,0,1:T(2,128)(2,1)} %copy.587), calls=%async_computation | async-start | bytes 524288 | tf_op jit(solution)/shard_map/all_to_all | solution.py:605
  82.2 67.1 %all-to-all-start.1 = ((bf16[8,256,832]{1,2,0:T(8,128)(2,1)}), bf16[8,256,832]{1,2,0:T(8,128)(2,1)S(1)}, u32[]{:S(2)}, u32[]{:S(2)}) async-start(bf16[8,256,832]{1,2,0:T(8,128)(2,1)} %fusion.240), calls=%async_computation.1 | async-start | bytes 6815744 | tf_op jit(solution)/shard_map/all_to_all | solution.py:82
  90.9 42.4 %collective-permute-start.2 = (bf16[64,2048]{1,0:T(8,128)(2,1)}, bf16[64,2048]{1,0:T(8,128)(2,1)}, u32[]{:S(2)}, u32[]{:S(2)}) collective-permute-start(bf16[64,2048]{1,0:T(8,128)(2,1)} %get-tuple-element.110), channel_id=1, source_target_pairs={{0,6},{1,7},{2,4},{3,5},{4,2},{5,3},{6,0},{7,1},{8,14},{9,15},{10,... | collective-permute-start | bytes 786440 | tf_op jit(solution)/shard_map/ppermute | solution.py:58
  93.8 43.7 %collective-permute-start.1 = (bf16[64,2048]{1,0:T(8,128)(2,1)}, bf16[64,2048]{1,0:T(8,128)(2,1)}, u32[]{:S(2)}, u32[]{:S(2)}) collective-permute-start(bf16[64,2048]{1,0:T(8,128)(2,1)} %get-tuple-element.110), channel_id=1, source_target_pairs={{0,4},{1,5},{2,6},{3,7},{4,0},{5,1},{6,2},{7,3},{8,12},{9,13},{10,... | collective-permute-start | bytes 786440 | tf_op jit(solution)/shard_map/ppermute | solution.py:58
  94.4 43.2 %collective-permute-start = (bf16[64,2048]{1,0:T(8,128)(2,1)}, bf16[64,2048]{1,0:T(8,128)(2,1)}, u32[]{:S(2)}, u32[]{:S(2)}) collective-permute-start(bf16[64,2048]{1,0:T(8,128)(2,1)} %get-tuple-element.110), channel_id=1, source_target_pairs={{0,2},{1,3},{2,0},{3,1},{4,6},{5,7},{6,4},{7,5},{8,10},{9,11},{10,... | collective-permute-start | bytes 786440 | tf_op jit(solution)/shard_map/ppermute | solution.py:58
  149.2 107.4 %all-to-all-start.3 = ((bf16[8,256,1536]{1,2,0:T(8,128)(2,1)}), bf16[8,256,1536]{1,2,0:T(8,128)(2,1)}, u32[]{:S(2)}, u32[]{:S(2)}) async-start(bf16[8,256,1536]{1,2,0:T(8,128)(2,1)} %maximum_bitcast_fusion), calls=%async_computation.3 | async-start | bytes 12582912 | tf_op jit(solution)/shard_map/all_to_all | solution.py:82
  198.4 38.9 %collective-permute-start.8 = (bf16[64,2048]{1,0:T(8,128)(2,1)S(1)}, bf16[64,2048]{1,0:T(8,128)(2,1)S(1)}, u32[]{:S(2)}, u32[]{:S(2)}) collective-permute-start(bf16[64,2048]{1,0:T(8,128)(2,1)S(1)} %get-tuple-element.234), channel_id=1, source_target_pairs={{0,6},{1,7},{2,4},{3,5},{4,2},{5,3},{6,0},{7,1},{8,14},{9,15},{10,... | collective-permute-start | bytes 786440 | tf_op jit(solution)/shard_map/ppermute | solution.py:58
  292.3 77.9 %all-to-all-start.4 = ((bf16[8,256,832]{1,2,0:T(8,128)(2,1)}), bf16[8,256,832]{1,2,0:T(8,128)(2,1)}, u32[]{:S(2)}, u32[]{:S(2)}) async-start(bf16[8,256,832]{1,2,0:T(8,128)(2,1)} %fusion.248), calls=%async_computation.4 | async-start | bytes 6815744 | tf_op jit(solution)/shard_map/all_to_all | solution.py:82
  298.8 43.8 %collective-permute-start.14 = (bf16[64,2048]{1,0:T(8,128)(2,1)}, bf16[64,2048]{1,0:T(8,128)(2,1)S(1)}, u32[]{:S(2)}, u32[]{:S(2)}) collective-permute-start(bf16[64,2048]{1,0:T(8,128)(2,1)} %get-tuple-element.230), channel_id=1, source_target_pairs={{0,2},{1,3},{2,0},{3,1},{4,6},{5,7},{6,4},{7,5},{8,10},{9,11},{10,... | collective-permute-start | bytes 786440 | tf_op jit(solution)/shard_map/ppermute | solution.py:58
  300.7 48.1 %collective-permute-start.16 = (bf16[64,2048]{1,0:T(8,128)(2,1)}, bf16[64,2048]{1,0:T(8,128)(2,1)}, u32[]{:S(2)}, u32[]{:S(2)}) collective-permute-start(bf16[64,2048]{1,0:T(8,128)(2,1)} %get-tuple-element.231), channel_id=1, source_target_pairs={{0,6},{1,7},{2,4},{3,5},{4,2},{5,3},{6,0},{7,1},{8,14},{9,15},{10,... | collective-permute-start | bytes 786440 | tf_op jit(solution)/shard_map/ppermute | solution.py:58
  302.2 46.6 %collective-permute-start.15 = (bf16[64,2048]{1,0:T(8,128)(2,1)}, bf16[64,2048]{1,0:T(8,128)(2,1)}, u32[]{:S(2)}, u32[]{:S(2)}) collective-permute-start(bf16[64,2048]{1,0:T(8,128)(2,1)} %get-tuple-element.232), channel_id=1, source_target_pairs={{0,4},{1,5},{2,6},{3,7},{4,0},{5,1},{6,2},{7,3},{8,12},{9,13},{10,... | collective-permute-start | bytes 786440 | tf_op jit(solution)/shard_map/ppermute | solution.py:58
  396.4 116.7 %all-to-all-start.6 = ((bf16[8,256,1536]{1,2,0:T(8,128)(2,1)}), bf16[8,256,1536]{1,2,0:T(8,128)(2,1)}, u32[]{:S(2)}, u32[]{:S(2)}) async-start(bf16[8,256,1536]{1,2,0:T(8,128)(2,1)} %maximum_bitcast_fusion.1), calls=%async_computation.6 | async-start | bytes 12582912 | tf_op jit(solution)/shard_map/all_to_all | solution.py:82
  401.2 1520.2 %all-reduce.41.cloned.1.call-start = ((), (), s32[]{:S(2)}) async-start(), calls=%async_computation.28 | async-start | bytes 393216 | tf_op jit(solution)/shard_map/psum | solution.py:597
  420.4 58.5 %collective-permute-start.36 = (bf16[64,2048]{1,0:T(8,128)(2,1)S(1)}, bf16[64,2048]{1,0:T(8,128)(2,1)S(1)}, u32[]{:S(2)}, u32[]{:S(2)}) collective-permute-start(bf16[64,2048]{1,0:T(8,128)(2,1)S(1)} %bitcast.1113), channel_id=1, source_target_pairs={{0,6},{1,7},{2,4},{3,5},{4,2},{5,3},{6,0},{7,1},{8,14},{9,15},{10,... | collective-permute-start | bytes 786440 | tf_op jit(solution)/shard_map/ppermute | solution.py:58
  423.2 60.3 %collective-permute-start.35 = (bf16[64,2048]{1,0:T(8,128)(2,1)S(1)}, bf16[64,2048]{1,0:T(8,128)(2,1)S(1)}, u32[]{:S(2)}, u32[]{:S(2)}) collective-permute-start(bf16[64,2048]{1,0:T(8,128)(2,1)S(1)} %bitcast.1114), channel_id=1, source_target_pairs={{0,4},{1,5},{2,6},{3,7},{4,0},{5,1},{6,2},{7,3},{8,12},{9,13},{10,... | collective-permute-start | bytes 786440 | tf_op jit(solution)/shard_map/ppermute | solution.py:58
  423.8 59.8 %collective-permute-start.34 = (bf16[64,2048]{1,0:T(8,128)(2,1)S(1)}, bf16[64,2048]{1,0:T(8,128)(2,1)S(1)}, u32[]{:S(2)}, u32[]{:S(2)}) collective-permute-start(bf16[64,2048]{1,0:T(8,128)(2,1)S(1)} %bitcast.1115), channel_id=1, source_target_pairs={{0,2},{1,3},{2,0},{3,1},{4,6},{5,7},{6,4},{7,5},{8,10},{9,11},{10,... | collective-permute-start | bytes 786440 | tf_op jit(solution)/shard_map/ppermute | solution.py:58
  424.7 64.4 %collective-permute-start.23 = (bf16[64,2048]{1,0:T(8,128)(2,1)S(1)}, bf16[64,2048]{1,0:T(8,128)(2,1)S(1)}, u32[]{:S(2)}, u32[]{:S(2)}) collective-permute-start(bf16[64,2048]{1,0:T(8,128)(2,1)S(1)} %get-tuple-element.227), channel_id=1, source_target_pairs={{0,2},{1,3},{2,0},{3,1},{4,6},{5,7},{6,4},{7,5},{8,10},{9,11},{10,... | collective-permute-start | bytes 786440 | tf_op jit(solution)/shard_map/ppermute | solution.py:58
  426.6 68.6 %collective-permute-start.25 = (bf16[64,2048]{1,0:T(8,128)(2,1)S(1)}, bf16[64,2048]{1,0:T(8,128)(2,1)S(1)}, u32[]{:S(2)}, u32[]{:S(2)}) collective-permute-start(bf16[64,2048]{1,0:T(8,128)(2,1)S(1)} %get-tuple-element.228), channel_id=1, source_target_pairs={{0,6},{1,7},{2,4},{3,5},{4,2},{5,3},{6,0},{7,1},{8,14},{9,15},{10,... | collective-permute-start | bytes 786440 | tf_op jit(solution)/shard_map/ppermute | solution.py:58
  682.6 165.7 %collective-permute-start.95 = (bf16[3,192,2048]{2,1,0:T(8,128)(2,1)}, bf16[3,192,2048]{2,1,0:T(8,128)(2,1)}, u32[]{:S(2)}, u32[]{:S(2)}) collective-permute-start(bf16[3,192,2048]{2,1,0:T(8,128)(2,1)} %constant_dynamic-slice_fusion.4), channel_id=1, source_target_pairs={{0,8},{24,16},{1,9},{25,17},{2,10},{26,18},{3,11},{27,19},{4,12},{... | collective-permute-start | bytes 7077896 | tf_op jit(solution)/shard_map/ppermute | solution.py:89
  699.0 57.9 %collective-permute-start.77 = (bf16[3,80,2048]{2,1,0:T(8,128)(2,1)}, bf16[3,80,2048]{2,1,0:T(8,128)(2,1)}, u32[]{:S(2)}, u32[]{:S(2)}) collective-permute-start(bf16[3,80,2048]{2,1,0:T(8,128)(2,1)} %constant_dynamic-slice_fusion.18), channel_id=1, source_target_pairs={{0,8},{24,16},{1,9},{25,17},{2,10},{26,18},{3,11},{27,19},{4,12},{... | collective-permute-start | bytes 2949128 | tf_op jit(solution)/shard_map/ppermute | solution.py:89
  711.9 47.6 %collective-permute-start.61 = (bf16[64,2048]{1,0:T(8,128)(2,1)S(1)}, bf16[64,2048]{1,0:T(8,128)(2,1)S(1)}, u32[]{:S(2)}, u32[]{:S(2)}) collective-permute-start(bf16[64,2048]{1,0:T(8,128)(2,1)S(1)} %get-tuple-element.79), channel_id=1, source_target_pairs={{0,6},{1,7},{2,4},{3,5},{4,2},{5,3},{6,0},{7,1},{8,14},{9,15},{10,... | collective-permute-start | bytes 786440 | tf_op jit(solution)/shard_map/ppermute | solution.py:58
  713.5 46.1 %collective-permute-start.60 = (bf16[64,2048]{1,0:T(8,128)(2,1)S(1)}, bf16[64,2048]{1,0:T(8,128)(2,1)S(1)}, u32[]{:S(2)}, u32[]{:S(2)}) collective-permute-start(bf16[64,2048]{1,0:T(8,128)(2,1)S(1)} %get-tuple-element.79), channel_id=1, source_target_pairs={{0,4},{1,5},{2,6},{3,7},{4,0},{5,1},{6,2},{7,3},{8,12},{9,13},{10,... | collective-permute-start | bytes 786440 | tf_op jit(solution)/shard_map/ppermute | solution.py:58
  714.0 45.5 %collective-permute-start.59 = (bf16[64,2048]{1,0:T(8,128)(2,1)S(1)}, bf16[64,2048]{1,0:T(8,128)(2,1)S(1)}, u32[]{:S(2)}, u32[]{:S(2)}) collective-permute-start(bf16[64,2048]{1,0:T(8,128)(2,1)S(1)} %get-tuple-element.79), channel_id=1, source_target_pairs={{0,2},{1,3},{2,0},{3,1},{4,6},{5,7},{6,4},{7,5},{8,10},{9,11},{10,... | collective-permute-start | bytes 786440 | tf_op jit(solution)/shard_map/ppermute | solution.py:58
  844.2 1095.0 %all-gather.25.cloned.1.call-start = ((), (), s32[]{:S(2)}) async-start(), calls=%async_computation.21 | async-start | bytes 1638400 | tf_op jit(solution)/shard_map/all_gather | solution.py:532
  846.3 1093.0 %all-gather.23.cloned.1.call-start = ((), (), s32[]{:S(2)}) async-start(), calls=%async_computation.20 | async-start | bytes 1638400 | tf_op jit(solution)/shard_map/all_gather | solution.py:532
  852.1 43.9 %collective-permute-start.96 = (bf16[2,192,2048]{2,1,0:T(8,128)(2,1)}, bf16[2,192,2048]{2,1,0:T(8,128)(2,1)}, u32[]{:S(2)}, u32[]{:S(2)}) collective-permute-start(bf16[2,192,2048]{2,1,0:T(8,128)(2,1)} %add_convert_fusion), channel_id=1, source_target_pairs={{8,16},{16,8},{9,17},{17,9},{10,18},{18,10},{11,19},{19,11},{12,20... | collective-permute-start | bytes 4718600 | tf_op jit(solution)/shard_map/ppermute | solution.py:94
  854.0 40.0 %collective-permute-start.76 = (bf16[80,2048]{1,0:T(8,128)(2,1)S(1)}, bf16[80,2048]{1,0:T(8,128)(2,1)S(1)}, u32[]{:S(2)}, u32[]{:S(2)}) collective-permute-start(bf16[80,2048]{1,0:T(8,128)(2,1)S(1)} %fusion.269), channel_id=1, source_target_pairs={{8,0},{16,24},{9,1},{17,25},{10,2},{18,26},{11,3},{19,27},{12,4},{... | collective-permute-start | bytes 983048 | tf_op jit(solution)/shard_map/ppermute | solution.py:98
  895.9 1047.7 %all-gather.37.cloned.1.call-start = ((), (), s32[]{:S(2)}) async-start(), calls=%async_computation.27 | async-start | bytes 3932160 | tf_op jit(solution)/shard_map/all_gather | solution.py:532
  897.6 61.8 %collective-permute-start.97 = (bf16[192,2048]{1,0:T(8,128)(2,1)S(1)}, bf16[192,2048]{1,0:T(8,128)(2,1)S(1)}, u32[]{:S(2)}, u32[]{:S(2)}) collective-permute-start(bf16[192,2048]{1,0:T(8,128)(2,1)S(1)} %fusion.125), channel_id=1, source_target_pairs={{8,0},{16,24},{9,1},{17,25},{10,2},{18,26},{11,3},{19,27},{12,4},{... | collective-permute-start | bytes 2359304 | tf_op jit(solution)/shard_map/ppermute | solution.py:98
  904.9 133.6 %collective-permute-start.92 = (bf16[3,192,2048]{2,1,0:T(8,128)(2,1)}, bf16[3,192,2048]{2,1,0:T(8,128)(2,1)S(1)}, u32[]{:S(2)}, u32[]{:S(2)}) collective-permute-start(bf16[3,192,2048]{2,1,0:T(8,128)(2,1)} %constant_dynamic-slice_fusion.19), channel_id=1, source_target_pairs={{0,8},{24,16},{1,9},{25,17},{2,10},{26,18},{3,11},{27,19},{4,12},{... | collective-permute-start | bytes 7077896 | tf_op jit(solution)/shard_map/ppermute | solution.py:89
  962.6 981.1 %all-gather.35.cloned.1.call-start = ((), (), s32[]{:S(2)}) async-start(), calls=%async_computation.26 | async-start | bytes 3932160 | tf_op jit(solution)/shard_map/all_gather | solution.py:532
  978.0 137.3 %collective-permute-start.71 = (bf16[3,8,64,832]{3,2,1,0:T(8,128)(2,1)}, bf16[3,8,64,832]{3,2,1,0:T(8,128)(2,1)}, u32[]{:S(2)}, u32[]{:S(2)}) collective-permute-start(bf16[3,8,64,832]{3,2,1,0:T(8,128)(2,1)} %copy_bitcast_fusion.2), channel_id=1, source_target_pairs={{0,8},{24,16},{1,9},{25,17},{2,10},{26,18},{3,11},{27,19},{4,12},{... | collective-permute-start | bytes 7667720 | tf_op jit(solution)/shard_map/ppermute | solution.py:89
  1044.7 290.2 %collective-permute-start.89 = (bf16[3,8,64,1536]{3,2,1,0:T(8,128)(2,1)}, bf16[3,8,64,1536]{3,2,1,0:T(8,128)(2,1)}, u32[]{:S(2)}, u32[]{:S(2)}) collective-permute-start(bf16[3,8,64,1536]{3,2,1,0:T(8,128)(2,1)} %copy_bitcast_fusion), channel_id=1, source_target_pairs={{0,8},{24,16},{1,9},{25,17},{2,10},{26,18},{3,11},{27,19},{4,12},{... | collective-permute-start | bytes 14155784 | tf_op jit(solution)/shard_map/ppermute | solution.py:89
  1064.9 257.5 %collective-permute-start.68 = (bf16[3,8,64,832]{3,2,1,0:T(8,128)(2,1)S(1)}, bf16[3,8,64,832]{3,2,1,0:T(8,128)(2,1)}, u32[]{:S(2)}, u32[]{:S(2)}) collective-permute-start(bf16[3,8,64,832]{3,2,1,0:T(8,128)(2,1)S(1)} %copy_bitcast_fusion.3), channel_id=1, source_target_pairs={{0,8},{24,16},{1,9},{25,17},{2,10},{26,18},{3,11},{27,19},{4,12},{... | collective-permute-start | bytes 7667720 | tf_op jit(solution)/shard_map/ppermute | solution.py:89
  1069.4 51.1 %collective-permute-start.94 = (bf16[192,2048]{1,0:T(8,128)(2,1)S(1)}, bf16[192,2048]{1,0:T(8,128)(2,1)S(1)}, u32[]{:S(2)}, u32[]{:S(2)}) collective-permute-start(bf16[192,2048]{1,0:T(8,128)(2,1)S(1)} %fusion.124), channel_id=1, source_target_pairs={{8,0},{16,24},{9,1},{17,25},{10,2},{18,26},{11,3},{19,27},{12,4},{... | collective-permute-start | bytes 2359304 | tf_op jit(solution)/shard_map/ppermute | solution.py:98
  1125.3 202.9 %collective-permute-start.73 = (bf16[8,64,832]{2,1,0:T(8,128)(2,1)S(1)}, bf16[8,64,832]{2,1,0:T(8,128)(2,1)S(1)}, u32[]{:S(2)}, u32[]{:S(2)}) collective-permute-start(bf16[8,64,832]{2,1,0:T(8,128)(2,1)S(1)} %fusion.34), channel_id=1, source_target_pairs={{8,0},{16,24},{9,1},{17,25},{10,2},{18,26},{11,3},{19,27},{12,4},{... | collective-permute-start | bytes 2555912 | tf_op jit(solution)/shard_map/ppermute | solution.py:98
  1340.5 80.1 %collective-permute-start.90 = (bf16[2,8,64,1536]{3,2,1,0:T(8,128)(2,1)}, bf16[2,8,64,1536]{3,2,1,0:T(8,128)(2,1)}, u32[]{:S(2)}, u32[]{:S(2)}) collective-permute-start(bf16[2,8,64,1536]{3,2,1,0:T(8,128)(2,1)} %fusion), channel_id=1, source_target_pairs={{8,16},{16,8},{9,17},{17,9},{10,18},{18,10},{11,19},{19,11},{12,20... | collective-permute-start | bytes 9437192 | tf_op jit(solution)/shard_map/ppermute | solution.py:94
  1397.2 554.9 %all-gather.17.cloned.1.call-start = ((), (), s32[]{:S(2)}) async-start(), calls=%async_computation.17 | async-start | bytes 1638400 | tf_op jit(solution)/shard_map/all_gather | solution.py:532
  1398.2 553.8 %all-gather.15.cloned.1.call-start = ((), (), s32[]{:S(2)}) async-start(), calls=%async_computation.16 | async-start | bytes 1638400 | tf_op jit(solution)/shard_map/all_gather | solution.py:532
  1403.3 166.6 %collective-permute-start.86 = (bf16[3,8,64,1536]{3,2,1,0:T(8,128)(2,1)}, bf16[3,8,64,1536]{3,2,1,0:T(8,128)(2,1)}, u32[]{:S(2)}, u32[]{:S(2)}) collective-permute-start(bf16[3,8,64,1536]{3,2,1,0:T(8,128)(2,1)} %copy_bitcast_fusion.1), channel_id=1, source_target_pairs={{0,8},{24,16},{1,9},{25,17},{2,10},{26,18},{3,11},{27,19},{4,12},{... | collective-permute-start | bytes 14155784 | tf_op jit(solution)/shard_map/ppermute | solution.py:89
  1419.1 537.4 %all-gather.21.cloned.1.call-start = ((), (), s32[]{:S(2)}) async-start(), calls=%async_computation.19 | async-start | bytes 1638400 | tf_op jit(solution)/shard_map/all_gather | solution.py:532
  1420.5 536.0 %all-gather.19.cloned.1.call-start = ((), (), s32[]{:S(2)}) async-start(), calls=%async_computation.18 | async-start | bytes 1638400 | tf_op jit(solution)/shard_map/all_gather | solution.py:532
  1424.1 155.1 %collective-permute-start.91 = (bf16[8,64,1536]{2,1,0:T(8,128)(2,1)}, bf16[8,64,1536]{2,1,0:T(8,128)(2,1)}, u32[]{:S(2)}, u32[]{:S(2)}) collective-permute-start(bf16[8,64,1536]{2,1,0:T(8,128)(2,1)} %fusion.4), channel_id=1, source_target_pairs={{8,0},{16,24},{9,1},{17,25},{10,2},{18,26},{11,3},{19,27},{12,4},{... | collective-permute-start | bytes 4718600 | tf_op jit(solution)/shard_map/ppermute | solution.py:98
  1579.1 381.8 %all-gather.29.cloned.1.call-start = ((), (), s32[]{:S(2)}) async-start(), calls=%async_computation.23 | async-start | bytes 3932160 | tf_op jit(solution)/shard_map/all_gather | solution.py:532
  1611.8 146.6 %collective-permute-start.88 = (bf16[8,64,1536]{2,1,0:T(8,128)(2,1)S(1)}, bf16[8,64,1536]{2,1,0:T(8,128)(2,1)S(1)}, u32[]{:S(2)}, u32[]{:S(2)}) collective-permute-start(bf16[8,64,1536]{2,1,0:T(8,128)(2,1)S(1)} %fusion.7), channel_id=1, source_target_pairs={{8,0},{16,24},{9,1},{17,25},{10,2},{18,26},{11,3},{19,27},{12,4},{... | collective-permute-start | bytes 4718600 | tf_op jit(solution)/shard_map/ppermute | solution.py:98
  1791.8 169.1 %all-gather.27.cloned.1.call-start = ((), (), s32[]{:S(2)}) async-start(), calls=%async_computation.22 | async-start | bytes 3932160 | tf_op jit(solution)/shard_map/all_gather | solution.py:532
  1874.0 95.7 %all-gather.33.cloned.1.call-start = ((), (), s32[]{:S(2)}) async-start(), calls=%async_computation.25 | async-start | bytes 3932160 | tf_op jit(solution)/shard_map/all_gather | solution.py:532
  1875.1 144.5 %all-gather.31.cloned.1.call-start = ((), (), s32[]{:S(2)}) async-start(), calls=%async_computation.24 | async-start | bytes 3932160 | tf_op jit(solution)/shard_map/all_gather | solution.py:532
  (381 other events, 4220.6 us)
Sparse Core Ops, SparseCore 0:
  844.3 258.3 all-reduce.40
Sparse Core Ops, SparseCore 1:
  846.3 41.2 all-gather.24
  896.0 40.5 all-gather.22
  962.7 108.6 all-gather.36
  1123.7 110.2 all-gather.34
  1399.5 50.1 all-gather.16
  1451.9 52.7 all-gather.14
  1506.1 52.7 all-gather.20
  1579.2 44.5 all-gather.18
  1625.8 87.2 all-gather.28
  1794.7 74.3 all-gather.26
  1876.0 79.5 all-gather.32
  1957.2 62.3 all-gather.30

commit v2 on v1

--- a/solution.py
+++ b/solution.py
@@ -83,32 +83,146 @@
 
 
 def section_sum(chunks):
-    rank = lax.axis_index("section")
-    pick = lambda value, at: lax.dynamic_index_in_dim(value, at, 0, keepdims=False)
-    part = lambda value, at, size: lax.dynamic_slice_in_dim(value, at, size, 0)
-    first = lax.ppermute(
-        part(chunks, jnp.where(rank == 0, 1, 0), 3), "section", [(0, 1), (3, 2)]
-    )
-    second_own = part(chunks, jnp.where(rank == 1, 2, 0), 2)
-    second_came = part(first, jnp.where(rank == 1, 1, 0), 2)
-    second = lax.ppermute(
-        low(high(second_own) + high(second_came)), "section", [(1, 2), (2, 1)]
-    )
-    lower_half = rank == 1
-    third = lax.ppermute(
-        low(
-            high(pick(chunks, jnp.where(lower_half, 0, 3)))
-            + high(pick(second, jnp.where(lower_half, 0, 1)))
+    return lax.psum_scatter(chunks, "section", scatter_dimension=0, tiled=False)
+
+
+def all_rows(block):
+    return lax.all_gather(block, ("dp", "section"), axis=0, tiled=True)
+
+
+def other_planes(value):
+    count = lax.axis_size("section")
+    return [
+        lax.ppermute(value, "section", [(at, at ^ k) for at in range(count)])
+        for k in range(1, count)
+    ]
+
+
+def columns_apart(first, second, layer, count):
+    rows, columns = first.shape[1], first.shape[2] // count
+    if columns % 128:
+        parts = [
+            part[layer].reshape(rows, count, columns).transpose(1, 0, 2)
+            for part in (first, second)
+        ]
+        return jnp.concatenate(parts, axis=2)
+
+    def kernel(first_ref, second_ref, out_ref):
+        out_ref[0, :, :columns] = first_ref[0]
+        out_ref[0, :, columns:] = second_ref[0]
+
+    return pl.pallas_call(
+        kernel,
+        out_shape=jax.ShapeDtypeStruct((count, rows, 2 * columns), first.dtype),
+        grid=(count,),
+        in_specs=[pl.BlockSpec((1, rows, columns), lambda at: (layer, 0, at))] * 2,
+        out_specs=pl.BlockSpec((1, rows, 2 * columns), lambda at: (at, 0, 0)),
+        cost_estimate=pl.CostEstimate(
+            flops=0, transcendentals=0, bytes_accessed=8 * count * rows * columns
         ),
-        "section",
-        [(1, 0), (2, 3)],
-    )
-    return (
-        high(pick(chunks, rank))
-        + high(pick(first, jnp.where(lower_half, 0, 2)))
-        + high(pick(second, jnp.where(lower_half, 1, 0)))
-        + high(third)
-    )
+        compiler_params=pltpu.CompilerParams(vmem_limit_bytes=16 * 1024 * 1024),
+    )(first, second)
+
+
+def packed_columns(branch, gate, blocks, layer, filler):
+    count, rows, extra = blocks.shape
+    own = R // count
+    width = WIN + own + filler + extra
+    if own % 64:
+        packs = []
+        for device in range(count):
+            begin, end, left, right = window_of(device, count)
+            packs.append(
+                jnp.concatenate(
+                    own_first(branch[layer], device, count)
+                    + [gate[layer][:, begin:end]]
+                    + [jnp.zeros((rows, filler), branch.dtype), blocks[device]],
+                    axis=1,
+                )
+            )
+        return jnp.stack(packs)
+
+    def kernel(branch_ref, gate_ref, blocks_ref, out_ref):
+        for device in range(count):
+            begin, end, left, right = window_of(device, count)
+            at = 0
+            for ref, start, stop in (
+                (branch_ref, begin, end),
+                (branch_ref, end, right),
+                (branch_ref, left, begin),
+                (gate_ref, begin, end),
+            ):
+                if stop > start:
+                    out_ref[device, :, at : at + stop - start] = ref[0, :, start:stop]
+                    at += stop - start
+            if filler:
+                out_ref[device, :, at : at + filler] = jnp.zeros((rows, filler), out_ref.dtype)
+            out_ref[device, :, at + filler :] = blocks_ref[device]
+
+    whole = pl.BlockSpec((1, rows, R), lambda at: (layer, 0, 0))
+    return pl.pallas_call(
+        kernel,
+        out_shape=jax.ShapeDtypeStruct((count, rows, width), branch.dtype),
+        grid=(1,),
+        in_specs=[whole, whole, pl.BlockSpec((count, rows, extra), lambda at: (0, 0, 0))],
+        out_specs=pl.BlockSpec((count, rows, width), lambda at: (0, 0, 0)),
+        cost_estimate=pl.CostEstimate(
+            flops=0, transcendentals=0, bytes_accessed=4 * count * rows * width
+        ),
+        compiler_params=pltpu.CompilerParams(vmem_limit_bytes=40 * 1024 * 1024),
+    )(branch, gate, blocks)
+
+
+def rows_kernel(part_ref, kept_ref, out_ref):
+    del kept_ref
+    out_ref[0] = part_ref[0].astype(jnp.float32)
+
+
+def first_rows_kernel(part_ref, out_ref):
+    out_ref[0] = part_ref[0].astype(jnp.float32)
+
+
+def joined_rows(part, which, layer, layers, out):
+    count, rows, columns = part.shape[0], part.shape[1], part.shape[2] // 2
+    if columns % 128:
+        part = part[:, :, which * columns : (which + 1) * columns]
+        whole = jnp.zeros((layers, rows, count * columns), jnp.float32) if out is None else out
+        piece = high(part.transpose(1, 0, 2).reshape(1, rows, -1))
+        return lax.dynamic_update_slice_in_dim(whole, piece, layer, 0)
+    operands = [part] + ([] if out is None else [out])
+    return pl.pallas_call(
+        first_rows_kernel if out is None else rows_kernel,
+        out_shape=jax.ShapeDtypeStruct((layers, rows, count * columns), jnp.float32),
+        grid=(count,),
+        in_specs=[pl.BlockSpec((1, rows, columns), lambda at: (at, 0, which))]
+        + [pl.BlockSpec(memory_space=pl.ANY)] * (len(operands) - 1),
+        out_specs=pl.BlockSpec((1, rows, columns), lambda at: (layer, 0, at)),
+        input_output_aliases={1: 0} if len(operands) > 1 else {},
+        cost_estimate=pl.CostEstimate(
+            flops=0, transcendentals=0, bytes_accessed=6 * count * rows * columns
+        ),
+        compiler_params=pltpu.CompilerParams(vmem_limit_bytes=16 * 1024 * 1024),
+    )(*operands)
+
+
+def after(value, *others):
+    return lax.optimization_barrier((value,) + others)
+
+
+def after_all(values, *others):
+    return lax.optimization_barrier(tuple(values) + others)[: len(values)]
+
+
+def lane_blocks(value, width):
+    rows, columns = value.shape[-2:]
+    split = value.reshape(value.shape[:-1] + (columns // width, width))
+    return jnp.swapaxes(split, -3, -2).reshape(value.shape[:-2] + (-1, width))
+
+
+def whole_rows(value, rows):
+    blocks = value.shape[-2] // rows
+    split = value.reshape(value.shape[:-2] + (blocks, rows, value.shape[-1]))
+    return jnp.swapaxes(split, -3, -2).reshape(value.shape[:-2] + (rows, -1))
 
 
 def window_of(device, count):
@@ -172,7 +286,8 @@
             def _(state=state, at=at):
                 carry_ref[at] = state
 
-            state = totals_ref[plane, 0, at] * state + totals_ref[plane, 1, at]
+            met = jnp.bitwise_xor(rank, plane)
+            state = totals_ref[met, 0, at] * state + totals_ref[met, 1, at]
 
 
 VMEM_SPEC = pl.BlockSpec(memory_space=pltpu.VMEM)
@@ -192,9 +307,8 @@
 def carried(totals, reverse):
     count = lax.axis_size("dp")
     channels = totals.shape[-1]
-    everything = lax.all_gather(
-        totals.reshape(2, count, MICRO, channels), "section", axis=0, tiled=False
-    )
+    totals = totals.reshape(2, count, MICRO, channels)
+    everything = jnp.stack([totals] + other_planes(totals))
     where = jnp.stack([lax.axis_index("dp"), lax.axis_index("section")]).astype(jnp.int32)
 
     def kernel(where_ref, totals_ref, carry_ref):
@@ -246,6 +360,7 @@
     wide = F // count
     strip = D // count
     thin = strip // planes
+    filler = D // 2 - BW // 2 - WIN - own
     order = jnp.array(meeting_order(count), jnp.int32)
     devices = jnp.bitwise_xor(me, order)
 
@@ -266,35 +381,48 @@
     def small_whole(layer, begin, each):
         return small_all[:, layer, begin : begin + each].reshape(count * each)
 
-    weights = []
-    for layer in range(LAYERS):
-        in_pack = jnp.stack(
-            [
-                jnp.concatenate(
-                    own_first(branch_in[layer], device, count)
-                    + [gate_in[layer][:, own * device : own * (device + 1)]],
-                    axis=1,
-                )
-                for device in range(count)
-            ]
-        )
-        gates = jnp.stack([rate_gate[layer], input_gate[layer]])
-        gate_pack = jnp.stack(
-            [
-                gates[:, window_of(device, count)[2] // BW : window_of(device, count)[3] // BW]
-                for device in range(count)
-            ]
-        )
-        mlp_pack = jnp.concatenate(
-            [
-                mlp_gate[layer].reshape(strip, count, wide),
-                mlp_up[layer].reshape(strip, count, wide),
-            ],
-            axis=2,
-        ).transpose(1, 0, 2)
-        in_weight = spread(in_pack).reshape(D, WIN + own)
-        gate_rows = spread(gate_pack)
-        blocks = gate_rows.transpose(1, 2, 0, 3, 4).reshape(2, 2, BW, BW)
+    def packed_in(layer, shared):
+        def cut(value, axis):
+            if not shared:
+                return value
+            size = value.shape[axis] // planes
+            return lax.dynamic_slice_in_dim(value, size * rank, size, axis)
+
+        gates = cut(jnp.stack([rate_gate[layer], input_gate[layer]]), 2)
+        blocks = []
+        for device in range(count):
+            begin, end, left, right = window_of(device, count)
+            height = thin if shared else strip
+            blocks.append(gates[:, left // BW : right // BW].reshape(height, -1))
+        branch, gate, at = branch_in, gate_in, layer
+        if shared:
+            branch, gate, at = cut(branch_in[layer:], 1), cut(gate_in[layer:], 1), 0
+        return packed_columns(branch, gate, jnp.stack(blocks), at, filler)
+
+    def by_features(value):
+        moved = value.reshape(MICRO, length, D)
+        return lax.all_to_all(moved, "section", split_axis=2, concat_axis=1, tiled=True)
+
+    both_ends = lax.all_to_all(
+        jnp.concatenate([inputs, cotangent], axis=0), "section", 1, 2, tiled=True
+    )
+    stream, grad = both_ends[:MICRO].reshape(rows, D), both_ends[MICRO:].reshape(rows, D)
+    top_grad_all = all_rows(grad)
+    in_moved = [None] * LAYERS
+    mlp_moved = [None] * LAYERS
+    in_moved[0] = spread(after(packed_in(0, False), small_all, stream)[0])
+    normed = low(rms_scale(high(stream), high(small_whole(0, 0, strip))))
+    first_normed = gather_rows(normed)
+    in_width = WIN + own + filler
+    first_both = dot(first_normed, in_moved[0].reshape(D, -1)[:, :in_width])
+    mlp_moved[0] = spread(after(columns_apart(mlp_gate, mlp_up, 0, count), first_both)[0])
+    def layer_weights(layer):
+        in_weight = in_moved[layer].reshape(D, -1)
+        blocks = in_weight[:, WIN + own + filler :]
+        parts = planes if layer else 1
+        blocks = blocks.reshape(count, parts, 2, 2, BW // count // parts, BW)
+        blocks = blocks.transpose(2, 3, 0, 1, 4, 5).reshape(2, 2, BW, BW)
+        in_weight = in_weight[:, : WIN + own + filler]
         empty = jnp.zeros((BW, BW), jnp.bfloat16)
         gate_weights = []
         for which in range(2):
@@ -315,7 +443,7 @@
         taps = taps.transpose(1, 0, 2).reshape(CONV + 1, R)
         taps = lax.dynamic_slice_in_dim(taps, BW * first_block, WIN, 1)
         taps = high(turned(taps, 1, shift))
-        weights.append(
+        return (
             {
                 "in": in_weight,
                 "gates": jnp.concatenate(gate_weights, axis=1),
@@ -327,7 +455,6 @@
                 "decay": high(decay_param[layer]),
                 "norm_rec": high(small_whole(layer, 0, strip)),
                 "norm_mlp": high(small_whole(layer, strip, strip)),
-                "mlp": spread(mlp_pack).reshape(D, 2 * wide),
                 "down": mlp_down[layer],
             }
         )
@@ -377,12 +504,12 @@
         rate = RATE_SCALE * jax.nn.softplus(-weight["decay"])
         return rate
 
-    def rec_forward(section_in, weight):
-        normed = low(rms_scale(high(section_in), weight["norm_rec"]))
-        normed = gather_rows(normed)
-        both = dot(normed, weight["in"])
+    def rec_forward(section_in, weight, normed, both, late):
+        if normed is None:
+            normed = gather_rows(low(rms_scale(high(section_in), weight["norm_rec"])))
+            both = dot(normed, weight["in"])
         branch = both[:, :WIN].reshape(segments, length, WIN)
-        side = both[:, WIN:].reshape(segments, length, own)
+        side = both[:, WIN : WIN + own].reshape(segments, length, own)
         extended = jnp.concatenate([edge(branch[:, length - MARGIN :], 1), branch], axis=1)
         conved = weight["bias"] + weight["taps"][0] * branch
         for lag in range(1, CONV):
@@ -407,6 +534,7 @@
         carry = carried(jnp.stack([cumulative[:, -1], partial[:, -1]]), False)
         states = partial + cumulative * carry[:, None]
         mixture = low(gelu_product(states, side)).reshape(tokens, own)
+        mixture = after(mixture, *late)[0]
         result = high(section_in) + scatter_product(
             lambda left: dot(left, weight["out"]), mixture
         )
@@ -427,21 +555,22 @@
         }
         return low(result), kept
 
-    def mlp_forward(section_in, weight):
+    def mlp_forward(section_in, weight, late):
         normed = low(rms_scale(high(section_in), weight["norm_mlp"]))
+        here = normed
         normed = gather_rows(normed)
         both = dot(normed, weight["mlp"])
         gate_val, up_val = both[:, :wide], both[:, wide:]
-        hidden = low(gated_gelu(gate_val, up_val))
+        hidden = after(low(gated_gelu(gate_val, up_val)), *late)[0]
         result = high(section_in) + scatter_product(
             lambda left: dot(left, weight["down"]), hidden
         )
         kept = {
             "section_in": section_in,
-            "normed": normed,
+            "normed": here,
+            "hidden": hidden,
             "gate_val": gate_val,
             "up_val": up_val,
-            "hidden": hidden,
         }
         return low(result), kept
 
@@ -450,18 +579,13 @@
         grad_hidden = dot_nt(grad_all, weight["down"])
         _, pull = jax.vjp(gated_gelu, kept["gate_val"], kept["up_val"])
         gate_grad, up_grad = pull(grad_hidden)
-        both = low(jnp.concatenate([gate_grad, up_grad], axis=1))
+        both = jnp.concatenate([low(gate_grad), low(up_grad)], axis=1)
         grad_normed = scatter_product(lambda left: dot_nt(left, weight["mlp"]), both)
         _, pull = jax.vjp(rms_scale, high(kept["section_in"]), weight["norm_mlp"])
         grad_in, norm_grad = pull(grad_normed)
-        terms = {
-            "mlp": dot_tn(kept["normed"], both),
-            "down": dot_tn(kept["hidden"], grad_all),
-            "norm_mlp": norm_grad,
-        }
-        return low(grad_in + high(grad)), terms
-
-    def rec_backward(grad, weight, kept):
+        return low(grad_in + high(grad)), {"norm_mlp": norm_grad}
+
+    def rec_backward(grad, weight, kept, early):
         grad_all = gather_rows(grad)
         shape = (segments, length, own)
         grad_mixture = dot_nt(grad_all, weight["out"]).reshape(shape)
@@ -474,7 +598,7 @@
             decays,
             grad_states0,
         )
-        carry = carried(top, True)
+        carry = carried(after(top, *early)[0], True)
         grad_states = partial + reached * carry[:, None]
         previous = jnp.concatenate([kept["carry"][:, None], kept["states"][:, :-1]], axis=1)
         conved, rate_sig, input_sig = kept["conved"], kept["rate_sig"], kept["input_sig"]
@@ -507,7 +631,10 @@
                 )
             )
         both = low(
-            jnp.concatenate([branch_grad, grad_side], axis=2).reshape(tokens, WIN + own)
+            jnp.concatenate(
+                [branch_grad, grad_side, jnp.zeros((segments, length, filler), jnp.float32)],
+                axis=2,
+            ).reshape(tokens, WIN + own + filler)
         )
         grad_normed = scatter_product(lambda left: dot_nt(left, weight["in"]), both)
         _, pull = jax.vjp(rms_scale, high(kept["section_in"]), weight["norm_rec"])
@@ -521,38 +648,22 @@
             "input_bias": jnp.sum(input_grad, axis=(0, 1)),
             "decay": jnp.sum(slope, axis=(0, 1)) * RATE_SCALE * jax.nn.sigmoid(-weight["decay"]),
             "norm_rec": norm_grad,
+            "in_grads": both,
         }
         return low(grad_in + high(grad)), terms
 
-    def planes_first(term):
-        split = low(term).reshape(count, planes, thin, term.shape[1])
-        return split.transpose(1, 0, 2, 3)
-
-    def gathered(piece, axis=0):
-        return lax.all_gather(piece, "section", axis=axis, tiled=True)
-
-    def mlp_gradients(terms):
-        mine = spread(low(section_sum(planes_first(terms["mlp"]))))
-        mine = mine.transpose(1, 0, 2)
-        gate = mine[:, :, :wide].reshape(thin, F)
-        up = mine[:, :, wide:].reshape(thin, F)
-        down = low(section_sum(low(terms["down"]).reshape(planes, wide // planes, D)))
-        return high(gathered(gate)), high(gathered(up)), high(gathered(down))
-
-    def rec_gradients(terms):
-        mine = high(spread(low(section_sum(planes_first(terms["in"])))))
-        gate = low(mine[:, :, WIN:]).transpose(1, 0, 2).reshape(thin, R)
-        branch = mine[:, :, :own].transpose(1, 0, 2).reshape(thin, R)
-        for device in range(count):
-            begin, end, left, right = window_of(device, count)
-            if right > end:
-                piece = mine[device, :, own : own + right - end]
-                branch = branch + jnp.pad(piece, ((0, 0), (end, R - right)))
-            if begin > left:
-                piece = mine[device, :, own + right - end : WIN]
-                branch = branch + jnp.pad(piece, ((0, 0), (left, R - begin)))
-        out = low(section_sum(low(terms["out"]).reshape(planes, own // planes, D)))
-        rows_each = BW // count
+    def mlp_gradients(normed, grad_all, weight):
+        both = dot(normed, weight["mlp"])
+        product, pull = jax.vjp(gated_gelu, both[:, :wide], both[:, wide:])
+        gate_grad, up_grad = pull(dot_nt(grad_all, weight["down"]))
+        both_grad = jnp.concatenate([low(gate_grad), low(up_grad)], axis=1)
+        return low(dot_tn(normed, both_grad)), dot_tn(low(product), grad_all)
+
+    def to_rows(part):
+        return spread(part.reshape(count, strip, 2 * wide))
+
+    def rec_shares(terms):
+        each = BW // count // planes
         blocks = []
         for which in range(2):
             square = jnp.concatenate(
@@ -564,23 +675,61 @@
             )
             square = turned(turned(square, 0, -shift), 1, -shift)
             blocks.append(jnp.stack([square[:BW, :BW], square[BW:, BW:]]))
-        blocks = low(jnp.stack(blocks)).reshape(
-            2, 2, count, planes, rows_each // planes, BW
-        )
-        blocks = spread(low(section_sum(blocks.transpose(3, 2, 0, 1, 4, 5))))
+        blocks = low(jnp.stack(blocks)).reshape(2, 2, count, planes, each, 2, BW // 2)
+        blocks = blocks.transpose(3, 2, 0, 1, 4, 5, 6).reshape(planes, count, 8 * each, BW // 2)
+        blocks = blocks.reshape(planes, count, thin, -1)
+        mixed = low(terms["in"]).reshape(count, planes, thin, WIN + own + filler)
+        mixed = jnp.concatenate([mixed.transpose(1, 0, 2, 3), blocks], axis=3)
+        width = mixed.shape[-1]
+        out = low(terms["out"]).reshape(planes, own // planes, D)
+        flat = jnp.concatenate(
+            [mixed.reshape(planes, count * thin, width), lane_blocks(out, width)], axis=1
+        )
+        return flat
+
+    def rec_pieces(flat):
+        each = BW // count // planes
+        width = WIN + own + filler + 8 * each * (BW // 2) // thin
+        out = whole_rows(flat[count * thin :], own // planes)
+        mine = spread(flat[: count * thin].reshape(count, thin, width))
+        blocks = mine[:, :, WIN + own + filler :].reshape(count, 2, 2, each, BW)
+        mine = high(mine)
+        gate = low(mine[:, :, WIN : WIN + own]).transpose(1, 0, 2).reshape(thin, R)
+        branch = mine[:, :, :own].transpose(1, 0, 2).reshape(thin, R)
+        for device in range(count):
+            begin, end, left, right = window_of(device, count)
+            if right > end:
+                piece = mine[device, :, own : own + right - end]
+                branch = branch + jnp.pad(piece, ((0, 0), (end, R - right)))
+            if begin > left:
+                piece = mine[device, :, own + right - end : WIN]
+                branch = branch + jnp.pad(piece, ((0, 0), (left, R - begin)))
         totals = [0.0] * H
         for device in range(count):
             first = window_of(device, count)[2] // BW
             for at in range(2):
                 totals[first + at] = totals[first + at] + high(blocks[device, :, at])
-        gates = gathered(low(jnp.stack(totals, axis=1)), 2)
-        return (
-            high(gathered(low(branch))),
-            high(gathered(gate)),
-            high(gathered(out)),
-            high(gates[0]),
-            high(gates[1]),
-        )
+        gates = low(jnp.stack(totals, axis=1))
+        return jnp.concatenate(
+            [
+                lane_blocks(low(branch), WIN),
+                lane_blocks(gate, WIN),
+                lane_blocks(out, WIN),
+                lane_blocks(gates.reshape(-1, 2 * BW), WIN),
+            ],
+            axis=0,
+        )
+
+    def rec_gradients(flat):
+        each = BW // count // planes
+        sizes = [thin * R // WIN, thin * R // WIN, own // planes * D // WIN]
+        at = [0, sizes[0], sizes[0] + sizes[1], sum(sizes)]
+        branch = whole_rows(flat[:, at[0] : at[1]], thin).reshape(strip, R)
+        gate = whole_rows(flat[:, at[1] : at[2]], thin).reshape(strip, R)
+        out = whole_rows(flat[:, at[2] : at[3]], own // planes).reshape(own, D)
+        gates = flat[:, at[3] :].reshape(planes, 2, H, each, BW)
+        gates = gates.transpose(1, 2, 0, 3, 4).reshape(2, H, BW // count, BW)
+        return branch, gate, out, gates[0], gates[1]
 
     def small_gradients(terms):
         taps = turned(terms["taps"], 1, -shift)
@@ -593,49 +742,108 @@
         )
         channels = jnp.concatenate([taps, owned], axis=0)
         norms = jnp.stack([terms["norm_rec"], terms["norm_mlp"]])
-        flat = jnp.concatenate([channels.reshape(-1), norms.reshape(-1)])
-        flat = lax.psum(flat.reshape(-1, 128), ("section", "dp")).reshape(-1)
-        channels = flat[: (CONV + 4) * R].reshape(CONV + 4, R)
-        norms = flat[(CONV + 4) * R :].reshape(2, D)
-        channels = lax.dynamic_slice_in_dim(channels, own_begin, own, 1)
-        norms = lax.dynamic_slice_in_dim(norms, strip * me, strip, 1)
+        pack = jnp.concatenate(
+            [
+                channels.reshape(CONV + 4, count, own).transpose(1, 0, 2).reshape(count, -1),
+                norms.reshape(2, count, strip).transpose(1, 0, 2).reshape(count, -1),
+            ],
+            axis=1,
+        )
+        mine = jnp.sum(spread(pack), axis=0)
+        mine = mine.reshape(-1, 128)
+        mine = (mine + sum(other_planes(mine))).reshape(-1)
+        channels = mine[: (CONV + 4) * own].reshape(CONV + 4, own)
+        norms = mine[(CONV + 4) * own :].reshape(2, strip)
         return channels, norms
 
-    def by_tokens(value):
-        moved = lax.all_to_all(value, "section", split_axis=1, concat_axis=2, tiled=True)
-        return moved.reshape(rows, D)
-
-    def by_features(value):
-        moved = value.reshape(MICRO, length, D)
-        return lax.all_to_all(moved, "section", split_axis=2, concat_axis=1, tiled=True)
-
-    stream = by_tokens(inputs)
+    weights = [layer_weights(0)]
+    weights[0]["mlp"] = mlp_moved[0].reshape(D, 2 * wide)
     kept = []
+    everyone = [None] * LAYERS
+    top = LAYERS - 1
     for layer in range(LAYERS):
-        stream, kept_rec = rec_forward(stream, weights[layer])
-        stream, kept_mlp = mlp_forward(stream, weights[layer])
+        weight = weights[layer]
+        first = layer == 0
+        stream, kept_rec = rec_forward(
+            stream,
+            weight,
+            first_normed if first else None,
+            first_both if first else None,
+            [weight["mlp"], top_grad_all] if first else [],
+        )
+        if first:
+            in_share = spread(after(packed_in(1, True), kept_rec["mixture"])[0])
+            in_moved[1] = lax.all_gather(in_share, "section", axis=1, tiled=True)
+            shares = [
+                lax.dynamic_slice_in_dim(part[1:], thin * rank, thin, 1)
+                for part in (mlp_gate, mlp_up)
+            ]
+            share = spread(after(columns_apart(*shares, 0, count), in_share)[0])
+            share = after(share, in_moved[1])[0]
+            mlp_moved[1] = lax.all_gather(share, "section", axis=1, tiled=True)
+            weights.append(layer_weights(1))
+        else:
+            everyone[0] = all_rows(after(kept[0][1]["normed"], kept_rec["mixture"])[0])
+        stream, kept_mlp = mlp_forward(stream, weight, [in_share] if first else [])
+        if first:
+            weights[1]["mlp"] = mlp_moved[1].reshape(D, 2 * wide)
+        else:
+            everyone[1] = all_rows(after(kept_mlp["normed"], stream)[0])
         kept.append((kept_rec, kept_mlp))
     output = by_features(stream)
-    grad = by_tokens(cotangent)
-    results = [None] * LAYERS
-    for layer in reversed(range(LAYERS)):
-        grad, mlp_terms = mlp_backward(grad, weights[layer], kept[layer][1])
-        mlp_grads = mlp_gradients(mlp_terms)
-        grad, rec_terms = rec_backward(grad, weights[layer], kept[layer][0])
-        rec_grads = rec_gradients(rec_terms)
-        channels, norms = small_gradients({**mlp_terms, **rec_terms})
-        results[layer] = rec_grads + (
-            channels[:CONV],
-            channels[CONV],
-            channels[CONV + 1],
-            channels[CONV + 2],
-            channels[CONV + 3],
-            norms[0],
-            norms[1],
-        ) + mlp_grads
+    mlp_downs = [None] * LAYERS
+    mlp_rows = [None] * LAYERS
+    rec_flat = [None] * LAYERS
+    smalls = [None] * LAYERS
+
+    grad_in = grad
+    grad, mlp_terms = mlp_backward(grad_in, weights[1], kept[1][1])
+    ins1, mlp_downs[1] = mlp_gradients(everyone[1], top_grad_all, weights[1])
+    grad, everyone[0] = after(grad, everyone[0])
+    grad, terms = rec_backward(grad, weights[1], kept[1][0], [output])
+    grad, everyone[1] = after(grad, everyone[1])
+    flat = section_sum(rec_shares(terms))
+    smalls[1] = small_gradients({**mlp_terms, **terms})
+    mlp_rows[1] = to_rows(ins1)
+
+    grad_in = grad
+    grad_mid, mlp_terms = mlp_backward(grad_in, weights[0], kept[0][1])
+    pieces1 = rec_pieces(after(flat, grad_mid)[0])
+    rec_flat[1] = lax.all_gather(pieces1, "section", axis=0, tiled=False)
+    grad_all = all_rows(grad_in)
+    grad, terms = rec_backward(grad_mid, weights[0], kept[0][0], [pieces1, ins1])
     input_grad = by_features(grad)
-    stacked = tuple(jnp.stack(parts) for parts in zip(*results))
-    return (output, input_grad) + stacked
+    flat = rec_shares(terms)
+    grad_all = after(grad_all, flat)[0]
+    flat = section_sum(flat)
+    smalls[0] = small_gradients({**mlp_terms, **terms})
+    ins0, mlp_downs[0] = mlp_gradients(everyone[0], grad_all, weights[0])
+    joined = [joined_rows(mlp_rows[1], which, 1, LAYERS, None) for which in range(2)]
+    flat = after(flat, ins0, rec_flat[1], input_grad, *smalls[0], *joined, *mlp_downs)[0]
+    pieces0 = rec_pieces(flat)
+    rec_flat[0] = lax.all_gather(pieces0, "section", axis=0, tiled=False)
+    mlp_rows[0] = to_rows(after(ins0, pieces0)[0])
+    mlp_results = tuple(
+        joined_rows(mlp_rows[0], which, 0, LAYERS, joined[which]) for which in range(2)
+    ) + (jnp.stack(mlp_downs),)
+    rec_flat[0] = after(rec_flat[0], *mlp_results)[0]
+    results = []
+    for layer in range(LAYERS):
+        channels, norms = smalls[layer]
+        results.append(
+            rec_gradients(rec_flat[layer])
+            + (
+                channels[:CONV],
+                channels[CONV],
+                channels[CONV + 1],
+                channels[CONV + 2],
+                channels[CONV + 3],
+                norms[0],
+                norms[1],
+            )
+        )
+    stacked = tuple(high(jnp.stack(parts)) for parts in zip(*results))
+    return (output, input_grad) + stacked + mlp_results
 
 
 def solution(mesh):

time: 2050 us -> 1200 us (0.59)
  waiting for transfers between devices: 1090 us -> 413 us
  matrix products: 105 us -> 235 us
  other arithmetic: 220 us -> 105 us
  starting transfers between devices: 240 us -> 139 us
  blocking collectives: 141 us -> 48.5 us
  Pallas kernels: 5.19 us -> 37 us
  local copies, waits for them, and re-layouts: 210 us -> 188 us
    ppermute x30 -> x18, waiting for transfers between devices: 746 us -> 16.7 us  [other_planes(): lax.ppermute(value, 'section', [(at, at ^ k) for at in range(count)])]
    all_to_all x11 -> x9, waiting for transfers between devices: 17.7 us -> 132 us  [spread(): return lax.all_to_all(pack, 'dp', 0, 0, tiled=False)]
    all_gather x6 -> x0, blocking collectives: 107 us -> none  [the longest x4 69.6 us: carried(): lax.all_gather(totals.reshape(2, count, MICRO, channels), 'section', axis...]
    ppermute x30 -> x18, starting transfers between devices: 109 us -> 26.6 us  [other_planes(): lax.ppermute(value, 'section', [(at, at ^ k) for at in range(count)])]
    convert_element_type x38 -> x10, other arithmetic: 80.2 us -> 9.53 us  [low(): return value.astype(jnp.bfloat16)]
    ppermute x64, waiting for transfers between devices: 263 us -> 198 us  [swapped(): return lax.ppermute(value, 'dp', [(at, at ^ offset) for at in range(count)])]
    dot_general x14 -> x16, matrix products: 31.4 us -> 77.1 us  [dot(): return jnp.dot(left, right, preferred_element_type=jnp.float32)]
    dot_general x10, matrix products: 33.3 us -> 78.7 us  [dot_tn(): lax.dot_general(left, right, (((0,), (0,)), ((), ())), preferred_element_...]
  transfers between devices with their start and end apart: 126 -> 107, of which waited for: 60 -> 56; matrix products, arithmetic and copies ran while one was open for 23% -> 39% of each run, Pallas kernels for 0% -> 3%
where the time goes in v2:
time: 1200 us; the launch traced here: 1180 us
  waiting for transfers between devices  413 us (34%)
  matrix products  235 us (20%)
  local copies, waits for them, and re-layouts  188 us (16%)
  starting transfers between devices  139 us (12%)
  other arithmetic  105 us (9%)
  blocking collectives  48.5 us (4%)
  Pallas kernels  37 us (3%)
  between operations  19.8 us (2%)
    ppermute x64, waiting for transfers between devices, swapped(): return lax.ppermute(value, 'dp', [(at, at ^ offset) for at in range(count)])  198 us
    all_to_all x9, waiting for transfers between devices, spread(): return lax.all_to_all(pack, 'dp', 0, 0, tiled=False)  132 us
    dot_general x10, matrix products, dot_tn(): lax.dot_general(left, right, (((0,), (0,)), ((), ())), preferred_element_...  78.7 us
    dot_general x16, matrix products, dot_nt(): lax.dot_general(left, right, (((1,), (1,)), ((), ())), preferred_element_...  78.5 us
    dot_general x16, matrix products, dot(): return jnp.dot(left, right, preferred_element_type=jnp.float32)  77.1 us
    ppermute x64, starting transfers between devices, swapped(): return lax.ppermute(value, 'dp', [(at, at ^ offset) for at in range(count)])  61.8 us
    unnamed x552, local copies, waits for them, and re-layouts  60.1 us
    all_to_all x9, starting transfers between devices, spread(): return lax.all_to_all(pack, 'dp', 0, 0, tiled=False)  36.9 us
  transfers between devices with their start and end apart: 107, of which 56 were waited for; matrix products, arithmetic and copies ran while one was open for 39% of the time, Pallas kernels for 3%

profile of v2, /device:TPU:0, one launch (start us, length us, event | category | flops | bytes accessed | tf_op | source)
XLA Modules:
  0.0 1184.7 jit_solution(50280904776029547)
XLA Ops:
  10.3 20.7 %all_to_all.109 = bf16[4,128,512]{2,0,1:T(4,128)(2,1)S(1)} all-to-all(bf16[4,128,512]{2,0,1:T(4,128)(2,1)S(1)} %pad_maximum_fusion.25), channel_id=1, replica_groups=mesh['section'=4,'dp'=8] {'section'}, dimensions={1} | all-to-all | bytes 1048576 | tf_op jit(solution)/shard_map/all_to_all | solution.py:406
  51.6 9.3 all-gather.3
  73.9 61.0 %collective-permute-done = bf16[64,2048]{1,0:T(8,128)(2,1)S(1)} collective-permute-done((bf16[64,2048]{1,0:T(8,128)(2,1)}, bf16[64,2048]{1,0:T(8,128)(2,1)S(1)}, u32[]{:S(2)}, u32[]{:S(2)}) %collective-permute-start) | collective-permute-done | bytes 262176 | tf_op jit(solution)/shard_map/ppermute | solution.py:58
  134.9 6.2 collective-permute-done.2
  158.9 6.2 fusion.48
  205.8 35.6 %all-to-all-done.2 = bf16[8,256,1536]{2,1,0:T(8,128)(2,1)} async-done(((bf16[8,256,1536]{2,1,0:T(8,128)(2,1)}), bf16[8,256,1536]{2,1,0:T(8,128)(2,1)}, u32[]{:S(2)}, u32[]{:S(2)}) %all-to-all-start.2) | async-done | bytes 6291488 | tf_op jit(solution)/shard_map/all_to_all | solution.py:82
  241.5 18.5 %all_to_all.110 = bf16[8,64,1024]{2,1,0:T(8,128)(2,1)} all-to-all(bf16[8,64,1024]{2,1,0:T(8,128)(2,1)S(1)} %shard_map.318), channel_id=1, replica_groups=mesh['section'=4,'dp'=8] {'dp'}, dimensions={0} | all-to-all | bytes 2097152 | tf_op jit(solution)/shard_map/all_to_all | solution.py:82
  271.3 8.5 collective-permute-done.10
  303.5 11.5 all-to-all-done.4
  315.0 24.4 %all-gather.15.cloned.1.call-done = bf16[8,256,1024]{2,1,0:T(8,128)(2,1)} async-done(((bf16[8,64,1024]{2,1,0:T(8,128)(2,1)}), bf16[8,256,1024]{2,1,0:T(8,128)(2,1)}) %all-gather.15.cloned.1.call-update) | async-done | bytes 4194320 | tf_op jit(solution)/shard_map/all_gather | solution.py:776
  339.4 6.2 fusion.432
  359.4 5.7 collective-permute-done.17
  365.1 6.0 collective-permute-done.18
  375.9 5.8 collective-permute-done.20
  400.6 6.3 collective-permute-done.24
  418.6 5.5 collective-permute-done.26
  451.2 6.4 collective-permute-done.30
  468.0 5.3 collective-permute-done.33
  478.2 6.5 fusion.433
  512.6 6.3 collective-permute-done.37
  520.8 8.3 collective-permute-done.39
  530.2 19.9 %all-gather.19.cloned.1.call-done = bf16[2048,2048]{1,0:T(8,128)(2,1)} async-done(((bf16[64,2048]{1,0:T(8,128)(2,1)}), bf16[2048,2048]{1,0:T(8,128)(2,1)}) %all-gather.19.cloned.1.call-update) | async-done | bytes 8388624 | tf_op jit(solution)/shard_map/all_gather | solution.py:90
  561.0 5.1 collective-permute-done.49
  615.1 6.1 collective-permute-done.55
  642.5 5.7 collective-permute-done.57
  648.2 6.1 collective-permute-done.58
  659.0 5.8 collective-permute-done.60
  681.6 17.9 %fusion.434 = f32[2048,1536]{0,1:T(8,128)} fusion(bf16[2048,2048]{1,0:T(8,128)(2,1)} %all-gather.21.cloned.1.call-done, bf16[2048,1536]{1,0:T(8,128)(2,1)S(1)} %bitcast.898), kind=kOutput, calls=%fused_computation.922 | convolution fusion | flops 12884901888 | bytes 27262976 | tf_op jit(solution)/shard_map/dot_general | solution.py:33
  707.8 17.3 %fusion.6 = (bf16[2048,768]{0,1:T(8,128)(2,1)}, bf16[2048,768]{0,1:T(8,128)(2,1)}) fusion(f32[2048,1536]{0,1:T(8,128)} %fusion.434, bf16[2048,2048]{1,0:T(8,128)(2,1)} %all-gather.13.cloned.1.call-done, bf16[2,768,2048]{2,1,0:T(8,128)(2,1)S(1)} %bitcast.904), kind=kOutput, calls=%fused_computation.13 | convolution fusion | flops 6480199680 | bytes 30408704 | tf_op jit(solution)/shard_map/dot_general | solution.py:37
  729.9 18.7 %convolution_convert_fusion.1 = bf16[2048,1536]{1,0:T(8,128)(2,1)} fusion(bf16[2048,2048]{1,0:T(8,128)(2,1)} %all-gather.21.cloned.1.call-done, bf16[2048,768]{0,1:T(8,128)(2,1)} %get-tuple-element.146, bf16[2048,768]{0,1:T(8,128)(2,1)S(1)} %copy-done.238), kind=kOutput, calls=%fused_computation.6 | convolution fusion | flops 12900630528 | bytes 20971520 | tf_op jit(solution)/shard_map/dot_general | solution.py:43
  768.8 6.5 all-to-all-done.6
  811.2 6.8 collective-permute-done.75
  844.5 6.9 collective-permute-done.78
  881.8 19.1 %fusion.435 = f32[2048,1536]{0,1:T(8,128)} fusion(bf16[2048,2048]{1,0:T(8,128)(2,1)} %all-gather.19.cloned.1.call-done, bf16[2048,1536]{1,0:T(8,128)(2,1)} %bitcast.54), kind=kOutput, calls=%fused_computation.923 | convolution fusion | flops 12884901888 | bytes 27262976 | tf_op jit(solution)/shard_map/dot_general | solution.py:33
  908.1 30.2 %all-to-all-done.9.part_ref = bf16[8,256,1536]{2,1,0:T(8,128)(2,1)} async-done(((bf16[8,256,1536]{2,1,0:T(8,128)(2,1)}), bf16[8,256,1536]{2,1,0:T(8,128)(2,1)}, u32[]{:S(2)}, u32[]{:S(2)}) %all-to-all-start.9) | async-done | bytes 6291488 | tf_op jit(solution)/shard_map/all_to_all | solution.py:82
  941.9 14.6 %fusion.21 = f32[768,2048]{1,0:T(8,128)} fusion(bf16[2048,2048]{1,0:T(8,128)(2,1)} %all-gather.13.cloned.1.call-done, f32[2048,1536]{0,1:T(8,128)} %fusion.434), kind=kOutput, calls=%fused_computation.38 | convolution fusion | flops 6458179584 | bytes 27262976 | tf_op jit(solution)/shard_map/dot_general | solution.py:43
  957.3 6.6 shard_map.326.kept_ref
  963.9 6.6 shard_map.327.kept_ref
  972.8 14.8 %fusion.20 = f32[768,2048]{1,0:T(8,128)} fusion(bf16[2048,2048]{1,0:T(8,128)(2,1)} %all-gather.23.cloned.1.call-done, f32[2048,1536]{0,1:T(8,128)} %fusion.435), kind=kOutput, calls=%fused_computation.37 | convolution fusion | flops 6458179584 | bytes 27262976 | tf_op jit(solution)/shard_map/dot_general | solution.py:43
  987.6 14.1 %fusion.13 = (bf16[2048,768]{0,1:T(8,128)(2,1)S(1)}, bf16[2048,768]{0,1:T(8,128)(2,1)S(1)}) fusion(f32[2048,1536]{0,1:T(8,128)} %fusion.435, bf16[2048,2048]{1,0:T(8,128)(2,1)S(1)} %copy-done.235, bf16[2,768,2048]{2,1,0:T(8,128)(2,1)} %param.36), kind=kOutput, calls=%fused_computation.20 | convolution fusion | flops 6480199680 | bytes 30408704 | tf_op jit(solution)/shard_map/dot_general | solution.py:37
  1001.7 17.6 %convolution_convert_fusion = bf16[2048,1536]{1,0:T(8,128)(2,1)} fusion(bf16[2048,2048]{1,0:T(8,128)(2,1)} %all-gather.19.cloned.1.call-done, bf16[2048,768]{0,1:T(8,128)(2,1)S(1)} %get-tuple-element.144, bf16[2048,768]{0,1:T(8,128)(2,1)S(1)} %get-tuple-element.143), kind=kOutput, calls=%fused_computation.5 | convolution fusion | flops 12900630528 | bytes 20971520 | tf_op jit(solution)/shard_map/dot_general | solution.py:43
  1029.3 11.3 all-to-all-done.10
  1051.7 5.1 all-to-all-done.12
  1056.8 5.1 all-to-all-start.11
  1094.1 11.6 pad_maximum_fusion
  1105.6 27.9 %all-to-all-done.11.part_ref = bf16[8,256,1536]{2,1,0:T(8,128)(2,1)} async-done(((bf16[8,256,1536]{2,1,0:T(8,128)(2,1)}), bf16[8,256,1536]{2,1,0:T(8,128)(2,1)}, u32[]{:S(2)}, u32[]{:S(2)}) %all-to-all-start.11) | async-done | bytes 6291488 | tf_op jit(solution)/shard_map/all_to_all | solution.py:82
  1133.6 6.6 shard_map.329
  1140.2 6.6 shard_map.328
  (1224 shorter events, 574.0 us)
Async XLA Ops:
  7.2 234.3 %all-gather.13.cloned.1.call-start = ((), (), s32[]{:S(2)}) async-start(), calls=%async_computation.15 | async-start | bytes 8650752 | tf_op jit(solution)/shard_map/all_gather | solution.py:90
  61.0 97.8 %all-to-all-start.1 = ((bf16[8,256,1024]{2,1,0:T(8,128)(2,1)}), bf16[8,256,1024]{2,1,0:T(8,128)(2,1)}, u32[]{:S(2)}, u32[]{:S(2)}) async-start(bf16[8,256,1024]{2,1,0:T(8,128)(2,1)} %copy-done.1), calls=%async_computation.1 | async-start | bytes 8388608 | tf_op jit(solution)/shard_map/all_to_all | solution.py:82
  69.3 65.5 %collective-permute-start = (bf16[64,2048]{1,0:T(8,128)(2,1)}, bf16[64,2048]{1,0:T(8,128)(2,1)S(1)}, u32[]{:S(2)}, u32[]{:S(2)}) collective-permute-start(bf16[64,2048]{1,0:T(8,128)(2,1)} %get-tuple-element.142), channel_id=1, source_target_pairs={{0,2},{1,3},{2,0},{3,1},{4,6},{5,7},{6,4},{7,5},{8,10},{9,11},{10,... | collective-permute-start | bytes 786440 | tf_op jit(solution)/shard_map/ppermute | solution.py:58
  71.2 63.7 %collective-permute-start.1 = (bf16[64,2048]{1,0:T(8,128)(2,1)}, bf16[64,2048]{1,0:T(8,128)(2,1)S(1)}, u32[]{:S(2)}, u32[]{:S(2)}) collective-permute-start(bf16[64,2048]{1,0:T(8,128)(2,1)} %get-tuple-element.142), channel_id=1, source_target_pairs={{0,4},{1,5},{2,6},{3,7},{4,0},{5,1},{6,2},{7,3},{8,12},{9,13},{10,... | collective-permute-start | bytes 786440 | tf_op jit(solution)/shard_map/ppermute | solution.py:58
  72.7 68.3 %collective-permute-start.2 = (bf16[64,2048]{1,0:T(8,128)(2,1)}, bf16[64,2048]{1,0:T(8,128)(2,1)}, u32[]{:S(2)}, u32[]{:S(2)}) collective-permute-start(bf16[64,2048]{1,0:T(8,128)(2,1)} %get-tuple-element.142), channel_id=1, source_target_pairs={{0,6},{1,7},{2,4},{3,5},{4,2},{5,3},{6,0},{7,1},{8,14},{9,15},{10,... | collective-permute-start | bytes 786440 | tf_op jit(solution)/shard_map/ppermute | solution.py:58
  165.1 76.4 %all-to-all-start.2 = ((bf16[8,256,1536]{2,1,0:T(8,128)(2,1)}), bf16[8,256,1536]{2,1,0:T(8,128)(2,1)}, u32[]{:S(2)}, u32[]{:S(2)}) async-start(bf16[8,256,1536]{2,1,0:T(8,128)(2,1)} %copy-done), calls=%async_computation.2 | async-start | bytes 12582912 | tf_op jit(solution)/shard_map/all_to_all | solution.py:82
  169.9 169.5 %all-gather.15.cloned.1.call-start = ((), (), s32[]{:S(2)}) async-start(), calls=%async_computation.16 | async-start | bytes 5242880 | tf_op jit(solution)/shard_map/all_gather | solution.py:776
  290.4 24.5 %all-to-all-start.4 = ((bf16[8,64,1536]{2,1,0:T(8,128)(2,1)}), bf16[8,64,1536]{2,1,0:T(8,128)(2,1)S(1)}, u32[]{:S(2)}, u32[]{:S(2)}) async-start(bf16[8,64,1536]{2,1,0:T(8,128)(2,1)} %shard_map.321), calls=%async_computation.4 | async-start | bytes 3145728 | tf_op jit(solution)/shard_map/all_to_all | solution.py:82
  294.0 184.2 %all-gather.17.cloned.1.call-start = ((), (), s32[]{:S(2)}) async-start(), calls=%async_computation.17 | async-start | bytes 7864320 | tf_op jit(solution)/shard_map/all_gather | solution.py:783
  339.4 210.7 %all-gather.19.cloned.1.call-start = ((), (), s32[]{:S(2)}) async-start(), calls=%async_computation.18 | async-start | bytes 8650752 | tf_op jit(solution)/shard_map/all_gather | solution.py:90
  428.3 227.2 %all-gather.21.cloned.1.call-start = ((), (), s32[]{:S(2)}) async-start(), calls=%async_computation.19 | async-start | bytes 8650752 | tf_op jit(solution)/shard_map/all_gather | solution.py:90
  432.3 14.8 %collective-permute-start.41 = (bf16[64,2048]{1,0:T(8,128)(2,1)S(1)}, bf16[64,2048]{1,0:T(8,128)(2,1)S(1)}, u32[]{:S(2)}, u32[]{:S(2)}) collective-permute-start(bf16[64,2048]{1,0:T(8,128)(2,1)S(1)} %bitcast.888), channel_id=1, source_target_pairs={{0,4},{1,5},{2,6},{3,7},{4,0},{5,1},{6,2},{7,3},{8,12},{9,13},{10,... | collective-permute-start | bytes 786440 | tf_op jit(solution)/shard_map/ppermute | solution.py:58
  436.0 15.2 %collective-permute-start.29 = (bf16[64,2048]{1,0:T(8,128)(2,1)S(1)}, bf16[64,2048]{1,0:T(8,128)(2,1)S(1)}, u32[]{:S(2)}, u32[]{:S(2)}) collective-permute-start(bf16[64,2048]{1,0:T(8,128)(2,1)S(1)} %get-tuple-element.213), channel_id=1, source_target_pairs={{0,2},{1,3},{2,0},{3,1},{4,6},{5,7},{6,4},{7,5},{8,10},{9,11},{10,... | collective-permute-start | bytes 786440 | tf_op jit(solution)/shard_map/ppermute | solution.py:58
  437.7 19.9 %collective-permute-start.30 = (bf16[64,2048]{1,0:T(8,128)(2,1)S(1)}, bf16[64,2048]{1,0:T(8,128)(2,1)S(1)}, u32[]{:S(2)}, u32[]{:S(2)}) collective-permute-start(bf16[64,2048]{1,0:T(8,128)(2,1)S(1)} %get-tuple-element.215), channel_id=1, source_target_pairs={{0,4},{1,5},{2,6},{3,7},{4,0},{5,1},{6,2},{7,3},{8,12},{9,13},{10,... | collective-permute-start | bytes 786440 | tf_op jit(solution)/shard_map/ppermute | solution.py:58
  439.9 17.7 %collective-permute-start.31 = (bf16[64,2048]{1,0:T(8,128)(2,1)S(1)}, bf16[64,2048]{1,0:T(8,128)(2,1)S(1)}, u32[]{:S(2)}, u32[]{:S(2)}) collective-permute-start(bf16[64,2048]{1,0:T(8,128)(2,1)S(1)} %get-tuple-element.214), channel_id=1, source_target_pairs={{0,6},{1,7},{2,4},{3,5},{4,2},{5,3},{6,0},{7,1},{8,14},{9,15},{10,... | collective-permute-start | bytes 786440 | tf_op jit(solution)/shard_map/ppermute | solution.py:58
  448.3 25.3 %collective-permute-start.43 = (bf16[256,2048]{1,0:T(8,128)(2,1)}, bf16[256,2048]{1,0:T(8,128)(2,1)}, u32[]{:S(2)}, u32[]{:S(2)}) collective-permute-start(bf16[256,2048]{1,0:T(8,128)(2,1)} %pad_maximum_fusion.13), channel_id=1, source_target_pairs={{0,1},{1,0},{2,3},{3,2},{4,5},{5,4},{6,7},{7,6},{8,9},{9,8},{10,11... | collective-permute-start | bytes 3145736 | tf_op jit(solution)/shard_map/ppermute | solution.py:58
  496.9 14.8 %collective-permute-start.46 = (bf16[64,2048]{1,0:T(8,128)(2,1)S(1)}, bf16[64,2048]{1,0:T(8,128)(2,1)S(1)}, u32[]{:S(2)}, u32[]{:S(2)}) collective-permute-start(bf16[64,2048]{1,0:T(8,128)(2,1)S(1)} %get-tuple-element.209), channel_id=1, source_target_pairs={{0,4},{1,5},{2,6},{3,7},{4,0},{5,1},{6,2},{7,3},{8,12},{9,13},{10,... | collective-permute-start | bytes 786440 | tf_op jit(solution)/shard_map/ppermute | solution.py:58
  500.9 18.1 %collective-permute-start.37 = (bf16[64,2048]{1,0:T(8,128)(2,1)S(1)}, bf16[64,2048]{1,0:T(8,128)(2,1)S(1)}, u32[]{:S(2)}, u32[]{:S(2)}) collective-permute-start(bf16[64,2048]{1,0:T(8,128)(2,1)S(1)} %get-tuple-element.210), channel_id=1, source_target_pairs={{0,2},{1,3},{2,0},{3,1},{4,6},{5,7},{6,4},{7,5},{8,10},{9,11},{10,... | collective-permute-start | bytes 786440 | tf_op jit(solution)/shard_map/ppermute | solution.py:58
  501.5 19.3 %collective-permute-start.38 = (bf16[64,2048]{1,0:T(8,128)(2,1)S(1)}, bf16[64,2048]{1,0:T(8,128)(2,1)S(1)}, u32[]{:S(2)}, u32[]{:S(2)}) collective-permute-start(bf16[64,2048]{1,0:T(8,128)(2,1)S(1)} %get-tuple-element.212), channel_id=1, source_target_pairs={{0,4},{1,5},{2,6},{3,7},{4,0},{5,1},{6,2},{7,3},{8,12},{9,13},{10,... | collective-permute-start | bytes 786440 | tf_op jit(solution)/shard_map/ppermute | solution.py:58
  505.5 23.6 %collective-permute-start.39 = (bf16[64,2048]{1,0:T(8,128)(2,1)S(1)}, bf16[64,2048]{1,0:T(8,128)(2,1)S(1)}, u32[]{:S(2)}, u32[]{:S(2)}) collective-permute-start(bf16[64,2048]{1,0:T(8,128)(2,1)S(1)} %get-tuple-element.211), channel_id=1, source_target_pairs={{0,6},{1,7},{2,4},{3,5},{4,2},{5,3},{6,0},{7,1},{8,14},{9,15},{10,... | collective-permute-start | bytes 786440 | tf_op jit(solution)/shard_map/ppermute | solution.py:58
  551.8 14.3 %collective-permute-start.49 = (bf16[64,2048]{1,0:T(8,128)(2,1)S(1)}, bf16[64,2048]{1,0:T(8,128)(2,1)}, u32[]{:S(2)}, u32[]{:S(2)}) collective-permute-start(bf16[64,2048]{1,0:T(8,128)(2,1)S(1)} %get-tuple-element.58), channel_id=1, source_target_pairs={{0,4},{1,5},{2,6},{3,7},{4,0},{5,1},{6,2},{7,3},{8,12},{9,13},{10,... | collective-permute-start | bytes 786440 | tf_op jit(solution)/shard_map/ppermute | solution.py:58
  552.1 15.0 %collective-permute-start.50 = (bf16[64,2048]{1,0:T(8,128)(2,1)S(1)}, bf16[64,2048]{1,0:T(8,128)(2,1)}, u32[]{:S(2)}, u32[]{:S(2)}) collective-permute-start(bf16[64,2048]{1,0:T(8,128)(2,1)S(1)} %get-tuple-element.58), channel_id=1, source_target_pairs={{0,6},{1,7},{2,4},{3,5},{4,2},{5,3},{6,0},{7,1},{8,14},{9,15},{10,... | collective-permute-start | bytes 786440 | tf_op jit(solution)/shard_map/ppermute | solution.py:58
  557.5 16.7 %all-to-all-start.5 = ((bf16[4,2,16384]{2,1,0:T(2,128)(2,1)}), bf16[4,2,16384]{2,1,0:T(2,128)(2,1)S(1)}, u32[]{:S(2)}, u32[]{:S(2)}) async-start(bf16[4,2,16384]{2,1,0:T(2,128)(2,1)} %reshape.1297), calls=%async_computation.5 | async-start | bytes 524288 | tf_op jit(solution)/shard_map/all_to_all | solution.py:404
  560.9 187.7 %reduce-scatter.3.cloned.1.call-start = ((), (), s32[]{:S(2)}) async-start(), calls=%async_computation.20 | async-start | bytes 6881280 | tf_op jit(solution)/shard_map/reduce_scatter | solution.py:86
  584.6 15.3 %collective-permute-start.52 = (f32[2,8,2,320]{3,2,1,0:T(2,128)S(1)}, f32[2,8,2,320]{3,2,1,0:T(2,128)S(1)}, u32[]{:S(2)}, u32[]{:S(2)}) collective-permute-start(f32[2,8,2,320]{3,2,1,0:T(2,128)S(1)} %reshape.1217), channel_id=1, source_target_pairs={{0,8},{8,0},{16,24},{24,16},{1,9},{9,1},{17,25},{25,17},{2,10},{10... | collective-permute-start | bytes 122888 | tf_op jit(solution)/shard_map/ppermute | solution.py:96
  584.7 15.2 %collective-permute-start.53 = (f32[2,8,2,320]{3,2,1,0:T(2,128)S(1)}, f32[2,8,2,320]{3,2,1,0:T(2,128)S(1)}, u32[]{:S(2)}, u32[]{:S(2)}) collective-permute-start(f32[2,8,2,320]{3,2,1,0:T(2,128)S(1)} %reshape.1217), channel_id=1, source_target_pairs={{0,16},{8,24},{16,0},{24,8},{1,17},{9,25},{17,1},{25,9},{2,18},{10... | collective-permute-start | bytes 122888 | tf_op jit(solution)/shard_map/ppermute | solution.py:96
  630.8 342.0 %all-gather.23.cloned.1.call-start = ((), (), s32[]{:S(2)}) async-start(), calls=%async_computation.22 | async-start | bytes 8650752 | tf_op jit(solution)/shard_map/all_gather | solution.py:90
  681.4 18.1 %collective-permute-start.64 = (bf16[256,2048]{1,0:T(8,128)(2,1)S(1)}, bf16[256,2048]{1,0:T(8,128)(2,1)S(1)}, u32[]{:S(2)}, u32[]{:S(2)}) collective-permute-start(bf16[256,2048]{1,0:T(8,128)(2,1)S(1)} %convolution_convert_fusion.6), channel_id=1, source_target_pairs={{0,1},{1,0},{2,3},{3,2},{4,5},{5,4},{6,7},{7,6},{8,9},{9,8},{10,11... | collective-permute-start | bytes 3145736 | tf_op jit(solution)/shard_map/ppermute | solution.py:58
  704.2 20.9 %collective-permute-start.65 = (bf16[64,2048]{1,0:T(8,128)(2,1)S(1)}, bf16[64,2048]{1,0:T(8,128)(2,1)S(1)}, u32[]{:S(2)}, u32[]{:S(2)}) collective-permute-start(bf16[64,2048]{1,0:T(8,128)(2,1)S(1)} %get-tuple-element.201), channel_id=1, source_target_pairs={{0,2},{1,3},{2,0},{3,1},{4,6},{5,7},{6,4},{7,5},{8,10},{9,11},{10,... | collective-permute-start | bytes 786440 | tf_op jit(solution)/shard_map/ppermute | solution.py:58
  705.6 19.5 %collective-permute-start.66 = (bf16[64,2048]{1,0:T(8,128)(2,1)S(1)}, bf16[64,2048]{1,0:T(8,128)(2,1)S(1)}, u32[]{:S(2)}, u32[]{:S(2)}) collective-permute-start(bf16[64,2048]{1,0:T(8,128)(2,1)S(1)} %get-tuple-element.203), channel_id=1, source_target_pairs={{0,4},{1,5},{2,6},{3,7},{4,0},{5,1},{6,2},{7,3},{8,12},{9,13},{10,... | collective-permute-start | bytes 786440 | tf_op jit(solution)/shard_map/ppermute | solution.py:58
  706.2 19.0 %collective-permute-start.67 = (bf16[64,2048]{1,0:T(8,128)(2,1)S(1)}, bf16[64,2048]{1,0:T(8,128)(2,1)S(1)}, u32[]{:S(2)}, u32[]{:S(2)}) collective-permute-start(bf16[64,2048]{1,0:T(8,128)(2,1)S(1)} %get-tuple-element.202), channel_id=1, source_target_pairs={{0,6},{1,7},{2,4},{3,5},{4,2},{5,3},{6,0},{7,1},{8,14},{9,15},{10,... | collective-permute-start | bytes 786440 | tf_op jit(solution)/shard_map/ppermute | solution.py:58
  726.4 35.6 %collective-permute-start.68 = (bf16[64,2048]{1,0:T(8,128)(2,1)S(1)}, bf16[64,2048]{1,0:T(8,128)(2,1)}, u32[]{:S(2)}, u32[]{:S(2)}) collective-permute-start(bf16[64,2048]{1,0:T(8,128)(2,1)S(1)} %get-tuple-element.115), channel_id=1, source_target_pairs={{0,2},{1,3},{2,0},{3,1},{4,6},{5,7},{6,4},{7,5},{8,10},{9,11},{10,... | collective-permute-start | bytes 786440 | tf_op jit(solution)/shard_map/ppermute | solution.py:58
  727.8 34.2 %collective-permute-start.69 = (bf16[64,2048]{1,0:T(8,128)(2,1)S(1)}, bf16[64,2048]{1,0:T(8,128)(2,1)}, u32[]{:S(2)}, u32[]{:S(2)}) collective-permute-start(bf16[64,2048]{1,0:T(8,128)(2,1)S(1)} %get-tuple-element.115), channel_id=1, source_target_pairs={{0,4},{1,5},{2,6},{3,7},{4,0},{5,1},{6,2},{7,3},{8,12},{9,13},{10,... | collective-permute-start | bytes 786440 | tf_op jit(solution)/shard_map/ppermute | solution.py:58
  728.3 33.7 %collective-permute-start.70 = (bf16[64,2048]{1,0:T(8,128)(2,1)S(1)}, bf16[64,2048]{1,0:T(8,128)(2,1)}, u32[]{:S(2)}, u32[]{:S(2)}) collective-permute-start(bf16[64,2048]{1,0:T(8,128)(2,1)S(1)} %get-tuple-element.115), channel_id=1, source_target_pairs={{0,6},{1,7},{2,4},{3,5},{4,2},{5,3},{6,0},{7,1},{8,14},{9,15},{10,... | collective-permute-start | bytes 786440 | tf_op jit(solution)/shard_map/ppermute | solution.py:58
  752.6 22.7 %all-to-all-start.6 = ((bf16[8,64,1024]{2,1,0:T(8,128)(2,1)}), bf16[8,64,1024]{2,1,0:T(8,128)(2,1)S(1)}, u32[]{:S(2)}, u32[]{:S(2)}) async-start(bf16[8,64,1024]{2,1,0:T(8,128)(2,1)} %bitcast.141), calls=%async_computation.7 | async-start | bytes 2097152 | tf_op jit(solution)/shard_map/all_to_all | solution.py:82
  756.2 263.1 %all-gather.25.cloned.1.call-start = ((), (), s32[]{:S(2)}) async-start(), calls=%async_computation.23 | async-start | bytes 5324800 | tf_op jit(solution)/shard_map/all_gather | solution.py:812
  764.2 18.8 %collective-permute-start.71 = (bf16[256,2048]{1,0:T(8,128)(2,1)}, bf16[256,2048]{1,0:T(8,128)(2,1)}, u32[]{:S(2)}, u32[]{:S(2)}) collective-permute-start(bf16[256,2048]{1,0:T(8,128)(2,1)} %pad_maximum_fusion.16), channel_id=1, source_target_pairs={{0,1},{1,0},{2,3},{3,2},{4,5},{5,4},{6,7},{7,6},{8,9},{9,8},{10,11... | collective-permute-start | bytes 3145736 | tf_op jit(solution)/shard_map/ppermute | solution.py:58
  837.3 14.1 %collective-permute-start.78 = (bf16[64,2048]{1,0:T(8,128)(2,1)S(1)}, bf16[64,2048]{1,0:T(8,128)(2,1)S(1)}, u32[]{:S(2)}, u32[]{:S(2)}) collective-permute-start(bf16[64,2048]{1,0:T(8,128)(2,1)S(1)} %get-tuple-element.200), channel_id=1, source_target_pairs={{0,4},{1,5},{2,6},{3,7},{4,0},{5,1},{6,2},{7,3},{8,12},{9,13},{10,... | collective-permute-start | bytes 786440 | tf_op jit(solution)/shard_map/ppermute | solution.py:58
  837.3 14.1 %collective-permute-start.79 = (bf16[64,2048]{1,0:T(8,128)(2,1)S(1)}, bf16[64,2048]{1,0:T(8,128)(2,1)S(1)}, u32[]{:S(2)}, u32[]{:S(2)}) collective-permute-start(bf16[64,2048]{1,0:T(8,128)(2,1)S(1)} %get-tuple-element.199), channel_id=1, source_target_pairs={{0,6},{1,7},{2,4},{3,5},{4,2},{5,3},{6,0},{7,1},{8,14},{9,15},{10,... | collective-permute-start | bytes 786440 | tf_op jit(solution)/shard_map/ppermute | solution.py:58
  861.9 76.5 %all-to-all-start.9 = ((bf16[8,256,1536]{2,1,0:T(8,128)(2,1)}), bf16[8,256,1536]{2,1,0:T(8,128)(2,1)}, u32[]{:S(2)}, u32[]{:S(2)}) async-start(bf16[8,256,1536]{2,1,0:T(8,128)(2,1)} %bitcast.899), calls=%async_computation.11 | async-start | bytes 12582912 | tf_op jit(solution)/shard_map/all_to_all | solution.py:82
  866.8 152.6 %reduce-scatter.5.cloned.1.call-start = ((), (), s32[]{:S(2)}) async-start(), calls=%async_computation.21 | async-start | bytes 6881280 | tf_op jit(solution)/shard_map/reduce_scatter | solution.py:86
  903.7 52.9 %collective-permute-start.80 = (f32[24,128]{1,0:T(8,128)S(1)}, f32[24,128]{1,0:T(8,128)S(1)}, u32[]{:S(2)}, u32[]{:S(2)}) collective-permute-start(f32[24,128]{1,0:T(8,128)S(1)} %bitcast.1034), channel_id=1, source_target_pairs={{0,8},{8,0},{16,24},{24,16},{1,9},{9,1},{17,25},{25,17},{2,10},{10... | collective-permute-start | bytes 36872 | tf_op jit(solution)/shard_map/ppermute | solution.py:96
  905.5 51.0 %collective-permute-start.81 = (f32[24,128]{1,0:T(8,128)S(1)}, f32[24,128]{1,0:T(8,128)S(1)}, u32[]{:S(2)}, u32[]{:S(2)}) collective-permute-start(f32[24,128]{1,0:T(8,128)S(1)} %bitcast.1035), channel_id=1, source_target_pairs={{0,16},{8,24},{16,0},{24,8},{1,17},{9,25},{17,1},{25,9},{2,18},{10... | collective-permute-start | bytes 36872 | tf_op jit(solution)/shard_map/ppermute | solution.py:96
  905.5 51.0 %collective-permute-start.82 = (f32[24,128]{1,0:T(8,128)S(1)}, f32[24,128]{1,0:T(8,128)S(1)}, u32[]{:S(2)}, u32[]{:S(2)}) collective-permute-start(f32[24,128]{1,0:T(8,128)S(1)} %bitcast.1036), channel_id=1, source_target_pairs={{0,24},{8,16},{16,8},{24,0},{1,25},{9,17},{17,9},{25,1},{2,26},{10... | collective-permute-start | bytes 36872 | tf_op jit(solution)/shard_map/ppermute | solution.py:96
  938.4 32.2 %all-to-all-start.7 = ((bf16[4,2,16384]{2,1,0:T(2,128)(2,1)}), bf16[4,2,16384]{2,1,0:T(2,128)(2,1)S(1)}, u32[]{:S(2)}, u32[]{:S(2)}) async-start(bf16[4,2,16384]{2,1,0:T(2,128)(2,1)} %reshape.1299), calls=%async_computation.8 | async-start | bytes 524288 | tf_op jit(solution)/shard_map/all_to_all | solution.py:404
  1021.7 18.9 %all-to-all-start.10 = ((bf16[8,64,1024]{2,1,0:T(8,128)(2,1)}), bf16[8,64,1024]{2,1,0:T(8,128)(2,1)S(1)}, u32[]{:S(2)}, u32[]{:S(2)}) async-start(bf16[8,64,1024]{2,1,0:T(8,128)(2,1)} %bitcast.218), calls=%async_computation.12 | async-start | bytes 2097152 | tf_op jit(solution)/shard_map/all_to_all | solution.py:82
  1025.3 121.5 %all-gather.27.cloned.1.call-start = ((), (), s32[]{:S(2)}) async-start(), calls=%async_computation.24 | async-start | bytes 5324800 | tf_op jit(solution)/shard_map/all_gather | solution.py:824
  1056.8 76.8 %all-to-all-start.11 = ((bf16[8,256,1536]{2,1,0:T(8,128)(2,1)}), bf16[8,256,1536]{2,1,0:T(8,128)(2,1)}, u32[]{:S(2)}, u32[]{:S(2)}) async-start(bf16[8,256,1536]{2,1,0:T(8,128)(2,1)} %bitcast.900), calls=%async_computation.13 | async-start | bytes 12582912 | tf_op jit(solution)/shard_map/all_to_all | solution.py:82
  (309 other events, 5744.6 us)
Sparse Core Ops, SparseCore 0:
  33.3 113.0 all-gather.12
  260.1 79.2 all-gather.14
  340.9 120.8 all-gather.16
  464.6 85.3 all-gather.18
  552.8 81.5 all-gather.20
  637.2 97.9 reduce-scatter.2
  738.1 83.6 all-gather.22
  824.0 81.4 all-gather.24
  907.8 100.7 reduce-scatter.4
  1047.1 82.4 all-gather.26

commit v3 on v2

--- a/solution.py
+++ b/solution.py
@@ -386,7 +386,7 @@
             if not shared:
                 return value
             size = value.shape[axis] // planes
-            return lax.dynamic_slice_in_dim(value, size * rank, size, axis)
+            return lax.dynamic_slice_in_dim(value, size * later_rank, size, axis)
 
         gates = cut(jnp.stack([rate_gate[layer], input_gate[layer]]), 2)
         blocks = []
@@ -410,12 +410,16 @@
     top_grad_all = all_rows(grad)
     in_moved = [None] * LAYERS
     mlp_moved = [None] * LAYERS
-    in_moved[0] = spread(after(packed_in(0, False), small_all, stream)[0])
+    first_pack = packed_in(0, False)
+    later_rank = after(rank, first_pack)[0]
+    in_moved[0] = spread(after(first_pack, small_all, stream)[0])
     normed = low(rms_scale(high(stream), high(small_whole(0, 0, strip))))
     first_normed = gather_rows(normed)
     in_width = WIN + own + filler
     first_both = dot(first_normed, in_moved[0].reshape(D, -1)[:, :in_width])
-    mlp_moved[0] = spread(after(columns_apart(mlp_gate, mlp_up, 0, count), first_both)[0])
+    in_share = spread(after(packed_in(1, True), first_both)[0])
+    in_moved[1] = lax.all_gather(in_share, "section", axis=1, tiled=True)
+    mlp_moved[0] = spread(after(columns_apart(mlp_gate, mlp_up, 0, count), in_share)[0])
     def layer_weights(layer):
         in_weight = in_moved[layer].reshape(D, -1)
         blocks = in_weight[:, WIN + own + filler :]
@@ -769,22 +773,20 @@
             weight,
             first_normed if first else None,
             first_both if first else None,
-            [weight["mlp"], top_grad_all] if first else [],
+            [top_grad_all] if first else [],
         )
         if first:
-            in_share = spread(after(packed_in(1, True), kept_rec["mixture"])[0])
-            in_moved[1] = lax.all_gather(in_share, "section", axis=1, tiled=True)
             shares = [
                 lax.dynamic_slice_in_dim(part[1:], thin * rank, thin, 1)
                 for part in (mlp_gate, mlp_up)
             ]
-            share = spread(after(columns_apart(*shares, 0, count), in_share)[0])
+            share = spread(after(columns_apart(*shares, 0, count), mlp_moved[0])[0])
             share = after(share, in_moved[1])[0]
             mlp_moved[1] = lax.all_gather(share, "section", axis=1, tiled=True)
             weights.append(layer_weights(1))
         else:
             everyone[0] = all_rows(after(kept[0][1]["normed"], kept_rec["mixture"])[0])
-        stream, kept_mlp = mlp_forward(stream, weight, [in_share] if first else [])
+        stream, kept_mlp = mlp_forward(stream, weight, [share] if first else [])
         if first:
             weights[1]["mlp"] = mlp_moved[1].reshape(D, 2 * wide)
         else:
@@ -809,24 +811,24 @@
     grad_in = grad
     grad_mid, mlp_terms = mlp_backward(grad_in, weights[0], kept[0][1])
     pieces1 = rec_pieces(after(flat, grad_mid)[0])
-    rec_flat[1] = lax.all_gather(pieces1, "section", axis=0, tiled=False)
     grad_all = all_rows(grad_in)
-    grad, terms = rec_backward(grad_mid, weights[0], kept[0][0], [pieces1, ins1])
+    grad, terms = rec_backward(grad_mid, weights[0], kept[0][0], [pieces1])
     input_grad = by_features(grad)
     flat = rec_shares(terms)
     grad_all = after(grad_all, flat)[0]
     flat = section_sum(flat)
+    rec_flat[1] = lax.all_gather(after(pieces1, flat)[0], "section", axis=0, tiled=False)
     smalls[0] = small_gradients({**mlp_terms, **terms})
     ins0, mlp_downs[0] = mlp_gradients(everyone[0], grad_all, weights[0])
     joined = [joined_rows(mlp_rows[1], which, 1, LAYERS, None) for which in range(2)]
-    flat = after(flat, ins0, rec_flat[1], input_grad, *smalls[0], *joined, *mlp_downs)[0]
+    flat = after(flat, ins0, mlp_rows[1])[0]
     pieces0 = rec_pieces(flat)
     rec_flat[0] = lax.all_gather(pieces0, "section", axis=0, tiled=False)
     mlp_rows[0] = to_rows(after(ins0, pieces0)[0])
     mlp_results = tuple(
         joined_rows(mlp_rows[0], which, 0, LAYERS, joined[which]) for which in range(2)
     ) + (jnp.stack(mlp_downs),)
-    rec_flat[0] = after(rec_flat[0], *mlp_results)[0]
+    rec_flat[0] = after(rec_flat[0], *mlp_results, input_grad, *smalls[0])[0]
     results = []
     for layer in range(LAYERS):
         channels, norms = smalls[layer]

time: 1200 us -> 1150 us (0.958)
  waiting for transfers between devices: 413 us -> 360 us
  blocking collectives: 48.5 us -> 30 us
    all_to_all x9 -> x10, waiting for transfers between devices: 132 us -> 77.2 us  [spread(): return lax.all_to_all(pack, 'dp', 0, 0, tiled=False)]
    all_gather x1, waiting for transfers between devices: 24.4 us -> 0.01 us  [local(): in_moved[1] = lax.all_gather(in_share, 'section', axis=1, tiled=True)]
    ppermute x64, waiting for transfers between devices: 198 us -> 218 us  [swapped(): return lax.ppermute(value, 'dp', [(at, at ^ offset) for at in range(count)])]
    all_to_all x1 -> x0, blocking collectives: 18.5 us -> none  [spread(): return lax.all_to_all(pack, 'dp', 0, 0, tiled=False)]
    all_to_all x2, waiting for transfers between devices: 0.41 us -> 18.8 us  [by_features(): lax.all_to_all(moved, 'section', split_axis=2, concat_axis=1, tiled=True)]
    all_to_all x9 -> x10, starting transfers between devices: 36.9 us -> 40.9 us  [spread(): return lax.all_to_all(pack, 'dp', 0, 0, tiled=False)]
    unnamed x552 -> x512, local copies, waits for them, and re-layouts: 60.1 us -> 56.7 us
  transfers between devices with their start and end apart: 107 -> 108, of which waited for: 56 -> 59; matrix products, arithmetic and copies ran while one was open for 39% -> 43% of each run, Pallas kernels for 3% -> 3%
where the time goes in v3:
time: 1150 us; the launch traced here: 1140 us
  waiting for transfers between devices  360 us (31%)
  matrix products  241 us (21%)
  local copies, waits for them, and re-layouts  198 us (17%)
  starting transfers between devices  142 us (12%)
  other arithmetic  111 us (10%)
  Pallas kernels  37.9 us (3%)
  blocking collectives  30 us (3%)
  between operations  19.1 us (2%)
    ppermute x64, waiting for transfers between devices, swapped(): return lax.ppermute(value, 'dp', [(at, at ^ offset) for at in range(count)])  218 us
    dot_general x16, matrix products, dot_nt(): lax.dot_general(left, right, (((1,), (1,)), ((), ())), preferred_element_...  83.9 us
    dot_general x10, matrix products, dot_tn(): lax.dot_general(left, right, (((0,), (0,)), ((), ())), preferred_element_...  81.4 us
    all_to_all x10, waiting for transfers between devices, spread(): return lax.all_to_all(pack, 'dp', 0, 0, tiled=False)  77.2 us
    dot_general x16, matrix products, dot(): return jnp.dot(left, right, preferred_element_type=jnp.float32)  75.1 us
    ppermute x64, starting transfers between devices, swapped(): return lax.ppermute(value, 'dp', [(at, at ^ offset) for at in range(count)])  59.3 us
    unnamed x512, local copies, waits for them, and re-layouts  56.7 us
    all_to_all x10, starting transfers between devices, spread(): return lax.all_to_all(pack, 'dp', 0, 0, tiled=False)  40.9 us
  transfers between devices with their start and end apart: 108, of which 59 were waited for; matrix products, arithmetic and copies ran while one was open for 43% of the time, Pallas kernels for 3%

profile of v3, /device:TPU:0, one launch (start us, length us, event | category | flops | bytes accessed | tf_op | source)
XLA Modules:
  0.0 1138.8 jit_solution(11338425520754716052)
XLA Ops:
  10.3 20.7 %all_to_all.109 = bf16[4,128,512]{2,0,1:T(4,128)(2,1)S(1)} all-to-all(bf16[4,128,512]{2,0,1:T(4,128)(2,1)S(1)} %pad_maximum_fusion.25), channel_id=1, replica_groups=mesh['section'=4,'dp'=8] {'section'}, dimensions={1} | all-to-all | bytes 1048576 | tf_op jit(solution)/shard_map/all_to_all | solution.py:406
  34.5 9.3 all-gather.3
  79.2 61.1 %collective-permute-done.2 = bf16[64,2048]{1,0:T(8,128)(2,1)S(1)} collective-permute-done((bf16[64,2048]{1,0:T(8,128)(2,1)S(1)}, bf16[64,2048]{1,0:T(8,128)(2,1)S(1)}, u32[]{:S(2)}, u32[]{:S(2)}) %collective-permute-start.2) | collective-permute-done | bytes 262176 | tf_op jit(solution)/shard_map/ppermute | solution.py:58
  166.8 6.2 fusion.46
  186.2 5.7 all-to-all-done.2
  232.8 37.0 %all-to-all-done.3 = bf16[8,256,1536]{2,1,0:T(8,128)(2,1)} async-done(((bf16[8,256,1536]{2,1,0:T(8,128)(2,1)}), bf16[8,256,1536]{2,1,0:T(8,128)(2,1)}, u32[]{:S(2)}, u32[]{:S(2)}) %all-to-all-start.3) | async-done | bytes 6291488 | tf_op jit(solution)/shard_map/all_to_all | solution.py:82
  274.4 6.6 collective-permute-done.11
  286.7 16.9 %collective-permute-done.14 = bf16[64,2048]{1,0:T(8,128)(2,1)S(1)} collective-permute-done((bf16[64,2048]{1,0:T(8,128)(2,1)S(1)}, bf16[64,2048]{1,0:T(8,128)(2,1)S(1)}, u32[]{:S(2)}, u32[]{:S(2)}) %collective-permute-start.14) | collective-permute-done | bytes 262176 | tf_op jit(solution)/shard_map/ppermute | solution.py:58
  303.6 5.0 collective-permute-done.13
  315.9 6.8 fusion.430
  331.8 5.6 collective-permute-done.17
  337.3 5.4 collective-permute-done.19
  350.3 5.1 collective-permute-done.22
  367.1 10.3 collective-permute-done.24
  423.8 5.5 collective-permute-done.31
  440.6 6.2 collective-permute-done.33
  451.8 6.8 fusion.431
  458.6 5.1 fusion.85
  480.5 6.9 collective-permute-done.47
  491.1 7.3 collective-permute-done.37
  498.4 11.0 collective-permute-done.39
  510.4 12.0 %all-gather.19.cloned.1.call-done = bf16[2048,2048]{1,0:T(8,128)(2,1)} async-done(((bf16[64,2048]{1,0:T(8,128)(2,1)}), bf16[2048,2048]{1,0:T(8,128)(2,1)}) %all-gather.19.cloned.1.call-update) | async-done | bytes 8388624 | tf_op jit(solution)/shard_map/all_gather | solution.py:90
  529.8 7.3 all-to-all-start.5
  545.8 4.8 all-to-all-done.5
  591.8 4.9 collective-permute-done.55
  618.2 5.7 collective-permute-done.57
  623.9 6.0 collective-permute-done.59
  635.4 6.4 collective-permute-done.62
  652.1 5.6 convolution_convert_fusion.6
  668.8 19.2 %fusion.432 = f32[2048,1536]{0,1:T(8,128)} fusion(bf16[2048,2048]{1,0:T(8,128)(2,1)} %all-gather.19.cloned.1.call-done, bf16[2048,1536]{1,0:T(8,128)(2,1)} %bitcast.56), kind=kOutput, calls=%fused_computation.922 | convolution fusion | flops 12884901888 | bytes 27262976 | tf_op jit(solution)/shard_map/dot_general | solution.py:33
  704.6 19.0 %fusion.433 = f32[2048,1536]{0,1:T(8,128)} fusion(bf16[2048,2048]{1,0:T(8,128)(2,1)} %all-gather.21.cloned.1.call-done, bf16[2048,1536]{1,0:T(8,128)(2,1)} %bitcast.894), kind=kOutput, calls=%fused_computation.923 | convolution fusion | flops 12884901888 | bytes 27262976 | tf_op jit(solution)/shard_map/dot_general | solution.py:33
  740.7 6.6 all-to-all-done.6
  803.4 17.7 %fusion.13 = (bf16[2048,768]{0,1:T(8,128)(2,1)S(1)}, bf16[2048,768]{0,1:T(8,128)(2,1)S(1)}) fusion(f32[2048,1536]{0,1:T(8,128)} %fusion.433, bf16[2048,2048]{1,0:T(8,128)(2,1)} %all-gather.13.cloned.1.call-done, bf16[2,768,2048]{2,1,0:T(8,128)(2,1)} %param.36), kind=kOutput, calls=%fused_computation.20 | convolution fusion | flops 6480199680 | bytes 30408704 | tf_op jit(solution)/shard_map/dot_general | solution.py:37
  821.1 17.5 %convolution_convert_fusion = bf16[2048,1536]{1,0:T(8,128)(2,1)} fusion(bf16[2048,2048]{1,0:T(8,128)(2,1)} %all-gather.21.cloned.1.call-done, bf16[2048,768]{0,1:T(8,128)(2,1)S(1)} %get-tuple-element.148, bf16[2048,768]{0,1:T(8,128)(2,1)S(1)} %get-tuple-element.147), kind=kOutput, calls=%fused_computation.5 | convolution fusion | flops 12900630528 | bytes 20971520 | tf_op jit(solution)/shard_map/dot_general | solution.py:43
  859.2 4.9 all-to-all-start.8
  876.5 20.0 %fusion.6 = (bf16[2048,768]{0,1:T(8,128)(2,1)}, bf16[2048,768]{0,1:T(8,128)(2,1)}) fusion(f32[2048,1536]{0,1:T(8,128)} %fusion.432, bf16[2048,2048]{1,0:T(8,128)(2,1)} %all-gather.23.cloned.1.call-done, bf16[2,768,2048]{2,1,0:T(8,128)(2,1)} %param.36), kind=kOutput, calls=%fused_computation.13 | convolution fusion | flops 6480199680 | bytes 30408704 | tf_op jit(solution)/shard_map/dot_general | solution.py:37
  899.3 19.2 %convolution_convert_fusion.1 = bf16[2048,1536]{1,0:T(8,128)(2,1)} fusion(bf16[2048,2048]{1,0:T(8,128)(2,1)} %all-gather.19.cloned.1.call-done, bf16[2048,768]{0,1:T(8,128)(2,1)} %get-tuple-element.150, bf16[2048,768]{0,1:T(8,128)(2,1)} %get-tuple-element.149), kind=kOutput, calls=%fused_computation.6 | convolution fusion | flops 12900630528 | bytes 20971520 | tf_op jit(solution)/shard_map/dot_general | solution.py:43
  918.5 20.7 %all-to-all-done.8.part_ref = bf16[8,256,1536]{2,1,0:T(8,128)(2,1)} async-done(((bf16[8,256,1536]{2,1,0:T(8,128)(2,1)}), bf16[8,256,1536]{2,1,0:T(8,128)(2,1)}, u32[]{:S(2)}, u32[]{:S(2)}) %all-to-all-start.8) | async-done | bytes 6291488 | tf_op jit(solution)/shard_map/all_to_all | solution.py:82
  952.1 7.2 all-to-all-done.9
  981.5 14.0 %all-to-all-done.7 = bf16[4,2,16384]{2,1,0:T(2,128)(2,1)S(1)} async-done(((bf16[4,2,16384]{2,1,0:T(2,128)(2,1)}), bf16[4,2,16384]{2,1,0:T(2,128)(2,1)S(1)}, u32[]{:S(2)}, u32[]{:S(2)}) %all-to-all-start.7) | async-done | bytes 262176 | tf_op jit(solution)/shard_map/all_to_all | solution.py:404
  995.5 4.8 all-to-all-start.10
  1000.4 14.7 %convolution_bitcast_fusion = f32[1,768,2048]{2,1,0:T(8,128)} fusion(bf16[2048,2048]{1,0:T(8,128)(2,1)} %all-gather.13.cloned.1.call-done, f32[2048,1536]{0,1:T(8,128)} %fusion.433), kind=kOutput, calls=%fused_computation.35 | convolution fusion | flops 6458179584 | bytes 27262976 | tf_op jit(solution)/shard_map/dot_general | solution.py:43
  1015.1 6.6 shard_map.328.kept_ref
  1021.7 6.6 shard_map.326.kept_ref
  1047.9 14.7 %convolution_bitcast_fusion.1 = f32[1,768,2048]{2,1,0:T(8,128)} fusion(bf16[2048,2048]{1,0:T(8,128)(2,1)} %all-gather.23.cloned.1.call-done, f32[2048,1536]{0,1:T(8,128)} %fusion.432), kind=kOutput, calls=%fused_computation.36 | convolution fusion | flops 6458179584 | bytes 27262976 | tf_op jit(solution)/shard_map/dot_general | solution.py:43
  1062.6 9.2 pad_maximum_fusion
  1088.1 6.6 shard_map.329
  1094.7 6.6 shard_map.327
  (1186 shorter events, 580.9 us)
Async XLA Ops:
  7.2 209.8 %all-gather.13.cloned.1.call-start = ((), (), s32[]{:S(2)}) async-start(), calls=%async_computation.15 | async-start | bytes 8650752 | tf_op jit(solution)/shard_map/all_gather | solution.py:90
  65.7 101.1 %all-to-all-start.1 = ((bf16[8,256,1024]{2,1,0:T(8,128)(2,1)}), bf16[8,256,1024]{2,1,0:T(8,128)(2,1)}, u32[]{:S(2)}, u32[]{:S(2)}) async-start(bf16[8,256,1024]{2,1,0:T(8,128)(2,1)} %copy-done.1), calls=%async_computation.1 | async-start | bytes 8388608 | tf_op jit(solution)/shard_map/all_to_all | solution.py:82
  75.0 65.4 %collective-permute-start.2 = (bf16[64,2048]{1,0:T(8,128)(2,1)S(1)}, bf16[64,2048]{1,0:T(8,128)(2,1)S(1)}, u32[]{:S(2)}, u32[]{:S(2)}) collective-permute-start(bf16[64,2048]{1,0:T(8,128)(2,1)S(1)} %get-tuple-element.146), channel_id=1, source_target_pairs={{0,6},{1,7},{2,4},{3,5},{4,2},{5,3},{6,0},{7,1},{8,14},{9,15},{10,... | collective-permute-start | bytes 786440 | tf_op jit(solution)/shard_map/ppermute | solution.py:58
  77.8 66.7 %collective-permute-start.1 = (bf16[64,2048]{1,0:T(8,128)(2,1)S(1)}, bf16[64,2048]{1,0:T(8,128)(2,1)S(1)}, u32[]{:S(2)}, u32[]{:S(2)}) collective-permute-start(bf16[64,2048]{1,0:T(8,128)(2,1)S(1)} %get-tuple-element.146), channel_id=1, source_target_pairs={{0,4},{1,5},{2,6},{3,7},{4,0},{5,1},{6,2},{7,3},{8,12},{9,13},{10,... | collective-permute-start | bytes 786440 | tf_op jit(solution)/shard_map/ppermute | solution.py:58
  78.3 66.2 %collective-permute-start = (bf16[64,2048]{1,0:T(8,128)(2,1)S(1)}, bf16[64,2048]{1,0:T(8,128)(2,1)S(1)}, u32[]{:S(2)}, u32[]{:S(2)}) collective-permute-start(bf16[64,2048]{1,0:T(8,128)(2,1)S(1)} %get-tuple-element.146), channel_id=1, source_target_pairs={{0,2},{1,3},{2,0},{3,1},{4,6},{5,7},{6,4},{7,5},{8,10},{9,11},{10,... | collective-permute-start | bytes 786440 | tf_op jit(solution)/shard_map/ppermute | solution.py:58
  144.7 19.9 %collective-permute-start.3 = (bf16[256,2048]{1,0:T(8,128)(2,1)S(1)}, bf16[256,2048]{1,0:T(8,128)(2,1)}, u32[]{:S(2)}, u32[]{:S(2)}) collective-permute-start(bf16[256,2048]{1,0:T(8,128)(2,1)S(1)} %pad_maximum_fusion.9), channel_id=1, source_target_pairs={{0,1},{1,0},{2,3},{3,2},{4,5},{5,4},{6,7},{7,6},{8,9},{9,8},{10,11... | collective-permute-start | bytes 3145736 | tf_op jit(solution)/shard_map/ppermute | solution.py:58
  173.1 18.9 %all-to-all-start.2 = ((bf16[8,64,1024]{2,1,0:T(8,128)(2,1)}), bf16[8,64,1024]{2,1,0:T(8,128)(2,1)S(1)}, u32[]{:S(2)}, u32[]{:S(2)}) async-start(bf16[8,64,1024]{2,1,0:T(8,128)(2,1)} %shard_map.318), calls=%async_computation.2 | async-start | bytes 2097152 | tf_op jit(solution)/shard_map/all_to_all | solution.py:82
  182.8 17.8 %collective-permute-start.4 = (f32[16,3,512]{2,1,0:T(4,128)S(1)}, f32[16,3,512]{2,1,0:T(4,128)S(1)}, u32[]{:S(2)}, u32[]{:S(2)}) collective-permute-start(f32[16,3,512]{2,1,0:T(4,128)S(1)} %slice.1505), channel_id=1, source_target_pairs={{0,8},{8,16},{16,24},{24,0},{1,9},{9,17},{17,25},{25,1},{2,10},{10... | collective-permute-start | bytes 294920 | tf_op jit(solution)/shard_map/ppermute | solution.py:499
  193.0 76.9 %all-to-all-start.3 = ((bf16[8,256,1536]{2,1,0:T(8,128)(2,1)}), bf16[8,256,1536]{2,1,0:T(8,128)(2,1)}, u32[]{:S(2)}, u32[]{:S(2)}) async-start(bf16[8,256,1536]{2,1,0:T(8,128)(2,1)} %copy-done), calls=%async_computation.3 | async-start | bytes 12582912 | tf_op jit(solution)/shard_map/all_to_all | solution.py:82
  197.8 111.9 %all-gather.15.cloned.1.call-start = ((), (), s32[]{:S(2)}) async-start(), calls=%async_computation.16 | async-start | bytes 5242880 | tf_op jit(solution)/shard_map/all_gather | solution.py:421
  226.2 48.2 %collective-permute-start.9 = (bf16[64,2048]{1,0:T(8,128)(2,1)}, bf16[64,2048]{1,0:T(8,128)(2,1)S(1)}, u32[]{:S(2)}, u32[]{:S(2)}) collective-permute-start(bf16[64,2048]{1,0:T(8,128)(2,1)} %get-tuple-element.223), channel_id=1, source_target_pairs={{0,2},{1,3},{2,0},{3,1},{4,6},{5,7},{6,4},{7,5},{8,10},{9,11},{10,... | collective-permute-start | bytes 786440 | tf_op jit(solution)/shard_map/ppermute | solution.py:58
  228.3 52.7 %collective-permute-start.11 = (bf16[64,2048]{1,0:T(8,128)(2,1)S(1)}, bf16[64,2048]{1,0:T(8,128)(2,1)S(1)}, u32[]{:S(2)}, u32[]{:S(2)}) collective-permute-start(bf16[64,2048]{1,0:T(8,128)(2,1)S(1)} %get-tuple-element.224), channel_id=1, source_target_pairs={{0,6},{1,7},{2,4},{3,5},{4,2},{5,3},{6,0},{7,1},{8,14},{9,15},{10,... | collective-permute-start | bytes 786440 | tf_op jit(solution)/shard_map/ppermute | solution.py:58
  229.7 51.3 %collective-permute-start.10 = (bf16[64,2048]{1,0:T(8,128)(2,1)S(1)}, bf16[64,2048]{1,0:T(8,128)(2,1)S(1)}, u32[]{:S(2)}, u32[]{:S(2)}) collective-permute-start(bf16[64,2048]{1,0:T(8,128)(2,1)S(1)} %get-tuple-element.225), channel_id=1, source_target_pairs={{0,4},{1,5},{2,6},{3,7},{4,0},{5,1},{6,2},{7,3},{8,12},{9,13},{10,... | collective-permute-start | bytes 786440 | tf_op jit(solution)/shard_map/ppermute | solution.py:58
  269.8 39.9 %all-to-all-start.4 = ((bf16[8,64,1536]{2,1,0:T(8,128)(2,1)}), bf16[8,64,1536]{2,1,0:T(8,128)(2,1)S(1)}, u32[]{:S(2)}, u32[]{:S(2)}) async-start(bf16[8,64,1536]{2,1,0:T(8,128)(2,1)} %shard_map.319), calls=%async_computation.4 | async-start | bytes 3145728 | tf_op jit(solution)/shard_map/all_to_all | solution.py:82
  273.4 178.4 %all-gather.17.cloned.1.call-start = ((), (), s32[]{:S(2)}) async-start(), calls=%async_computation.17 | async-start | bytes 7864320 | tf_op jit(solution)/shard_map/all_gather | solution.py:785
  283.2 20.3 %collective-permute-start.14 = (bf16[64,2048]{1,0:T(8,128)(2,1)S(1)}, bf16[64,2048]{1,0:T(8,128)(2,1)S(1)}, u32[]{:S(2)}, u32[]{:S(2)}) collective-permute-start(bf16[64,2048]{1,0:T(8,128)(2,1)S(1)} %get-tuple-element.60), channel_id=1, source_target_pairs={{0,6},{1,7},{2,4},{3,5},{4,2},{5,3},{6,0},{7,1},{8,14},{9,15},{10,... | collective-permute-start | bytes 786440 | tf_op jit(solution)/shard_map/ppermute | solution.py:58
  283.3 25.2 %collective-permute-start.13 = (bf16[64,2048]{1,0:T(8,128)(2,1)S(1)}, bf16[64,2048]{1,0:T(8,128)(2,1)S(1)}, u32[]{:S(2)}, u32[]{:S(2)}) collective-permute-start(bf16[64,2048]{1,0:T(8,128)(2,1)S(1)} %get-tuple-element.60), channel_id=1, source_target_pairs={{0,4},{1,5},{2,6},{3,7},{4,0},{5,1},{6,2},{7,3},{8,12},{9,13},{10,... | collective-permute-start | bytes 786440 | tf_op jit(solution)/shard_map/ppermute | solution.py:58
  285.3 23.3 %collective-permute-start.12 = (bf16[64,2048]{1,0:T(8,128)(2,1)S(1)}, bf16[64,2048]{1,0:T(8,128)(2,1)S(1)}, u32[]{:S(2)}, u32[]{:S(2)}) collective-permute-start(bf16[64,2048]{1,0:T(8,128)(2,1)S(1)} %get-tuple-element.60), channel_id=1, source_target_pairs={{0,2},{1,3},{2,0},{3,1},{4,6},{5,7},{6,4},{7,5},{8,10},{9,11},{10,... | collective-permute-start | bytes 786440 | tf_op jit(solution)/shard_map/ppermute | solution.py:58
  310.9 211.4 %all-gather.19.cloned.1.call-start = ((), (), s32[]{:S(2)}) async-start(), calls=%async_computation.18 | async-start | bytes 8650752 | tf_op jit(solution)/shard_map/all_gather | solution.py:90
  400.4 231.5 %all-gather.21.cloned.1.call-start = ((), (), s32[]{:S(2)}) async-start(), calls=%async_computation.19 | async-start | bytes 8650752 | tf_op jit(solution)/shard_map/all_gather | solution.py:90
  409.1 20.3 %collective-permute-start.31 = (bf16[64,2048]{1,0:T(8,128)(2,1)S(1)}, bf16[64,2048]{1,0:T(8,128)(2,1)S(1)}, u32[]{:S(2)}, u32[]{:S(2)}) collective-permute-start(bf16[64,2048]{1,0:T(8,128)(2,1)S(1)} %get-tuple-element.218), channel_id=1, source_target_pairs={{0,6},{1,7},{2,4},{3,5},{4,2},{5,3},{6,0},{7,1},{8,14},{9,15},{10,... | collective-permute-start | bytes 786440 | tf_op jit(solution)/shard_map/ppermute | solution.py:58
  412.9 16.4 %collective-permute-start.30 = (bf16[64,2048]{1,0:T(8,128)(2,1)S(1)}, bf16[64,2048]{1,0:T(8,128)(2,1)S(1)}, u32[]{:S(2)}, u32[]{:S(2)}) collective-permute-start(bf16[64,2048]{1,0:T(8,128)(2,1)S(1)} %get-tuple-element.219), channel_id=1, source_target_pairs={{0,4},{1,5},{2,6},{3,7},{4,0},{5,1},{6,2},{7,3},{8,12},{9,13},{10,... | collective-permute-start | bytes 786440 | tf_op jit(solution)/shard_map/ppermute | solution.py:58
  419.3 27.9 %collective-permute-start.43 = (bf16[256,2048]{1,0:T(8,128)(2,1)}, bf16[256,2048]{1,0:T(8,128)(2,1)}, u32[]{:S(2)}, u32[]{:S(2)}) collective-permute-start(bf16[256,2048]{1,0:T(8,128)(2,1)} %pad_maximum_fusion.13), channel_id=1, source_target_pairs={{0,1},{1,0},{2,3},{3,2},{4,5},{5,4},{6,7},{7,6},{8,9},{9,8},{10,11... | collective-permute-start | bytes 3145736 | tf_op jit(solution)/shard_map/ppermute | solution.py:58
  471.1 16.3 %collective-permute-start.47 = (bf16[64,2048]{1,0:T(8,128)(2,1)S(1)}, bf16[64,2048]{1,0:T(8,128)(2,1)S(1)}, u32[]{:S(2)}, u32[]{:S(2)}) collective-permute-start(bf16[64,2048]{1,0:T(8,128)(2,1)S(1)} %get-tuple-element.212), channel_id=1, source_target_pairs={{0,6},{1,7},{2,4},{3,5},{4,2},{5,3},{6,0},{7,1},{8,14},{9,15},{10,... | collective-permute-start | bytes 786440 | tf_op jit(solution)/shard_map/ppermute | solution.py:58
  472.9 17.2 %collective-permute-start.46 = (bf16[64,2048]{1,0:T(8,128)(2,1)S(1)}, bf16[64,2048]{1,0:T(8,128)(2,1)S(1)}, u32[]{:S(2)}, u32[]{:S(2)}) collective-permute-start(bf16[64,2048]{1,0:T(8,128)(2,1)S(1)} %get-tuple-element.213), channel_id=1, source_target_pairs={{0,4},{1,5},{2,6},{3,7},{4,0},{5,1},{6,2},{7,3},{8,12},{9,13},{10,... | collective-permute-start | bytes 786440 | tf_op jit(solution)/shard_map/ppermute | solution.py:58
  474.8 23.6 %collective-permute-start.37 = (bf16[64,2048]{1,0:T(8,128)(2,1)S(1)}, bf16[64,2048]{1,0:T(8,128)(2,1)S(1)}, u32[]{:S(2)}, u32[]{:S(2)}) collective-permute-start(bf16[64,2048]{1,0:T(8,128)(2,1)S(1)} %get-tuple-element.214), channel_id=1, source_target_pairs={{0,2},{1,3},{2,0},{3,1},{4,6},{5,7},{6,4},{7,5},{8,10},{9,11},{10,... | collective-permute-start | bytes 786440 | tf_op jit(solution)/shard_map/ppermute | solution.py:58
  475.8 33.6 %collective-permute-start.39 = (bf16[64,2048]{1,0:T(8,128)(2,1)S(1)}, bf16[64,2048]{1,0:T(8,128)(2,1)S(1)}, u32[]{:S(2)}, u32[]{:S(2)}) collective-permute-start(bf16[64,2048]{1,0:T(8,128)(2,1)S(1)} %get-tuple-element.215), channel_id=1, source_target_pairs={{0,6},{1,7},{2,4},{3,5},{4,2},{5,3},{6,0},{7,1},{8,14},{9,15},{10,... | collective-permute-start | bytes 786440 | tf_op jit(solution)/shard_map/ppermute | solution.py:58
  479.4 29.9 %collective-permute-start.38 = (bf16[64,2048]{1,0:T(8,128)(2,1)S(1)}, bf16[64,2048]{1,0:T(8,128)(2,1)S(1)}, u32[]{:S(2)}, u32[]{:S(2)}) collective-permute-start(bf16[64,2048]{1,0:T(8,128)(2,1)S(1)} %get-tuple-element.216), channel_id=1, source_target_pairs={{0,4},{1,5},{2,6},{3,7},{4,0},{5,1},{6,2},{7,3},{8,12},{9,13},{10,... | collective-permute-start | bytes 786440 | tf_op jit(solution)/shard_map/ppermute | solution.py:58
  529.8 20.7 %all-to-all-start.5 = ((bf16[4,2,16384]{2,1,0:T(2,128)(2,1)}), bf16[4,2,16384]{2,1,0:T(2,128)(2,1)S(1)}, u32[]{:S(2)}, u32[]{:S(2)}) async-start(bf16[4,2,16384]{2,1,0:T(2,128)(2,1)} %reshape.1297), calls=%async_computation.5 | async-start | bytes 524288 | tf_op jit(solution)/shard_map/all_to_all | solution.py:404
  537.1 186.6 %reduce-scatter.3.cloned.1.call-start = ((), (), s32[]{:S(2)}) async-start(), calls=%async_computation.20 | async-start | bytes 6881280 | tf_op jit(solution)/shard_map/reduce_scatter | solution.py:86
  539.6 16.7 %collective-permute-start.51 = (bf16[256,2048]{1,0:T(8,128)(2,1)}, bf16[256,2048]{1,0:T(8,128)(2,1)}, u32[]{:S(2)}, u32[]{:S(2)}) collective-permute-start(bf16[256,2048]{1,0:T(8,128)(2,1)} %pad_maximum_fusion.14), channel_id=1, source_target_pairs={{0,1},{1,0},{2,3},{3,2},{4,5},{5,4},{6,7},{7,6},{8,9},{9,8},{10,11... | collective-permute-start | bytes 3145736 | tf_op jit(solution)/shard_map/ppermute | solution.py:58
  606.3 270.2 %all-gather.23.cloned.1.call-start = ((), (), s32[]{:S(2)}) async-start(), calls=%async_computation.22 | async-start | bytes 8650752 | tf_op jit(solution)/shard_map/all_gather | solution.py:90
  665.3 22.9 %collective-permute-start.65 = (bf16[64,2048]{1,0:T(8,128)(2,1)S(1)}, bf16[64,2048]{1,0:T(8,128)(2,1)S(1)}, u32[]{:S(2)}, u32[]{:S(2)}) collective-permute-start(bf16[64,2048]{1,0:T(8,128)(2,1)S(1)} %get-tuple-element.205), channel_id=1, source_target_pairs={{0,2},{1,3},{2,0},{3,1},{4,6},{5,7},{6,4},{7,5},{8,10},{9,11},{10,... | collective-permute-start | bytes 786440 | tf_op jit(solution)/shard_map/ppermute | solution.py:58
  665.9 22.3 %collective-permute-start.67 = (bf16[64,2048]{1,0:T(8,128)(2,1)S(1)}, bf16[64,2048]{1,0:T(8,128)(2,1)S(1)}, u32[]{:S(2)}, u32[]{:S(2)}) collective-permute-start(bf16[64,2048]{1,0:T(8,128)(2,1)S(1)} %get-tuple-element.206), channel_id=1, source_target_pairs={{0,6},{1,7},{2,4},{3,5},{4,2},{5,3},{6,0},{7,1},{8,14},{9,15},{10,... | collective-permute-start | bytes 786440 | tf_op jit(solution)/shard_map/ppermute | solution.py:58
  667.4 20.8 %collective-permute-start.66 = (bf16[64,2048]{1,0:T(8,128)(2,1)S(1)}, bf16[64,2048]{1,0:T(8,128)(2,1)S(1)}, u32[]{:S(2)}, u32[]{:S(2)}) collective-permute-start(bf16[64,2048]{1,0:T(8,128)(2,1)S(1)} %get-tuple-element.207), channel_id=1, source_target_pairs={{0,4},{1,5},{2,6},{3,7},{4,0},{5,1},{6,2},{7,3},{8,12},{9,13},{10,... | collective-permute-start | bytes 786440 | tf_op jit(solution)/shard_map/ppermute | solution.py:58
  704.5 27.0 %collective-permute-start.71 = (bf16[256,2048]{1,0:T(8,128)(2,1)}, bf16[256,2048]{1,0:T(8,128)(2,1)}, u32[]{:S(2)}, u32[]{:S(2)}) collective-permute-start(bf16[256,2048]{1,0:T(8,128)(2,1)} %pad_maximum_fusion.16), channel_id=1, source_target_pairs={{0,1},{1,0},{2,3},{3,2},{4,5},{5,4},{6,7},{7,6},{8,9},{9,8},{10,11... | collective-permute-start | bytes 3145736 | tf_op jit(solution)/shard_map/ppermute | solution.py:58
  726.7 20.6 %all-to-all-start.6 = ((bf16[8,64,1024]{2,1,0:T(8,128)(2,1)}), bf16[8,64,1024]{2,1,0:T(8,128)(2,1)S(1)}, u32[]{:S(2)}, u32[]{:S(2)}) async-start(bf16[8,64,1024]{2,1,0:T(8,128)(2,1)} %bitcast.141), calls=%async_computation.7 | async-start | bytes 2097152 | tf_op jit(solution)/shard_map/all_to_all | solution.py:82
  730.4 168.8 %reduce-scatter.5.cloned.1.call-start = ((), (), s32[]{:S(2)}) async-start(), calls=%async_computation.21 | async-start | bytes 6881280 | tf_op jit(solution)/shard_map/reduce_scatter | solution.py:86
  759.8 15.8 %collective-permute-start.74 = (f32[2,8,2,320]{3,2,1,0:T(2,128)S(1)}, f32[2,8,2,320]{3,2,1,0:T(2,128)S(1)}, u32[]{:S(2)}, u32[]{:S(2)}) collective-permute-start(f32[2,8,2,320]{3,2,1,0:T(2,128)S(1)} %reshape.1228), channel_id=1, source_target_pairs={{0,24},{8,16},{16,8},{24,0},{1,25},{9,17},{17,9},{25,1},{2,26},{10... | collective-permute-start | bytes 122888 | tf_op jit(solution)/shard_map/ppermute | solution.py:96
  859.2 80.0 %all-to-all-start.8 = ((bf16[8,256,1536]{2,1,0:T(8,128)(2,1)}), bf16[8,256,1536]{2,1,0:T(8,128)(2,1)}, u32[]{:S(2)}, u32[]{:S(2)}) async-start(bf16[8,256,1536]{2,1,0:T(8,128)(2,1)} %bitcast.898), calls=%async_computation.10 | async-start | bytes 12582912 | tf_op jit(solution)/shard_map/all_to_all | solution.py:82
  864.1 207.8 %all-gather.27.cloned.1.call-start = ((), (), s32[]{:S(2)}) async-start(), calls=%async_computation.24 | async-start | bytes 5324800 | tf_op jit(solution)/shard_map/all_gather | solution.py:820
  864.8 163.5 %collective-permute-start.85 = (f32[24,128]{1,0:T(8,128)}, f32[24,128]{1,0:T(8,128)}, u32[]{:S(2)}, u32[]{:S(2)}) collective-permute-start(f32[24,128]{1,0:T(8,128)} %bitcast.282), channel_id=1, source_target_pairs={{0,24},{8,16},{16,8},{24,0},{1,25},{9,17},{17,9},{25,1},{2,26},{10... | collective-permute-start | bytes 36872 | tf_op jit(solution)/shard_map/ppermute | solution.py:96
  864.8 163.5 %collective-permute-start.84 = (f32[24,128]{1,0:T(8,128)}, f32[24,128]{1,0:T(8,128)}, u32[]{:S(2)}, u32[]{:S(2)}) collective-permute-start(f32[24,128]{1,0:T(8,128)} %bitcast.282), channel_id=1, source_target_pairs={{0,16},{8,24},{16,0},{24,8},{1,17},{9,25},{17,1},{25,9},{2,18},{10... | collective-permute-start | bytes 36872 | tf_op jit(solution)/shard_map/ppermute | solution.py:96
  867.1 161.2 %collective-permute-start.83 = (f32[24,128]{1,0:T(8,128)}, f32[24,128]{1,0:T(8,128)}, u32[]{:S(2)}, u32[]{:S(2)}) collective-permute-start(f32[24,128]{1,0:T(8,128)} %bitcast.282), channel_id=1, source_target_pairs={{0,8},{8,0},{16,24},{24,16},{1,9},{9,1},{17,25},{25,17},{2,10},{10... | collective-permute-start | bytes 36872 | tf_op jit(solution)/shard_map/ppermute | solution.py:96
  940.2 19.1 %all-to-all-start.9 = ((bf16[8,64,1024]{2,1,0:T(8,128)(2,1)}), bf16[8,64,1024]{2,1,0:T(8,128)(2,1)S(1)}, u32[]{:S(2)}, u32[]{:S(2)}) async-start(bf16[8,64,1024]{2,1,0:T(8,128)(2,1)} %bitcast.207), calls=%async_computation.11 | async-start | bytes 2097152 | tf_op jit(solution)/shard_map/all_to_all | solution.py:82
  974.9 20.6 %all-to-all-start.7 = ((bf16[4,2,16384]{2,1,0:T(2,128)(2,1)}), bf16[4,2,16384]{2,1,0:T(2,128)(2,1)S(1)}, u32[]{:S(2)}, u32[]{:S(2)}) async-start(bf16[4,2,16384]{2,1,0:T(2,128)(2,1)} %reshape.1299), calls=%async_computation.8 | async-start | bytes 524288 | tf_op jit(solution)/shard_map/all_to_all | solution.py:404
  978.3 123.0 %all-gather.25.cloned.1.call-start = ((), (), s32[]{:S(2)}) async-start(), calls=%async_computation.23 | async-start | bytes 5324800 | tf_op jit(solution)/shard_map/all_gather | solution.py:826
  995.5 92.6 %all-to-all-start.10 = ((bf16[8,256,1536]{2,1,0:T(8,128)(2,1)}), bf16[8,256,1536]{2,1,0:T(8,128)(2,1)}, u32[]{:S(2)}, u32[]{:S(2)}) async-start(bf16[8,256,1536]{2,1,0:T(8,128)(2,1)} %bitcast.897), calls=%async_computation.12 | async-start | bytes 12582912 | tf_op jit(solution)/shard_map/all_to_all | solution.py:82
  (291 other events, 3710.5 us)
Sparse Core Ops, SparseCore 0:
  33.3 119.9 all-gather.12
  202.5 79.9 all-gather.14
  311.0 119.4 all-gather.16
  433.3 88.9 all-gather.18
  525.1 84.6 all-gather.20
  612.5 98.5 reduce-scatter.2
  714.6 81.4 all-gather.22
  803.5 95.6 reduce-scatter.4
  900.8 97.5 all-gather.26
  1000.4 81.2 all-gather.24

commit v4 on v3

--- a/solution.py
+++ b/solution.py
@@ -821,7 +821,7 @@
     smalls[0] = small_gradients({**mlp_terms, **terms})
     ins0, mlp_downs[0] = mlp_gradients(everyone[0], grad_all, weights[0])
     joined = [joined_rows(mlp_rows[1], which, 1, LAYERS, None) for which in range(2)]
-    flat = after(flat, ins0, mlp_rows[1])[0]
+    flat = after(flat, ins0, mlp_rows[1], input_grad)[0]
     pieces0 = rec_pieces(flat)
     rec_flat[0] = lax.all_gather(pieces0, "section", axis=0, tiled=False)
     mlp_rows[0] = to_rows(after(ins0, pieces0)[0])

time: 1150 us -> 1140 us (level)
  local copies, waits for them, and re-layouts: 198 us -> 185 us
    reduce_scatter x2, waiting for transfers between devices: 2.85 us -> 17.8 us  [section_sum(): return lax.psum_scatter(chunks, 'section', scatter_dimension=0, tiled=False)]
    all_to_all x2, waiting for transfers between devices: 18.8 us -> 4.6 us  [by_features(): lax.all_to_all(moved, 'section', split_axis=2, concat_axis=1, tiled=True)]
    unnamed x512 -> x496, local copies, waits for them, and re-layouts: 56.7 us -> 53 us
  transfers between devices with their start and end apart: 108 -> 108, of which waited for: 59 -> 61; matrix products, arithmetic and copies ran while one was open for 43% -> 42% of each run, Pallas kernels for 3% -> 3%
where the time goes in v4:
time: 1140 us; the launch traced here: 1130 us
  waiting for transfers between devices  366 us (32%)
  matrix products  241 us (21%)
  local copies, waits for them, and re-layouts  185 us (16%)
  starting transfers between devices  143 us (13%)
  other arithmetic  104 us (9%)
  Pallas kernels  38.2 us (3%)
  blocking collectives  30 us (3%)
  between operations  19.5 us (2%)
    ppermute x64, waiting for transfers between devices, swapped(): return lax.ppermute(value, 'dp', [(at, at ^ offset) for at in range(count)])  226 us
    dot_general x16, matrix products, dot_nt(): lax.dot_general(left, right, (((1,), (1,)), ((), ())), preferred_element_...  84.2 us
    dot_general x10, matrix products, dot_tn(): lax.dot_general(left, right, (((0,), (0,)), ((), ())), preferred_element_...  82.6 us
    dot_general x16, matrix products, dot(): return jnp.dot(left, right, preferred_element_type=jnp.float32)  74 us
    all_to_all x10, waiting for transfers between devices, spread(): return lax.all_to_all(pack, 'dp', 0, 0, tiled=False)  72.2 us
    ppermute x64, starting transfers between devices, swapped(): return lax.ppermute(value, 'dp', [(at, at ^ offset) for at in range(count)])  59.8 us
    unnamed x496, local copies, waits for them, and re-layouts  53 us
    all_to_all x10, starting transfers between devices, spread(): return lax.all_to_all(pack, 'dp', 0, 0, tiled=False)  41.5 us
  transfers between devices with their start and end apart: 108, of which 61 were waited for; matrix products, arithmetic and copies ran while one was open for 42% of the time, Pallas kernels for 3%

profile of v4, /device:TPU:0, one launch (start us, length us, event | category | flops | bytes accessed | tf_op | source)
XLA Modules:
  0.0 1127.7 jit_solution(12726742306828409203)
XLA Ops:
  10.3 20.7 %all_to_all.109 = bf16[4,128,512]{2,0,1:T(4,128)(2,1)S(1)} all-to-all(bf16[4,128,512]{2,0,1:T(4,128)(2,1)S(1)} %pad_maximum_fusion.25), channel_id=1, replica_groups=mesh['section'=4,'dp'=8] {'section'}, dimensions={1} | all-to-all | bytes 1048576 | tf_op jit(solution)/shard_map/all_to_all | solution.py:406
  34.5 9.3 all-gather.3
  79.2 61.1 %collective-permute-done.2 = bf16[64,2048]{1,0:T(8,128)(2,1)S(1)} collective-permute-done((bf16[64,2048]{1,0:T(8,128)(2,1)S(1)}, bf16[64,2048]{1,0:T(8,128)(2,1)S(1)}, u32[]{:S(2)}, u32[]{:S(2)}) %collective-permute-start.2) | collective-permute-done | bytes 262176 | tf_op jit(solution)/shard_map/ppermute | solution.py:58
  167.0 6.2 fusion.46
  186.2 6.0 all-to-all-done.2
  233.1 36.9 %all-to-all-done.3 = bf16[8,256,1536]{2,1,0:T(8,128)(2,1)} async-done(((bf16[8,256,1536]{2,1,0:T(8,128)(2,1)}), bf16[8,256,1536]{2,1,0:T(8,128)(2,1)}, u32[]{:S(2)}, u32[]{:S(2)}) %all-to-all-start.3) | async-done | bytes 6291488 | tf_op jit(solution)/shard_map/all_to_all | solution.py:82
  274.6 6.6 collective-permute-done.11
  286.9 16.9 %collective-permute-done.14 = bf16[64,2048]{1,0:T(8,128)(2,1)S(1)} collective-permute-done((bf16[64,2048]{1,0:T(8,128)(2,1)S(1)}, bf16[64,2048]{1,0:T(8,128)(2,1)S(1)}, u32[]{:S(2)}, u32[]{:S(2)}) %collective-permute-start.14) | collective-permute-done | bytes 262176 | tf_op jit(solution)/shard_map/ppermute | solution.py:58
  303.7 5.0 collective-permute-done.13
  316.0 6.8 fusion.430
  331.9 5.6 collective-permute-done.17
  337.5 5.4 collective-permute-done.19
  350.4 5.1 collective-permute-done.22
  367.4 10.3 collective-permute-done.24
  424.1 5.4 collective-permute-done.31
  440.8 6.2 collective-permute-done.33
  451.9 6.5 fusion.431
  458.5 5.2 fusion.85
  480.4 6.3 collective-permute-done.47
  491.0 6.8 collective-permute-done.37
  497.7 10.9 collective-permute-done.39
  509.7 12.5 %all-gather.19.cloned.1.call-done = bf16[2048,2048]{1,0:T(8,128)(2,1)} async-done(((bf16[64,2048]{1,0:T(8,128)(2,1)}), bf16[2048,2048]{1,0:T(8,128)(2,1)}) %all-gather.19.cloned.1.call-update) | async-done | bytes 8388624 | tf_op jit(solution)/shard_map/all_gather | solution.py:90
  529.7 7.5 all-to-all-start.5
  617.9 5.7 collective-permute-done.57
  623.6 5.7 collective-permute-done.59
  635.4 6.4 collective-permute-done.62
  659.5 5.9 fusion.429
  669.8 5.0 collective-permute-done.65
  674.8 5.0 collective-permute-done.67
  687.5 18.0 %fusion.433 = f32[2048,1536]{0,1:T(8,128)S(1)} fusion(bf16[2048,2048]{1,0:T(8,128)(2,1)} %all-gather.21.cloned.1.call-done, bf16[2048,1536]{1,0:T(8,128)(2,1)} %bitcast.894), kind=kOutput, calls=%fused_computation.923 | convolution fusion | flops 12884901888 | bytes 27262976 | tf_op jit(solution)/shard_map/dot_general | solution.py:33
  706.7 19.3 %fusion.13 = (bf16[2048,768]{0,1:T(8,128)(2,1)}, bf16[2048,768]{0,1:T(8,128)(2,1)}) fusion(f32[2048,1536]{0,1:T(8,128)S(1)} %fusion.433, bf16[2048,2048]{1,0:T(8,128)(2,1)} %all-gather.13.cloned.1.call-done, bf16[2,768,2048]{2,1,0:T(8,128)(2,1)} %param.36), kind=kOutput, calls=%fused_computation.20 | convolution fusion | flops 6480199680 | bytes 30408704 | tf_op jit(solution)/shard_map/dot_general | solution.py:37
  743.9 10.2 all-to-all-done.6
  821.1 6.3 collective-permute-done.79
  836.2 19.2 %convolution_convert_fusion = bf16[2048,1536]{1,0:T(8,128)(2,1)} fusion(bf16[2048,2048]{1,0:T(8,128)(2,1)} %all-gather.21.cloned.1.call-done, bf16[2048,768]{0,1:T(8,128)(2,1)} %get-tuple-element.148, bf16[2048,768]{0,1:T(8,128)(2,1)} %get-tuple-element.147), kind=kOutput, calls=%fused_computation.5 | convolution fusion | flops 12900630528 | bytes 20971520 | tf_op jit(solution)/shard_map/dot_general | solution.py:43
  860.3 19.4 %fusion.432 = f32[2048,1536]{0,1:T(8,128)} fusion(bf16[2048,2048]{1,0:T(8,128)(2,1)} %all-gather.19.cloned.1.call-done, bf16[2048,1536]{1,0:T(8,128)(2,1)} %bitcast.56), kind=kOutput, calls=%fused_computation.922 | convolution fusion | flops 12884901888 | bytes 27262976 | tf_op jit(solution)/shard_map/dot_general | solution.py:33
  883.7 19.6 %fusion.6 = (bf16[2048,768]{0,1:T(8,128)(2,1)}, bf16[2048,768]{0,1:T(8,128)(2,1)}) fusion(f32[2048,1536]{0,1:T(8,128)} %fusion.432, bf16[2048,2048]{1,0:T(8,128)(2,1)} %all-gather.23.cloned.1.call-done, bf16[2,768,2048]{2,1,0:T(8,128)(2,1)} %param.36), kind=kOutput, calls=%fused_computation.13 | convolution fusion | flops 6480199680 | bytes 30408704 | tf_op jit(solution)/shard_map/dot_general | solution.py:37
  903.3 17.8 %reduce-scatter.5.cloned.1.call-done = bf16[1,672,1024]{2,1,0:T(8,128)(2,1)} async-done(((bf16[4,672,1024]{2,1,0:T(8,128)(2,1)}), bf16[1,672,1024]{2,1,0:T(8,128)(2,1)}) %reduce-scatter.5.cloned.1.call-update) | async-done | bytes 1376272 | tf_op jit(solution)/shard_map/reduce_scatter | solution.py:86
  921.1 10.6 all-to-all-done.8.part_ref
  935.3 19.3 %convolution_convert_fusion.1 = bf16[2048,1536]{1,0:T(8,128)(2,1)} fusion(bf16[2048,2048]{1,0:T(8,128)(2,1)} %all-gather.19.cloned.1.call-done, bf16[2048,768]{0,1:T(8,128)(2,1)} %get-tuple-element.150, bf16[2048,768]{0,1:T(8,128)(2,1)} %get-tuple-element.149), kind=kOutput, calls=%fused_computation.6 | convolution fusion | flops 12900630528 | bytes 20971520 | tf_op jit(solution)/shard_map/dot_general | solution.py:43
  966.9 8.4 all-to-all-done.9
  987.1 5.0 all-to-all-start.10
  992.1 14.5 %convolution_bitcast_fusion = f32[1,768,2048]{2,1,0:T(8,128)} fusion(bf16[2048,2048]{1,0:T(8,128)(2,1)} %all-gather.13.cloned.1.call-done, f32[2048,1536]{0,1:T(8,128)} %copy-done.212), kind=kOutput, calls=%fused_computation.35 | convolution fusion | flops 6458179584 | bytes 27262976 | tf_op jit(solution)/shard_map/dot_general | solution.py:43
  1006.6 6.6 shard_map.328.kept_ref
  1013.2 6.9 shard_map.326.kept_ref
  1036.5 14.7 %convolution_bitcast_fusion.1 = f32[1,768,2048]{2,1,0:T(8,128)} fusion(bf16[2048,2048]{1,0:T(8,128)(2,1)} %all-gather.23.cloned.1.call-done, f32[2048,1536]{0,1:T(8,128)} %fusion.432), kind=kOutput, calls=%fused_computation.36 | convolution fusion | flops 6458179584 | bytes 27262976 | tf_op jit(solution)/shard_map/dot_general | solution.py:43
  1051.3 9.2 pad_maximum_fusion
  1076.8 6.6 shard_map.329
  1083.5 6.6 shard_map.327
  (1170 shorter events, 567.0 us)
Async XLA Ops:
  7.2 209.5 %all-gather.13.cloned.1.call-start = ((), (), s32[]{:S(2)}) async-start(), calls=%async_computation.15 | async-start | bytes 8650752 | tf_op jit(solution)/shard_map/all_gather | solution.py:90
  65.7 101.3 %all-to-all-start.1 = ((bf16[8,256,1024]{2,1,0:T(8,128)(2,1)}), bf16[8,256,1024]{2,1,0:T(8,128)(2,1)}, u32[]{:S(2)}, u32[]{:S(2)}) async-start(bf16[8,256,1024]{2,1,0:T(8,128)(2,1)} %copy-done.1), calls=%async_computation.1 | async-start | bytes 8388608 | tf_op jit(solution)/shard_map/all_to_all | solution.py:82
  75.0 65.4 %collective-permute-start.2 = (bf16[64,2048]{1,0:T(8,128)(2,1)S(1)}, bf16[64,2048]{1,0:T(8,128)(2,1)S(1)}, u32[]{:S(2)}, u32[]{:S(2)}) collective-permute-start(bf16[64,2048]{1,0:T(8,128)(2,1)S(1)} %get-tuple-element.146), channel_id=1, source_target_pairs={{0,6},{1,7},{2,4},{3,5},{4,2},{5,3},{6,0},{7,1},{8,14},{9,15},{10,... | collective-permute-start | bytes 786440 | tf_op jit(solution)/shard_map/ppermute | solution.py:58
  77.8 66.7 %collective-permute-start.1 = (bf16[64,2048]{1,0:T(8,128)(2,1)S(1)}, bf16[64,2048]{1,0:T(8,128)(2,1)S(1)}, u32[]{:S(2)}, u32[]{:S(2)}) collective-permute-start(bf16[64,2048]{1,0:T(8,128)(2,1)S(1)} %get-tuple-element.146), channel_id=1, source_target_pairs={{0,4},{1,5},{2,6},{3,7},{4,0},{5,1},{6,2},{7,3},{8,12},{9,13},{10,... | collective-permute-start | bytes 786440 | tf_op jit(solution)/shard_map/ppermute | solution.py:58
  78.3 66.2 %collective-permute-start = (bf16[64,2048]{1,0:T(8,128)(2,1)S(1)}, bf16[64,2048]{1,0:T(8,128)(2,1)S(1)}, u32[]{:S(2)}, u32[]{:S(2)}) collective-permute-start(bf16[64,2048]{1,0:T(8,128)(2,1)S(1)} %get-tuple-element.146), channel_id=1, source_target_pairs={{0,2},{1,3},{2,0},{3,1},{4,6},{5,7},{6,4},{7,5},{8,10},{9,11},{10,... | collective-permute-start | bytes 786440 | tf_op jit(solution)/shard_map/ppermute | solution.py:58
  144.6 20.1 %collective-permute-start.3 = (bf16[256,2048]{1,0:T(8,128)(2,1)S(1)}, bf16[256,2048]{1,0:T(8,128)(2,1)}, u32[]{:S(2)}, u32[]{:S(2)}) collective-permute-start(bf16[256,2048]{1,0:T(8,128)(2,1)S(1)} %pad_maximum_fusion.9), channel_id=1, source_target_pairs={{0,1},{1,0},{2,3},{3,2},{4,5},{5,4},{6,7},{7,6},{8,9},{9,8},{10,11... | collective-permute-start | bytes 3145736 | tf_op jit(solution)/shard_map/ppermute | solution.py:58
  173.3 18.9 %all-to-all-start.2 = ((bf16[8,64,1024]{2,1,0:T(8,128)(2,1)}), bf16[8,64,1024]{2,1,0:T(8,128)(2,1)S(1)}, u32[]{:S(2)}, u32[]{:S(2)}) async-start(bf16[8,64,1024]{2,1,0:T(8,128)(2,1)} %shard_map.318), calls=%async_computation.2 | async-start | bytes 2097152 | tf_op jit(solution)/shard_map/all_to_all | solution.py:82
  183.1 17.7 %collective-permute-start.4 = (f32[16,3,512]{2,1,0:T(4,128)S(1)}, f32[16,3,512]{2,1,0:T(4,128)S(1)}, u32[]{:S(2)}, u32[]{:S(2)}) collective-permute-start(f32[16,3,512]{2,1,0:T(4,128)S(1)} %slice.1505), channel_id=1, source_target_pairs={{0,8},{8,16},{16,24},{24,0},{1,9},{9,17},{17,25},{25,1},{2,10},{10... | collective-permute-start | bytes 294920 | tf_op jit(solution)/shard_map/ppermute | solution.py:499
  193.1 76.9 %all-to-all-start.3 = ((bf16[8,256,1536]{2,1,0:T(8,128)(2,1)}), bf16[8,256,1536]{2,1,0:T(8,128)(2,1)}, u32[]{:S(2)}, u32[]{:S(2)}) async-start(bf16[8,256,1536]{2,1,0:T(8,128)(2,1)} %copy-done), calls=%async_computation.3 | async-start | bytes 12582912 | tf_op jit(solution)/shard_map/all_to_all | solution.py:82
  198.0 111.9 %all-gather.15.cloned.1.call-start = ((), (), s32[]{:S(2)}) async-start(), calls=%async_computation.16 | async-start | bytes 5242880 | tf_op jit(solution)/shard_map/all_gather | solution.py:421
  225.9 48.6 %collective-permute-start.9 = (bf16[64,2048]{1,0:T(8,128)(2,1)}, bf16[64,2048]{1,0:T(8,128)(2,1)S(1)}, u32[]{:S(2)}, u32[]{:S(2)}) collective-permute-start(bf16[64,2048]{1,0:T(8,128)(2,1)} %get-tuple-element.223), channel_id=1, source_target_pairs={{0,2},{1,3},{2,0},{3,1},{4,6},{5,7},{6,4},{7,5},{8,10},{9,11},{10,... | collective-permute-start | bytes 786440 | tf_op jit(solution)/shard_map/ppermute | solution.py:58
  228.5 52.7 %collective-permute-start.11 = (bf16[64,2048]{1,0:T(8,128)(2,1)S(1)}, bf16[64,2048]{1,0:T(8,128)(2,1)S(1)}, u32[]{:S(2)}, u32[]{:S(2)}) collective-permute-start(bf16[64,2048]{1,0:T(8,128)(2,1)S(1)} %get-tuple-element.224), channel_id=1, source_target_pairs={{0,6},{1,7},{2,4},{3,5},{4,2},{5,3},{6,0},{7,1},{8,14},{9,15},{10,... | collective-permute-start | bytes 786440 | tf_op jit(solution)/shard_map/ppermute | solution.py:58
  229.9 51.3 %collective-permute-start.10 = (bf16[64,2048]{1,0:T(8,128)(2,1)S(1)}, bf16[64,2048]{1,0:T(8,128)(2,1)S(1)}, u32[]{:S(2)}, u32[]{:S(2)}) collective-permute-start(bf16[64,2048]{1,0:T(8,128)(2,1)S(1)} %get-tuple-element.225), channel_id=1, source_target_pairs={{0,4},{1,5},{2,6},{3,7},{4,0},{5,1},{6,2},{7,3},{8,12},{9,13},{10,... | collective-permute-start | bytes 786440 | tf_op jit(solution)/shard_map/ppermute | solution.py:58
  270.0 39.9 %all-to-all-start.4 = ((bf16[8,64,1536]{2,1,0:T(8,128)(2,1)}), bf16[8,64,1536]{2,1,0:T(8,128)(2,1)S(1)}, u32[]{:S(2)}, u32[]{:S(2)}) async-start(bf16[8,64,1536]{2,1,0:T(8,128)(2,1)} %shard_map.319), calls=%async_computation.4 | async-start | bytes 3145728 | tf_op jit(solution)/shard_map/all_to_all | solution.py:82
  273.6 178.3 %all-gather.17.cloned.1.call-start = ((), (), s32[]{:S(2)}) async-start(), calls=%async_computation.17 | async-start | bytes 7864320 | tf_op jit(solution)/shard_map/all_gather | solution.py:785
  283.4 20.3 %collective-permute-start.14 = (bf16[64,2048]{1,0:T(8,128)(2,1)S(1)}, bf16[64,2048]{1,0:T(8,128)(2,1)S(1)}, u32[]{:S(2)}, u32[]{:S(2)}) collective-permute-start(bf16[64,2048]{1,0:T(8,128)(2,1)S(1)} %get-tuple-element.60), channel_id=1, source_target_pairs={{0,6},{1,7},{2,4},{3,5},{4,2},{5,3},{6,0},{7,1},{8,14},{9,15},{10,... | collective-permute-start | bytes 786440 | tf_op jit(solution)/shard_map/ppermute | solution.py:58
  283.5 25.2 %collective-permute-start.13 = (bf16[64,2048]{1,0:T(8,128)(2,1)S(1)}, bf16[64,2048]{1,0:T(8,128)(2,1)S(1)}, u32[]{:S(2)}, u32[]{:S(2)}) collective-permute-start(bf16[64,2048]{1,0:T(8,128)(2,1)S(1)} %get-tuple-element.60), channel_id=1, source_target_pairs={{0,4},{1,5},{2,6},{3,7},{4,0},{5,1},{6,2},{7,3},{8,12},{9,13},{10,... | collective-permute-start | bytes 786440 | tf_op jit(solution)/shard_map/ppermute | solution.py:58
  285.4 23.3 %collective-permute-start.12 = (bf16[64,2048]{1,0:T(8,128)(2,1)S(1)}, bf16[64,2048]{1,0:T(8,128)(2,1)S(1)}, u32[]{:S(2)}, u32[]{:S(2)}) collective-permute-start(bf16[64,2048]{1,0:T(8,128)(2,1)S(1)} %get-tuple-element.60), channel_id=1, source_target_pairs={{0,2},{1,3},{2,0},{3,1},{4,6},{5,7},{6,4},{7,5},{8,10},{9,11},{10,... | collective-permute-start | bytes 786440 | tf_op jit(solution)/shard_map/ppermute | solution.py:58
  311.1 211.2 %all-gather.19.cloned.1.call-start = ((), (), s32[]{:S(2)}) async-start(), calls=%async_computation.18 | async-start | bytes 8650752 | tf_op jit(solution)/shard_map/all_gather | solution.py:90
  400.6 231.3 %all-gather.21.cloned.1.call-start = ((), (), s32[]{:S(2)}) async-start(), calls=%async_computation.19 | async-start | bytes 8650752 | tf_op jit(solution)/shard_map/all_gather | solution.py:90
  409.4 20.1 %collective-permute-start.31 = (bf16[64,2048]{1,0:T(8,128)(2,1)S(1)}, bf16[64,2048]{1,0:T(8,128)(2,1)S(1)}, u32[]{:S(2)}, u32[]{:S(2)}) collective-permute-start(bf16[64,2048]{1,0:T(8,128)(2,1)S(1)} %get-tuple-element.218), channel_id=1, source_target_pairs={{0,6},{1,7},{2,4},{3,5},{4,2},{5,3},{6,0},{7,1},{8,14},{9,15},{10,... | collective-permute-start | bytes 786440 | tf_op jit(solution)/shard_map/ppermute | solution.py:58
  413.1 16.4 %collective-permute-start.30 = (bf16[64,2048]{1,0:T(8,128)(2,1)S(1)}, bf16[64,2048]{1,0:T(8,128)(2,1)S(1)}, u32[]{:S(2)}, u32[]{:S(2)}) collective-permute-start(bf16[64,2048]{1,0:T(8,128)(2,1)S(1)} %get-tuple-element.219), channel_id=1, source_target_pairs={{0,4},{1,5},{2,6},{3,7},{4,0},{5,1},{6,2},{7,3},{8,12},{9,13},{10,... | collective-permute-start | bytes 786440 | tf_op jit(solution)/shard_map/ppermute | solution.py:58
  419.5 27.8 %collective-permute-start.43 = (bf16[256,2048]{1,0:T(8,128)(2,1)}, bf16[256,2048]{1,0:T(8,128)(2,1)}, u32[]{:S(2)}, u32[]{:S(2)}) collective-permute-start(bf16[256,2048]{1,0:T(8,128)(2,1)} %pad_maximum_fusion.13), channel_id=1, source_target_pairs={{0,1},{1,0},{2,3},{3,2},{4,5},{5,4},{6,7},{7,6},{8,9},{9,8},{10,11... | collective-permute-start | bytes 3145736 | tf_op jit(solution)/shard_map/ppermute | solution.py:58
  470.9 15.8 %collective-permute-start.47 = (bf16[64,2048]{1,0:T(8,128)(2,1)S(1)}, bf16[64,2048]{1,0:T(8,128)(2,1)S(1)}, u32[]{:S(2)}, u32[]{:S(2)}) collective-permute-start(bf16[64,2048]{1,0:T(8,128)(2,1)S(1)} %get-tuple-element.212), channel_id=1, source_target_pairs={{0,6},{1,7},{2,4},{3,5},{4,2},{5,3},{6,0},{7,1},{8,14},{9,15},{10,... | collective-permute-start | bytes 786440 | tf_op jit(solution)/shard_map/ppermute | solution.py:58
  472.8 17.2 %collective-permute-start.46 = (bf16[64,2048]{1,0:T(8,128)(2,1)S(1)}, bf16[64,2048]{1,0:T(8,128)(2,1)S(1)}, u32[]{:S(2)}, u32[]{:S(2)}) collective-permute-start(bf16[64,2048]{1,0:T(8,128)(2,1)S(1)} %get-tuple-element.213), channel_id=1, source_target_pairs={{0,4},{1,5},{2,6},{3,7},{4,0},{5,1},{6,2},{7,3},{8,12},{9,13},{10,... | collective-permute-start | bytes 786440 | tf_op jit(solution)/shard_map/ppermute | solution.py:58
  474.7 23.0 %collective-permute-start.37 = (bf16[64,2048]{1,0:T(8,128)(2,1)S(1)}, bf16[64,2048]{1,0:T(8,128)(2,1)S(1)}, u32[]{:S(2)}, u32[]{:S(2)}) collective-permute-start(bf16[64,2048]{1,0:T(8,128)(2,1)S(1)} %get-tuple-element.214), channel_id=1, source_target_pairs={{0,2},{1,3},{2,0},{3,1},{4,6},{5,7},{6,4},{7,5},{8,10},{9,11},{10,... | collective-permute-start | bytes 786440 | tf_op jit(solution)/shard_map/ppermute | solution.py:58
  475.5 33.1 %collective-permute-start.39 = (bf16[64,2048]{1,0:T(8,128)(2,1)S(1)}, bf16[64,2048]{1,0:T(8,128)(2,1)S(1)}, u32[]{:S(2)}, u32[]{:S(2)}) collective-permute-start(bf16[64,2048]{1,0:T(8,128)(2,1)S(1)} %get-tuple-element.215), channel_id=1, source_target_pairs={{0,6},{1,7},{2,4},{3,5},{4,2},{5,3},{6,0},{7,1},{8,14},{9,15},{10,... | collective-permute-start | bytes 786440 | tf_op jit(solution)/shard_map/ppermute | solution.py:58
  479.3 29.4 %collective-permute-start.38 = (bf16[64,2048]{1,0:T(8,128)(2,1)S(1)}, bf16[64,2048]{1,0:T(8,128)(2,1)S(1)}, u32[]{:S(2)}, u32[]{:S(2)}) collective-permute-start(bf16[64,2048]{1,0:T(8,128)(2,1)S(1)} %get-tuple-element.216), channel_id=1, source_target_pairs={{0,4},{1,5},{2,6},{3,7},{4,0},{5,1},{6,2},{7,3},{8,12},{9,13},{10,... | collective-permute-start | bytes 786440 | tf_op jit(solution)/shard_map/ppermute | solution.py:58
  529.7 20.7 %all-to-all-start.5 = ((bf16[4,2,16384]{2,1,0:T(2,128)(2,1)}), bf16[4,2,16384]{2,1,0:T(2,128)(2,1)S(1)}, u32[]{:S(2)}, u32[]{:S(2)}) async-start(bf16[4,2,16384]{2,1,0:T(2,128)(2,1)} %reshape.1297), calls=%async_computation.5 | async-start | bytes 524288 | tf_op jit(solution)/shard_map/all_to_all | solution.py:404
  537.1 190.3 %reduce-scatter.3.cloned.1.call-start = ((), (), s32[]{:S(2)}) async-start(), calls=%async_computation.20 | async-start | bytes 6881280 | tf_op jit(solution)/shard_map/reduce_scatter | solution.py:86
  539.5 16.8 %collective-permute-start.51 = (bf16[256,2048]{1,0:T(8,128)(2,1)}, bf16[256,2048]{1,0:T(8,128)(2,1)}, u32[]{:S(2)}, u32[]{:S(2)}) collective-permute-start(bf16[256,2048]{1,0:T(8,128)(2,1)} %pad_maximum_fusion.14), channel_id=1, source_target_pairs={{0,1},{1,0},{2,3},{3,2},{4,5},{5,4},{6,7},{7,6},{8,9},{9,8},{10,11... | collective-permute-start | bytes 3145736 | tf_op jit(solution)/shard_map/ppermute | solution.py:58
  606.2 277.5 %all-gather.23.cloned.1.call-start = ((), (), s32[]{:S(2)}) async-start(), calls=%async_computation.22 | async-start | bytes 8650752 | tf_op jit(solution)/shard_map/all_gather | solution.py:90
  684.0 21.5 %collective-permute-start.70 = (bf16[64,2048]{1,0:T(8,128)(2,1)S(1)}, bf16[64,2048]{1,0:T(8,128)(2,1)S(1)}, u32[]{:S(2)}, u32[]{:S(2)}) collective-permute-start(bf16[64,2048]{1,0:T(8,128)(2,1)S(1)} %get-tuple-element.119), channel_id=1, source_target_pairs={{0,6},{1,7},{2,4},{3,5},{4,2},{5,3},{6,0},{7,1},{8,14},{9,15},{10,... | collective-permute-start | bytes 786440 | tf_op jit(solution)/shard_map/ppermute | solution.py:58
  685.7 19.8 %collective-permute-start.69 = (bf16[64,2048]{1,0:T(8,128)(2,1)S(1)}, bf16[64,2048]{1,0:T(8,128)(2,1)S(1)}, u32[]{:S(2)}, u32[]{:S(2)}) collective-permute-start(bf16[64,2048]{1,0:T(8,128)(2,1)S(1)} %get-tuple-element.119), channel_id=1, source_target_pairs={{0,4},{1,5},{2,6},{3,7},{4,0},{5,1},{6,2},{7,3},{8,12},{9,13},{10,... | collective-permute-start | bytes 786440 | tf_op jit(solution)/shard_map/ppermute | solution.py:58
  686.8 18.7 %collective-permute-start.68 = (bf16[64,2048]{1,0:T(8,128)(2,1)S(1)}, bf16[64,2048]{1,0:T(8,128)(2,1)S(1)}, u32[]{:S(2)}, u32[]{:S(2)}) collective-permute-start(bf16[64,2048]{1,0:T(8,128)(2,1)S(1)} %get-tuple-element.119), channel_id=1, source_target_pairs={{0,2},{1,3},{2,0},{3,1},{4,6},{5,7},{6,4},{7,5},{8,10},{9,11},{10,... | collective-permute-start | bytes 786440 | tf_op jit(solution)/shard_map/ppermute | solution.py:58
  706.7 27.9 %collective-permute-start.71 = (bf16[256,2048]{1,0:T(8,128)(2,1)}, bf16[256,2048]{1,0:T(8,128)(2,1)}, u32[]{:S(2)}, u32[]{:S(2)}) collective-permute-start(bf16[256,2048]{1,0:T(8,128)(2,1)} %pad_maximum_fusion.16), channel_id=1, source_target_pairs={{0,1},{1,0},{2,3},{3,2},{4,5},{5,4},{6,7},{7,6},{8,9},{9,8},{10,11... | collective-permute-start | bytes 3145736 | tf_op jit(solution)/shard_map/ppermute | solution.py:58
  729.7 24.4 %all-to-all-start.6 = ((bf16[8,64,1024]{2,1,0:T(8,128)(2,1)}), bf16[8,64,1024]{2,1,0:T(8,128)(2,1)S(1)}, u32[]{:S(2)}, u32[]{:S(2)}) async-start(bf16[8,64,1024]{2,1,0:T(8,128)(2,1)} %bitcast.141), calls=%async_computation.7 | async-start | bytes 2097152 | tf_op jit(solution)/shard_map/all_to_all | solution.py:82
  733.4 187.7 %reduce-scatter.5.cloned.1.call-start = ((), (), s32[]{:S(2)}) async-start(), calls=%async_computation.21 | async-start | bytes 6881280 | tf_op jit(solution)/shard_map/reduce_scatter | solution.py:86
  832.8 22.6 %all-to-all-start.7 = ((bf16[4,2,16384]{2,1,0:T(2,128)(2,1)}), bf16[4,2,16384]{2,1,0:T(2,128)(2,1)S(1)}, u32[]{:S(2)}, u32[]{:S(2)}) async-start(bf16[4,2,16384]{2,1,0:T(2,128)(2,1)} %reshape.1299), calls=%async_computation.8 | async-start | bytes 524288 | tf_op jit(solution)/shard_map/all_to_all | solution.py:404
  855.4 76.3 %all-to-all-start.8 = ((bf16[8,256,1536]{2,1,0:T(8,128)(2,1)}), bf16[8,256,1536]{2,1,0:T(8,128)(2,1)}, u32[]{:S(2)}, u32[]{:S(2)}) async-start(bf16[8,256,1536]{2,1,0:T(8,128)(2,1)} %bitcast.898), calls=%async_computation.10 | async-start | bytes 12582912 | tf_op jit(solution)/shard_map/all_to_all | solution.py:82
  860.3 200.2 %all-gather.27.cloned.1.call-start = ((), (), s32[]{:S(2)}) async-start(), calls=%async_computation.24 | async-start | bytes 5324800 | tf_op jit(solution)/shard_map/all_gather | solution.py:820
  931.7 23.9 %all-to-all-start.12 = ((f32[8,1,3072]{2,1,0:T(1,128)}), f32[8,1,3072]{2,1,0:T(1,128)S(1)}, u32[]{:S(2)}, u32[]{:S(2)}) async-start(f32[8,1,3072]{2,1,0:T(1,128)} %copy.314), calls=%async_computation.14 | async-start | bytes 196608 | tf_op jit(solution)/shard_map/all_to_all | solution.py:82
  955.6 19.6 %all-to-all-start.9 = ((bf16[8,64,1024]{2,1,0:T(8,128)(2,1)}), bf16[8,64,1024]{2,1,0:T(8,128)(2,1)S(1)}, u32[]{:S(2)}, u32[]{:S(2)}) async-start(bf16[8,64,1024]{2,1,0:T(8,128)(2,1)} %bitcast.207), calls=%async_computation.11 | async-start | bytes 2097152 | tf_op jit(solution)/shard_map/all_to_all | solution.py:82
  961.2 58.9 %collective-permute-start.85 = (f32[24,128]{1,0:T(8,128)}, f32[24,128]{1,0:T(8,128)}, u32[]{:S(2)}, u32[]{:S(2)}) collective-permute-start(f32[24,128]{1,0:T(8,128)} %bitcast.282), channel_id=1, source_target_pairs={{0,24},{8,16},{16,8},{24,0},{1,25},{9,17},{17,9},{25,1},{2,26},{10... | collective-permute-start | bytes 36872 | tf_op jit(solution)/shard_map/ppermute | solution.py:96
  964.9 55.2 %collective-permute-start.84 = (f32[24,128]{1,0:T(8,128)}, f32[24,128]{1,0:T(8,128)}, u32[]{:S(2)}, u32[]{:S(2)}) collective-permute-start(f32[24,128]{1,0:T(8,128)} %bitcast.282), channel_id=1, source_target_pairs={{0,16},{8,24},{16,0},{24,8},{1,17},{9,25},{17,1},{25,9},{2,18},{10... | collective-permute-start | bytes 36872 | tf_op jit(solution)/shard_map/ppermute | solution.py:96
  964.9 55.2 %collective-permute-start.83 = (f32[24,128]{1,0:T(8,128)}, f32[24,128]{1,0:T(8,128)}, u32[]{:S(2)}, u32[]{:S(2)}) collective-permute-start(f32[24,128]{1,0:T(8,128)} %bitcast.282), channel_id=1, source_target_pairs={{0,8},{8,0},{16,24},{24,16},{1,9},{9,1},{17,25},{25,17},{2,10},{10... | collective-permute-start | bytes 36872 | tf_op jit(solution)/shard_map/ppermute | solution.py:96
  979.2 110.8 %all-gather.25.cloned.1.call-start = ((), (), s32[]{:S(2)}) async-start(), calls=%async_computation.23 | async-start | bytes 5324800 | tf_op jit(solution)/shard_map/all_gather | solution.py:826
  987.1 89.7 %all-to-all-start.10 = ((bf16[8,256,1536]{2,1,0:T(8,128)(2,1)}), bf16[8,256,1536]{2,1,0:T(8,128)(2,1)}, u32[]{:S(2)}, u32[]{:S(2)}) async-start(bf16[8,256,1536]{2,1,0:T(8,128)(2,1)} %bitcast.897), calls=%async_computation.12 | async-start | bytes 12582912 | tf_op jit(solution)/shard_map/all_to_all | solution.py:82
  (283 other events, 3768.0 us)
Sparse Core Ops, SparseCore 0:
  33.3 119.9 all-gather.12
  202.7 80.1 all-gather.14
  311.2 119.5 all-gather.16
  433.6 88.6 all-gather.18
  525.0 84.3 all-gather.20
  612.1 98.6 reduce-scatter.2
  713.8 85.0 all-gather.22
  820.4 100.6 reduce-scatter.4
  922.7 83.5 all-gather.26
  1008.3 81.2 all-gather.24
